TPU v7x, 32 devices: a whole 2x2x4 slice. The times are simulated.
32 devices in a mesh: groups: 2 (over y), seq: 16 (over z, x, core).
Axes of the slice: x: 2, y: 2, z: 4, core: 2. Of those that a mesh axis runs over, the one named last changes fastest.
Arguments:
- xbc: bfloat16 [16384, 2304], P(('groups', 'seq')), parts along dimension 0, may hold values from -24 to 24
- conv_weight: float32 [4, 2304], replicated, may hold values from -3 to 3
- log_decay: float32 [16, 16384], P(None, ('groups', 'seq')), parts along dimension 1, may hold values from -1 to 0, as said below
- level_weights: float32 [16, 14, 16384], P(None, None, ('groups', 'seq')), parts along dimension 2, may hold values from 0.1 to 1
- gain: float32 [2048], replicated, may hold values from 0.25 to 1.75
Outputs:
- mixed: bfloat16 [16384, 2048], P(('groups', 'seq')), parts along dimension 0
There are 2 independent parts, one for each index of `groups`. A program takes and returns all parts, laid end to end along the dimension named above; an argument that names none is the same for every part. Nothing has to cross between parts.
Inputs may be any that keep to these rules, and one draw needn't show every extreme that they name: `log_decay`: every entry is negative.
All inputs are finite; a program needn't handle non-finite values.
Results may differ from a plain program's by a relative error of at most 0.0034.
Values may be sent and summed in bfloat16 or wider, within the bound.
No kernel may reach another device: no remote copies, remote signals or barrier semaphores. Data moves between devices by JAX's collectives and lax.ppermute only.
A program may use at most 128 MiB of HBM per device.

v0:
```python
import jax
import jax.numpy as jnp
from jax import lax
from jax.sharding import PartitionSpec as P


def from_behind(block, axis, distance):
    devices = range(lax.axis_size(axis))
    route = [(i - distance, i) for i in devices if i - distance in devices]
    return lax.ppermute(block, axis, route)


def swapped(value, axis, apart):
    return lax.ppermute(value, axis, [(i, i ^ 1 << apart) for i in range(lax.axis_size(axis))])


def bit_length(numbers, limit):
    counted = jnp.zeros(numbers.shape, jnp.int32)
    for power_index in range(limit):
        counted = counted + (numbers >= 1 << power_index).astype(jnp.int32)
    return counted


def compute_near(values_rows, in_map, out_map, local_log, level_gain, head_count):
    row_count = values_rows.shape[0]
    head_dim = values_rows.shape[1] // head_count
    local_bits = row_count.bit_length() - 1
    scores = lax.dot_general(
        out_map, in_map, (((1,), (1,)), ((), ())), preferred_element_type=jnp.float32
    )
    element_index = lax.iota(jnp.int32, row_count)
    level_index = bit_length(
        jnp.bitwise_xor(element_index[:, None], element_index[None, :]), local_bits
    )
    causal = element_index[None, :] <= element_index[:, None]
    chosen = jnp.zeros((head_count, row_count, row_count), jnp.float32)
    for level_step in range(local_bits + 1):
        chosen = jnp.where(
            (level_index == level_step)[None], level_gain[:, level_step, :, None], chosen
        )
    gap_log = jnp.where(causal[None], local_log[:, :, None] - local_log[:, None, :], -1e30)
    weight = (chosen * jnp.exp(gap_log) * scores[None]).astype(jnp.bfloat16)
    shaped = values_rows.reshape(row_count, head_count, head_dim)
    near_heads = jnp.einsum("hts,shp->thp", weight, shaped, preferred_element_type=jnp.float32)
    return near_heads.reshape(row_count, head_count * head_dim)


def silu_conv(xbc, conv_weight):
    kernel = conv_weight.shape[0]
    row_count = xbc.shape[0]
    earlier = from_behind(xbc[row_count - kernel + 1 :], "seq", 1)
    padded = jnp.concatenate([earlier, xbc], axis=0).astype(jnp.float32)
    convolved = padded[0:row_count] * conv_weight[0]
    for offset in range(1, kernel):
        convolved = convolved + padded[offset : offset + row_count] * conv_weight[offset]
    return jax.nn.silu(convolved).astype(jnp.bfloat16)


def combine_groups(aggregate, partner, group_span, partner_span, is_upper, head_dim):
    left_part = jnp.where(is_upper, partner, aggregate)
    right_part = jnp.where(is_upper, aggregate, partner)
    right_span = jnp.where(is_upper, group_span, partner_span)
    carry_decay = jnp.repeat(jnp.exp(right_span), head_dim)
    return left_part * carry_decay[None, :] + right_part


def add_level(running, queries_wide, partner, factor, head_count):
    product = jnp.dot(
        queries_wide, partner, precision=lax.Precision.HIGHEST, preferred_element_type=jnp.float32
    )
    row_count = product.shape[0]
    shaped = product.reshape(row_count, head_count, -1) * factor.T[:, :, None]
    return running + shaped.reshape(row_count, -1)


def on_device(xbc, conv_weight, log_decay, level_weights, gain):
    row_count = xbc.shape[0]
    head_count = log_decay.shape[0]
    inner_width = gain.shape[0]
    head_dim = inner_width // head_count
    state_size = (xbc.shape[1] - inner_width) // 2
    activated = silu_conv(xbc, conv_weight)
    values_rows = activated[:, :inner_width]
    in_map = activated[:, inner_width : inner_width + state_size]
    out_map = activated[:, inner_width + state_size :]
    local_log = jnp.cumsum(log_decay, axis=1)
    block_total = local_log[:, row_count - 1]
    tail_decay = jnp.exp(block_total[:, None] - local_log)
    decayed = (
        (values_rows.reshape(row_count, head_count, head_dim) * tail_decay.T[:, :, None])
        .reshape(row_count, inner_width)
        .astype(jnp.bfloat16)
    )
    block_state = lax.dot_general(
        in_map, decayed, (((0,), (0,)), ((), ())), preferred_element_type=jnp.float32
    )
    local_bits = row_count.bit_length() - 1
    seq_bits = lax.axis_size("seq").bit_length() - 1
    element_index = lax.axis_index("seq")
    queries_wide = out_map.astype(jnp.float32)
    far_term = jnp.zeros((row_count, inner_width), jnp.float32)
    aggregate = block_state
    group_span = block_total
    group_prefix = jnp.zeros_like(block_total)
    for bit_index in range(seq_bits):
        is_upper = element_index >> bit_index & 1 == 1
        partner, partner_span = swapped((aggregate, group_span), "seq", bit_index)
        gap_log = group_prefix
        group_prefix = jnp.where(is_upper, group_prefix + partner_span, group_prefix)
        exponent = jnp.where(is_upper, local_log + gap_log[:, None], -1e30)
        factor = level_weights[:, local_bits + bit_index + 1, :] * jnp.exp(exponent)

        def taken(running):
            return add_level(running, queries_wide, partner, factor, head_count)

        def skipped(running):
            return running

        far_term = lax.cond(is_upper, taken, skipped, far_term)
        if bit_index + 1 < seq_bits:
            aggregate = combine_groups(
                aggregate, partner, group_span, partner_span, is_upper, head_dim
            )
            group_span = group_span + partner_span
    near_term = compute_near(values_rows, in_map, out_map, local_log, level_weights, head_count)
    mixed_sum = (near_term + far_term).reshape(row_count, head_count, head_dim)
    inv_rms = lax.rsqrt(jnp.mean(mixed_sum * mixed_sum, axis=2, keepdims=True) + 1e-05)
    return ((mixed_sum * inv_rms).reshape(row_count, inner_width) * gain).astype(jnp.bfloat16)


def solution(mesh):
    in_specs = (
        P(("groups", "seq"), None),
        P(),
        P(None, ("groups", "seq")),
        P(None, None, ("groups", "seq")),
        P(),
    )
    out_specs = P(("groups", "seq"), None)
    return jax.shard_map(
        on_device, mesh=mesh, in_specs=in_specs, out_specs=out_specs, check_vma=False
    )
```

profile of v0, /device:TPU:27, one launch (start us, length us, event | category | flops | bytes accessed | tf_op | source)
XLA Modules:
  0.0 186.7 jit_solution(15527379835954160170)
XLA Ops:
  0.8 1.3 collective-permute-start
  2.1 1.2 reduce-window.6
  3.8 1.0 slice_reduce_fusion.4
  5.0 2.1 %maximum_convert_fusion = f32[515,2304]{1,0:T(8,128)S(1)} fusion(bf16[512,2304]{1,0:T(8,128)(2,1)} %param.13, bf16[3,2304]{1,0:T(4,128)(2,1)S(1)} %collective-permute-done), kind=kLoop, calls=%fused_computation.67 | loop fusion | flops 4746240 | bytes 7119360 | tf_op jit(solution)/shard_map/convert_element_type | solution.py:52
  7.2 2.9 %multiply_convert_fusion.2 = bf16[512,2304]{1,0:T(8,128)(2,1)S(1)} fusion(f32[515,2304]{1,0:T(8,128)S(1)} %maximum_convert_fusion, f32[2304]{0:T(1024)S(1)} %get-tuple-element.290, f32[2304]{0:T(1024)S(1)} %get-tuple-element.291, f32[2304]{0:T(1024)S(1)} %get-tuple-element.289, f32[2304]{0:T(1024)S(1)} %get-tuple-element.288), kind=kLoop, calls=%fused_computation.60 | loop fusion | flops 14155776 | bytes 21270528 | tf_op jit(solution)/shard_map/convert_element_type | solution.py:56
  10.1 1.1 mul.194
  11.2 2.5 %fusion.46 = f32[128,2048]{1,0:T(8,128)} fusion(f32[64,8,16,128]{3,2,1,0:T(8,128)S(1)} %bitcast.123, bf16[512,2304]{1,0:T(8,128)(2,1)S(1)} %multiply_convert_fusion.2), kind=kOutput, calls=%fused_computation.68 | convolution fusion | flops 271581184 | bytes 7471104 | tf_op jit(solution)/shard_map/dot_general | solution.py:94
  13.7 1.5 collective-permute-start.1
  15.5 1.2 broadcast_compare_fusion.1
  17.8 2.7 %select_add_fusion.2 = f32[128,2048]{1,0:T(8,128)} fusion(f32[128,2048]{1,0:T(8,128)} %fusion.46, f32[128,2048]{1,0:T(8,128)} %collective-permute-done.1, f32[2048]{0:T(1024)S(1)} %broadcast_bitcast_fusion.2, pred[]{:T(512)} %eq.119), kind=kLoop, calls=%fused_computation.71 | loop fusion | flops 1048576 | bytes 3153921 | tf_op jit(solution)/shard_map/add | solution.py:64
  20.5 1.5 collective-permute-start.3
  22.0 1.2 broadcast_compare_fusion.3
  23.2 1.1 broadcast_compare_fusion.5
  24.3 1.1 broadcast_compare_fusion.7
  25.5 19.8 %collective-permute-done.4 = f32[16]{0:T(128)S(1)} collective-permute-done((f32[16]{0:T(128)S(1)}, f32[16]{0:T(128)S(1)}, u32[]{:S(2)}, u32[]{:S(2)}) %collective-permute-start.4) | collective-permute-done | bytes 96 | tf_op jit(solution)/shard_map/ppermute | solution.py:14
  45.3 2.7 %select_add_fusion.1 = f32[128,2048]{1,0:T(8,128)} fusion(f32[128,2048]{1,0:T(8,128)} %select_add_fusion.2, f32[128,2048]{1,0:T(8,128)} %collective-permute-done.3, f32[2048]{0:T(1024)S(1)} %broadcast_bitcast_fusion.1, pred[]{:T(512)} %eq.118), kind=kLoop, calls=%fused_computation.70 | loop fusion | flops 1048576 | bytes 3153921 | tf_op jit(solution)/shard_map/add | solution.py:64
  48.1 1.7 collective-permute-start.5
  51.5 20.8 %collective-permute-done.6 = f32[16]{0:T(128)S(1)} collective-permute-done((f32[16]{0:T(128)S(1)}, f32[16]{0:T(128)S(1)}, u32[]{:S(2)}, u32[]{:S(2)}) %collective-permute-start.6) | collective-permute-done | bytes 96 | tf_op jit(solution)/shard_map/ppermute | solution.py:14
  72.6 2.7 %select_add_fusion = f32[128,2048]{1,0:T(8,128)} fusion(f32[128,2048]{1,0:T(8,128)} %select_add_fusion.1, f32[128,2048]{1,0:T(8,128)} %collective-permute-done.5, f32[2048]{0:T(1024)S(1)} %broadcast_bitcast_fusion, pred[]{:T(512)} %eq.117), kind=kLoop, calls=%fused_computation.69 | loop fusion | flops 1048576 | bytes 3153921 | tf_op jit(solution)/shard_map/add | solution.py:64
  75.3 1.4 collective-permute-start.7
  76.8 20.9 %multiply_convert_fusion.5 = bf16[16,512,512]{2,1,0:T(8,128)(2,1)} fusion(f32[512,512]{1,0:T(8,128)S(1)} %fusion.58, f32[16,512]{1,0:T(8,128)S(1)} %copy_bitcast_fusion, f32[16,512]{1,0:T(8,128)S(1)} %get-tuple-element.297, f32[16,512]{1,0:T(8,128)S(1)} %get-tuple-element.298, f32[16,512]{1,0:T(8,128)S(1)} %get-tuple-element.299, ...), kind=kLoop, calls=%fused_computation.25.clone.clone.1 | loop fusion | flops 62914560 | bytes 12681216 | tf_op jit(solution)/shard_map/hts,shp->thp/dot_general | solution.py:44
  97.7 1.6 slice.127
  99.3 3.9 %copy.55 = bf16[512,2048]{0,1:T(8,128)(2,1)} copy(bf16[512,2048]{1,0:T(8,128)(2,1)} %slice.127) | data formatting | bytes 4194304 | tf_op jit(solution)/shard_map/slice | solution.py:83
  103.3 8.8 %fusion.13 = f32[16,128,512]{2,1,0:T(8,128)} fusion(bf16[512,16,128]{0,2,1:T(8,128)(2,1)} %bitcast.130, bf16[16,512,512]{2,1,0:T(8,128)(2,1)} %multiply_convert_fusion.5), kind=kOutput, calls=%fused_computation.26 | convolution fusion | flops 1073741824 | bytes 14680064 | tf_op jit(solution)/shard_map/hts,shp->thp/dot_general | solution.py:44
  112.1 5.4 %copy.67 = f32[512,2048]{1,0:T(8,128)} copy(f32[512,2048]{0,1:T(8,128)} %bitcast.122) | data formatting | bytes 8388608 | tf_op jit(solution)/shard_map/reshape | solution.py:45
  117.5 12.0 %conditional.4 = (f32[512,2048]{1,0:T(8,128)}) conditional(s32[]{:T(128)} %convert_element_type.517, () %tuple.29, (f32[512,128]{1,0:T(8,128)S(1)}, f32[128,2048]{1,0:T(8,128)}, f32[16,14,512]{2,0,1:T(8,128)S(1)}, pred[]{:T(512)}, f32[16,512]{1,0:T(8,128)S(1)}, /*index=5*/f32[16,512]{0,1:T(8,128)S(1)}) %tuple.85), branch_computations={%region_2.3_spmd, %region_3.4_spmd} | conditional | flops 1611677696 | bytes 15040521 | solution.py:119
  117.7 2.4 %copy.59 = f32[16,14,512]{0,2,1:T(8,128)} copy(f32[16,14,512]{2,0,1:T(8,128)S(1)} %get-tuple-element.258) | data formatting | bytes 917504 | tf_op jit(solution)/shard_map
  121.2 1.1 mul.57
  122.3 7.2 %bitcast_multiply_fusion = f32[512,2048]{1,0:T(8,128)} fusion(f32[64,8,16,128]{3,2,1,0:T(8,128)S(1)} %bitcast.124, f32[512,128]{1,0:T(8,128)S(1)} %get-tuple-element.74, f32[128,2048]{1,0:T(8,128)} %get-tuple-element.75), kind=kOutput, calls=%fused_computation | convolution fusion | flops 1611661312 | bytes 9699328 | tf_op jit(solution)/shard_map/cond/branch_1_fun/dot_general | solution.py:68
  129.5 12.9 %conditional.5 = (f32[512,2048]{1,0:T(8,128)}) conditional(s32[]{:T(128)} %convert_element_type.516, f32[512,2048]{1,0:T(8,128)} %get-tuple-element.322, (f32[512,128]{1,0:T(8,128)S(1)}, f32[128,2048]{1,0:T(8,128)}, f32[16,14,512]{2,0,1:T(8,128)S(1)}, f32[512,2048]{1,0:T(8,128)}, pred[]{:T(512)}, /*index=5*/f32[16,512]{1,0:T(8,128)S(1)}, ...), branch_computations={%region_4.5_spmd, %region_5.6_spmd} | conditional | flops 1612734464 | bytes 19234888 | solution.py:119
  129.5 2.4 %copy.61 = f32[16,14,512]{0,2,1:T(8,128)} copy(f32[16,14,512]{2,0,1:T(8,128)S(1)} %get-tuple-element.264) | data formatting | bytes 917504 | tf_op jit(solution)/shard_map
  132.0 1.0 fusion.4
  133.1 1.1 mul.60
  134.2 8.2 %fusion.2 = f32[512,2048]{1,0:T(8,128)} fusion(f32[512,2048]{1,0:T(8,128)} %get-tuple-element.77, f32[64,8,16,128]{3,2,1,0:T(8,128)S(1)} %bitcast.126, f32[512,128]{1,0:T(8,128)S(1)} %get-tuple-element.78, f32[128,2048]{1,0:T(8,128)} %get-tuple-element.79), kind=kOutput, calls=%fused_computation.6 | convolution fusion | flops 1612709888 | bytes 13893632 | tf_op jit(solution)/shard_map/cond/branch_1_fun/dot_general | solution.py:68
  142.4 12.9 %conditional.6 = (f32[512,2048]{1,0:T(8,128)}) conditional(s32[]{:T(128)} %convert_element_type.515, f32[512,2048]{1,0:T(8,128)} %get-tuple-element.323, (f32[512,128]{1,0:T(8,128)S(1)}, f32[128,2048]{1,0:T(8,128)}, f32[16,14,512]{2,0,1:T(8,128)S(1)}, f32[512,2048]{1,0:T(8,128)}, pred[]{:T(512)}, /*index=5*/f32[16,512]{1,0:T(8,128)S(1)}, ...), branch_computations={%region_6.7_spmd, %region_7.8_spmd} | conditional | flops 1612734464 | bytes 19234888 | solution.py:119
  142.4 2.4 %copy.63 = f32[16,14,512]{0,2,1:T(8,128)} copy(f32[16,14,512]{2,0,1:T(8,128)S(1)} %get-tuple-element.272) | data formatting | bytes 917504 | tf_op jit(solution)/shard_map
  146.0 1.1 mul.63
  147.1 8.2 %fusion.6 = f32[512,2048]{1,0:T(8,128)} fusion(f32[512,2048]{1,0:T(8,128)} %get-tuple-element.81, f32[64,8,16,128]{3,2,1,0:T(8,128)S(1)} %bitcast.127, f32[512,128]{1,0:T(8,128)S(1)} %get-tuple-element.82, f32[128,2048]{1,0:T(8,128)} %get-tuple-element.83), kind=kOutput, calls=%fused_computation.13 | convolution fusion | flops 1612709888 | bytes 13893632 | tf_op jit(solution)/shard_map/cond/branch_1_fun/dot_general | solution.py:68
  155.4 12.9 %conditional.7 = (f32[512,2048]{1,0:T(8,128)}) conditional(s32[]{:T(128)} %convert_element_type.514, f32[512,2048]{1,0:T(8,128)} %get-tuple-element.324, (f32[512,128]{1,0:T(8,128)S(1)}, f32[128,2048]{1,0:T(8,128)}, f32[16,14,512]{2,0,1:T(8,128)S(1)}, pred[]{:T(512)}, pred[]{:T(512)}, /*index=5*/f32[16]{0:T(128)S(1)}, f32[16]{0:T(128)S(1)}, ...), branch_computations={%region_8.9_spmd, %region_9.10_spmd} | conditional | flops 1612734464 | bytes 19235082 | solution.py:119
  155.4 2.4 %copy.65 = f32[16,14,512]{0,2,1:T(8,128)} copy(f32[16,14,512]{2,0,1:T(8,128)S(1)} %get-tuple-element.280) | data formatting | bytes 917504 | tf_op jit(solution)/shard_map
  158.9 1.1 mul.137
  160.1 8.2 %fusion.10 = f32[512,2048]{1,0:T(8,128)} fusion(f32[512,2048]{1,0:T(8,128)} %get-tuple-element.85, f32[64,8,16,128]{3,2,1,0:T(8,128)S(1)} %bitcast.128, f32[512,128]{1,0:T(8,128)S(1)} %get-tuple-element.86, f32[128,2048]{1,0:T(8,128)} %get-tuple-element.87), kind=kOutput, calls=%fused_computation.20 | convolution fusion | flops 1612709888 | bytes 13893632 | tf_op jit(solution)/shard_map/cond/branch_1_fun/dot_general | solution.py:68
  168.3 6.7 %multiply_bitcast_fusion = (f32[64,8,16,128]{3,1,2,0:T(8,128)S(1)}, f32[512,2048]{1,0:T(8,128)}) fusion(f32[512,2048]{1,0:T(8,128)} %copy.67, f32[512,2048]{1,0:T(8,128)} %get-tuple-element.325), kind=kLoop, calls=%fused_computation.66 | loop fusion | flops 2097152 | bytes 16777216
  175.0 2.9 %copy.77 = f32[64,8,16,128]{3,2,1,0:T(8,128)} copy(f32[64,8,16,128]{3,1,2,0:T(8,128)S(1)} %get-tuple-element.292) | data formatting | bytes 8388608
  177.9 3.4 %reduce_sum.9 = f32[512,16]{1,0:T(8,128)S(1)} reduce(f32[512,16,128]{2,1,0:T(8,128)} %bitcast.129, f32[]{:T(128)} %constant.14.clone.1), dimensions={2}, to_apply=%region_10.11 | reduce | flops 1040384 | bytes 4227076 | tf_op jit(solution)/shard_map/reduce_sum | solution.py:127
  181.5 1.1 mul.211
  182.6 1.0 copy-done.2
  183.7 3.1 %fusion.44 = bf16[512,2048]{1,0:T(8,128)(2,1)} fusion(f32[512,2048]{1,0:T(8,128)S(1)} %copy-done.2, f32[64,8,16,128]{3,2,1,0:T(8,128)S(1)} %bitcast.125, f32[2048]{0:T(1024)S(1)} %copy-done.18), kind=kLoop, calls=%fused_computation.63 | loop fusion | flops 3145728 | bytes 10493952 | tf_op jit(solution)/shard_map/convert_element_type | solution.py:128
  (78 shorter events, 8.9 us)
Async XLA Ops:
  0.0 2.1 %copy-start = (f32[16,512]{1,0:T(8,128)S(1)}, f32[16,512]{1,0:T(8,128)}, u32[]{:S(2)}) copy-start(f32[16,512]{1,0:T(8,128)} %param.15) | copy-start | bytes 98308
  0.8 4.2 %collective-permute-start = (bf16[3,2304]{1,0:T(4,128)(2,1)S(1)}, bf16[3,2304]{1,0:T(4,128)(2,1)S(1)}, u32[]{:S(2)}, u32[]{:S(2)}) collective-permute-start(bf16[3,2304]{1,0:T(4,128)(2,1)S(1)} %slice.88), channel_id=1, source_target_pairs={{0,1},{1,2},{2,3},{3,4},{4,5},{5,6},{6,7},{7,8},{8,9},{9,10},{10,1... | collective-permute-start | bytes 41480 | tf_op jit(solution)/shard_map/ppermute | solution.py:10
  13.7 4.2 %collective-permute-start.1 = (f32[128,2048]{1,0:T(8,128)}, f32[128,2048]{1,0:T(8,128)}, u32[]{:S(2)}, u32[]{:S(2)}) collective-permute-start(f32[128,2048]{1,0:T(8,128)} %fusion.46), channel_id=1, source_target_pairs={{0,1},{1,0},{2,3},{3,2},{4,5},{5,4},{6,7},{7,6},{8,9},{9,8},{10,11... | collective-permute-start | bytes 3145736 | tf_op jit(solution)/shard_map/ppermute | solution.py:14
  15.2 2.1 %collective-permute-start.2 = (f32[16]{0:T(128)S(1)}, f32[16]{0:T(128)S(1)}, u32[]{:S(2)}, u32[]{:S(2)}) collective-permute-start(f32[16]{0:T(128)S(1)} %slice_reduce_fusion.5), channel_id=1, source_target_pairs={{0,1},{1,0},{2,3},{3,2},{4,5},{5,4},{6,7},{7,6},{8,9},{9,8},{10,11... | collective-permute-start | bytes 200 | tf_op jit(solution)/shard_map/ppermute | solution.py:14
  16.7 34.0 %copy-start.3 = (f32[16,14,512]{2,0,1:T(8,128)S(1)}, f32[16,14,512]{2,0,1:T(8,128)}, u32[]{:S(2)}) copy-start(f32[16,14,512]{2,0,1:T(8,128)} %param.16) | copy-start | bytes 1376260
  20.5 24.8 %collective-permute-start.3 = (f32[128,2048]{1,0:T(8,128)}, f32[128,2048]{1,0:T(8,128)}, u32[]{:S(2)}, u32[]{:S(2)}) collective-permute-start(f32[128,2048]{1,0:T(8,128)} %select_add_fusion.2), channel_id=1, source_target_pairs={{0,2},{1,3},{2,0},{3,1},{4,6},{5,7},{6,4},{7,5},{8,10},{9,11},{10,... | collective-permute-start | bytes 3145736 | tf_op jit(solution)/shard_map/ppermute | solution.py:14
  25.5 19.8 %collective-permute-start.4 = (f32[16]{0:T(128)S(1)}, f32[16]{0:T(128)S(1)}, u32[]{:S(2)}, u32[]{:S(2)}) collective-permute-start(f32[16]{0:T(128)S(1)} %get-tuple-element.308), channel_id=1, source_target_pairs={{0,2},{1,3},{2,0},{3,1},{4,6},{5,7},{6,4},{7,5},{8,10},{9,11},{10,... | collective-permute-start | bytes 200 | tf_op jit(solution)/shard_map/ppermute | solution.py:14
  48.1 24.6 %collective-permute-start.5 = (f32[128,2048]{1,0:T(8,128)}, f32[128,2048]{1,0:T(8,128)}, u32[]{:S(2)}, u32[]{:S(2)}) collective-permute-start(f32[128,2048]{1,0:T(8,128)} %select_add_fusion.1), channel_id=1, source_target_pairs={{0,4},{1,5},{2,6},{3,7},{4,0},{5,1},{6,2},{7,3},{8,12},{9,13},{10,... | collective-permute-start | bytes 3145736 | tf_op jit(solution)/shard_map/ppermute | solution.py:14
  51.4 20.9 %collective-permute-start.6 = (f32[16]{0:T(128)S(1)}, f32[16]{0:T(128)S(1)}, u32[]{:S(2)}, u32[]{:S(2)}) collective-permute-start(f32[16]{0:T(128)S(1)} %get-tuple-element.306), channel_id=1, source_target_pairs={{0,4},{1,5},{2,6},{3,7},{4,0},{5,1},{6,2},{7,3},{8,12},{9,13},{10,... | collective-permute-start | bytes 200 | tf_op jit(solution)/shard_map/ppermute | solution.py:14
  51.4 25.4 %copy-start.4 = (pred[512,512]{1,0:T(8,128)(4,1)S(1)}, pred[512,512]{1,0:T(8,128)(4,1)}, u32[]{:S(2)}) copy-start(pred[512,512]{1,0:T(8,128)(4,1)} %get-tuple-element.314) | copy-start | bytes 786436
  51.4 25.4 %copy-start.5 = (pred[512,512]{1,0:T(8,128)(4,1)S(1)}, pred[512,512]{1,0:T(8,128)(4,1)}, u32[]{:S(2)}) copy-start(pred[512,512]{1,0:T(8,128)(4,1)} %get-tuple-element.315) | copy-start | bytes 786436
  51.4 25.4 %copy-start.6 = (pred[512,512]{1,0:T(8,128)(4,1)S(1)}, pred[512,512]{1,0:T(8,128)(4,1)}, u32[]{:S(2)}) copy-start(pred[512,512]{1,0:T(8,128)(4,1)} %get-tuple-element.316) | copy-start | bytes 786436
  51.4 25.3 %copy-start.7 = (pred[512,512]{1,0:T(8,128)(4,1)S(1)}, pred[512,512]{1,0:T(8,128)(4,1)}, u32[]{:S(2)}) copy-start(pred[512,512]{1,0:T(8,128)(4,1)} %get-tuple-element.317) | copy-start | bytes 786436
  51.4 25.3 %copy-start.8 = (pred[512,512]{1,0:T(8,128)(4,1)S(1)}, pred[512,512]{1,0:T(8,128)(4,1)}, u32[]{:S(2)}) copy-start(pred[512,512]{1,0:T(8,128)(4,1)} %get-tuple-element.318) | copy-start | bytes 786436
  51.4 25.3 %copy-start.9 = (pred[512,512]{1,0:T(8,128)(4,1)S(1)}, pred[512,512]{1,0:T(8,128)(4,1)}, u32[]{:S(2)}) copy-start(pred[512,512]{1,0:T(8,128)(4,1)} %get-tuple-element.319) | copy-start | bytes 786436
  51.4 25.3 %copy-start.10 = (pred[512,512]{1,0:T(8,128)(4,1)S(1)}, pred[512,512]{1,0:T(8,128)(4,1)}, u32[]{:S(2)}) copy-start(pred[512,512]{1,0:T(8,128)(4,1)} %get-tuple-element.320) | copy-start | bytes 786436
  51.4 25.3 %copy-start.11 = (pred[512,512]{1,0:T(8,128)(4,1)S(1)}, pred[512,512]{1,0:T(8,128)(4,1)}, u32[]{:S(2)}) copy-start(pred[512,512]{1,0:T(8,128)(4,1)} %get-tuple-element.321) | copy-start | bytes 786436
  51.4 25.3 %copy-start.12 = (pred[512,512]{1,0:T(8,128)(4,1)S(1)}, pred[512,512]{1,0:T(8,128)(4,1)}, u32[]{:S(2)}) copy-start(pred[512,512]{1,0:T(8,128)(4,1)} %broadcast_compare_fusion.9) | copy-start | bytes 786436
  51.4 25.3 %copy-start.13 = (f32[16,512]{1,0:T(8,128)S(1)}, f32[16,512]{1,0:T(8,128)}, u32[]{:S(2)}) copy-start(f32[16,512]{1,0:T(8,128)} %get-tuple-element.301) | copy-start | bytes 98308
  51.5 25.3 %copy-start.14 = (f32[16,512]{1,0:T(8,128)S(1)}, f32[16,512]{1,0:T(8,128)}, u32[]{:S(2)}) copy-start(f32[16,512]{1,0:T(8,128)} %get-tuple-element.302) | copy-start | bytes 98308
  51.5 25.3 %copy-start.15 = (f32[16,512]{1,0:T(8,128)S(1)}, f32[16,512]{1,0:T(8,128)}, u32[]{:S(2)}) copy-start(f32[16,512]{1,0:T(8,128)} %get-tuple-element.303) | copy-start | bytes 98308
  51.5 25.3 %copy-start.16 = (f32[16,512]{1,0:T(8,128)S(1)}, f32[16,512]{1,0:T(8,128)}, u32[]{:S(2)}) copy-start(f32[16,512]{1,0:T(8,128)} %get-tuple-element.304) | copy-start | bytes 98308
  51.5 25.3 %copy-start.17 = (f32[16,512]{1,0:T(8,128)S(1)}, f32[16,512]{1,0:T(8,128)}, u32[]{:S(2)}) copy-start(f32[16,512]{1,0:T(8,128)} %get-tuple-element.305) | copy-start | bytes 98308
  75.3 80.0 %collective-permute-start.7 = (f32[128,2048]{1,0:T(8,128)}, f32[128,2048]{1,0:T(8,128)}, u32[]{:S(2)}, u32[]{:S(2)}) collective-permute-start(f32[128,2048]{1,0:T(8,128)} %select_add_fusion), channel_id=1, source_target_pairs={{0,8},{1,9},{2,10},{3,11},{4,12},{5,13},{6,14},{7,15},{8,0},{9,1},... | collective-permute-start | bytes 3145736 | tf_op jit(solution)/shard_map/ppermute | solution.py:14
  177.9 4.8 %copy-start.18 = (f32[2048]{0:T(1024)S(1)}, f32[2048]{0:T(1024)}, u32[]{:S(2)}) copy-start(f32[2048]{0:T(1024)} %param.17) | copy-start | bytes 24580
  181.5 2.2 %copy-start.2 = (f32[512,2048]{1,0:T(8,128)S(1)}, f32[512,2048]{1,0:T(8,128)}, u32[]{:S(2)}) copy-start(f32[512,2048]{1,0:T(8,128)} %get-tuple-element.293) | copy-start | bytes 12582916
  182.6 4.1 %copy-start.1 = (f32[16,512]{1,0:T(8,128)S(1)}, f32[16,512]{1,0:T(8,128)}, u32[]{:S(2)}) copy-start(f32[16,512]{1,0:T(8,128)} %param.15) | copy-start | bytes 98308
where the time goes:
time: 187 us
  other arithmetic  58.4 us (31%)
  matrix products  43.5 us (23%)
  waiting for transfers between devices  41.6 us (22%)
  local copies, waits for them, and re-layouts  35.2 us (19%)
  starting transfers between devices  7.36 us (4%)
    ppermute x7, waiting for transfers between devices, swapped(): lax.ppermute(value, axis, [(i, i ^ 1 << apart) for i in range(lax.axis_si...  41.6 us
    dot_general x4, matrix products, add_level(): jnp.dot(queries_wide, partner, precision=lax.Precision.HIGHEST, preferred...  31.9 us
    dot_general x1, other arithmetic, compute_near(): jnp.einsum('hts,shp->thp', weight, shaped, preferred_element_type=jnp.flo...  20.9 us
    another operation x9, local copies, waits for them, and re-layouts  10.1 us
    dot_general x1, matrix products, compute_near(): jnp.einsum('hts,shp->thp', weight, shaped, preferred_element_type=jnp.flo...  8.79 us
    add x3, other arithmetic, combine_groups(): return left_part * carry_decay[None, :] + right_part  8.11 us
    unnamed x1, other arithmetic  6.66 us
    ppermute x7, starting transfers between devices, swapped(): lax.ppermute(value, axis, [(i, i ^ 1 << apart) for i in range(lax.axis_si...  6.07 us
  transfers between devices with their start and end apart: 8, of which 4 were waited for; matrix products, arithmetic and copies ran while one was open for 47% of the time, Pallas kernels for 0%

commit v1 on v0

v1 whole, which is shorter than its diff:
```python
import functools

import jax
import jax.numpy as jnp
from jax import lax
from jax.experimental import pallas as pl
from jax.experimental.pallas import tpu as pltpu
from jax.sharding import PartitionSpec as P

F32 = jnp.float32
BF16 = jnp.bfloat16
LANES = 128
GROUP = 8
PARTS = 3
VMEM_LIMIT = 24 << 20
HBM_SPEC = pl.BlockSpec(memory_space=pltpu.HBM)
VMEM_SPEC = pl.BlockSpec(memory_space=pltpu.VMEM)


def in_vmem(*arrays):
    return [pltpu.with_memory_space_constraint(array, pltpu.VMEM) for array in arrays]


def in_hbm(*arrays):
    return [pltpu.with_memory_space_constraint(array, pltpu.HBM) for array in arrays]


def params():
    return pltpu.CompilerParams(vmem_limit_bytes=VMEM_LIMIT)


def product(left, right):
    return jnp.dot(left, right, preferred_element_type=F32)


def write_spans(message_ref, first_row, spans):
    head_count = spans.shape[0]
    for part in range(PARTS):
        rounded = spans.astype(BF16)
        start = first_row + part * head_count
        message_ref[start : start + head_count, :] = rounded
        spans = spans - rounded.astype(F32)


def read_spans(message_ref, first_row, head_count):
    total = None
    for part in range(PARTS):
        start = first_row + part * head_count
        piece = message_ref[start : start + head_count, :].astype(F32)
        total = piece if total is None else total + piece
    return total


def running_sum(logs):
    column = lax.broadcasted_iota(jnp.int32, logs.shape, 1)
    shift = 1
    while shift < logs.shape[1]:
        logs = logs + jnp.where(column >= shift, pltpu.roll(logs, shift, 1), 0.0)
        shift *= 2
    return logs


def front_kernel(
    xbc_hbm, edge_ref, taps_hbm, decay_hbm, acts_ref, maps_ref, state_ref, message_ref, log_ref,
    xbc_buf, taps_buf, decay_buf, padded, sems, small_sems, chunk
):
    rows, width = xbc_buf.shape
    taps = taps_buf.shape[0]
    head_count = decay_buf.shape[0]
    state_size = maps_ref.shape[1]
    steps = width // chunk
    small = [
        pltpu.make_async_copy(decay_hbm, decay_buf, small_sems.at[0]),
        pltpu.make_async_copy(taps_hbm, taps_buf, small_sems.at[1]),
    ]
    copies = []
    for step in range(steps):
        part = pl.ds(step * chunk, chunk)
        copies.append(
            pltpu.make_async_copy(xbc_hbm.at[:, part], xbc_buf.at[:, part], sems.at[step])
        )
    for copy in small + copies[-1:] + copies[:-1]:
        copy.start()

    def activated(start):
        part = pl.ds(start, chunk)
        weights = taps_buf[:, part]
        values = xbc_buf[:, part].astype(F32)
        padded[GROUP : GROUP + rows, :] = values
        padded[GROUP - taps + 1 : GROUP, :] = edge_ref[:, part].astype(F32)
        total = None
        for tap in range(taps):
            first = GROUP - taps + 1 + tap
            shifted = values if tap == taps - 1 else padded[first : first + rows, :]
            term = shifted * weights[tap : tap + 1]
            total = term if total is None else total + term
        return (total / (1.0 + jnp.exp(-total))).astype(BF16)

    small[0].wait()
    local_log = running_sum(decay_buf[...])
    log_ref[...] = local_log
    totals = jnp.broadcast_to(local_log[:, rows - 1 : rows], (head_count, LANES))
    write_spans(message_ref, state_ref.shape[0], totals)
    small[1].wait()
    copies[-1].wait()
    last = activated(width - chunk)
    maps_ref[...] = last[:, :state_size]
    acts_ref[width - chunk :, :] = last.T
    per_chunk = chunk // state_size

    for step in range(steps - 1):
        copies[step].wait()
        turned = activated(step * chunk).T
        acts_ref[step * chunk : (step + 1) * chunk, :] = turned
        for part in range(per_chunk):
            head = step * per_chunk + part
            logs = log_ref[head : head + 1, :]
            tail = jnp.exp(logs[:, rows - 1 : rows] - logs)
            own = turned[part * LANES : (part + 1) * LANES].astype(F32)
            decayed = (own * tail).astype(BF16)
            state = product(decayed, maps_ref[...])
            state_ref[head * LANES : (head + 1) * LANES, :] = state
            message_ref[head * LANES : (head + 1) * LANES, :] = state.astype(BF16)


def front(xbc, edge, conv_weight, log_decay):
    rows, width = xbc.shape
    taps = conv_weight.shape[0]
    head_count = log_decay.shape[0]
    inner = head_count * LANES
    state_size = (width - inner) // 2
    chunk = 2 * state_size
    return pl.pallas_call(
        functools.partial(front_kernel, chunk=chunk),
        in_specs=[HBM_SPEC, VMEM_SPEC, HBM_SPEC, HBM_SPEC],
        out_specs=[VMEM_SPEC] * 5,
        out_shape=[
            pltpu.VMEM((width, rows), BF16),
            pltpu.VMEM((rows, state_size), BF16),
            pltpu.VMEM((inner, state_size), F32),
            pltpu.VMEM((inner + PARTS * head_count, state_size), BF16),
            pltpu.VMEM((head_count, rows), F32),
        ],
        scratch_shapes=[
            pltpu.VMEM((rows, width), BF16),
            pltpu.VMEM((taps, width), F32),
            pltpu.VMEM((head_count, rows), F32),
            pltpu.VMEM((rows + GROUP, chunk), F32),
            pltpu.SemaphoreType.DMA((width // chunk,)),
            pltpu.SemaphoreType.DMA((2,)),
        ],
        compiler_params=params(),
        name="front",
    )(*in_hbm(xbc), *in_vmem(edge), *in_hbm(conv_weight, log_decay))


def pair_kernel(state_ref, log_ref, got_ref, own_ref, stats_ref, send_ref, rest_ref, shards):
    head_count, rows = log_ref.shape
    inner = state_ref.shape[0]
    index = lax.axis_index("seq")
    is_upper = index % 2 == 1
    mine = jnp.broadcast_to(log_ref[:, rows - 1 : rows], (head_count, LANES))
    theirs = read_spans(got_ref, inner, head_count)
    stats_ref[0] = mine + theirs
    stats_ref[1] = jnp.where(is_upper, theirs, 0.0)
    write_spans(send_ref, inner // shards, mine + theirs)
    write_spans(rest_ref, inner // shards, mine + theirs)
    stats_ref[2] = jnp.exp(mine)
    stats_ref[3] = jnp.exp(theirs)
    shard = index % shards
    share = head_count // shards

    def joined(head):
        at = pl.ds(pl.multiple_of(head * LANES, LANES), LANES)
        own = state_ref[at, :]
        got = got_ref[at, :].astype(F32)
        late = jnp.where(is_upper, own, got)
        early = jnp.where(is_upper, got, own)
        late_row = jnp.where(is_upper, 2, 3)
        return early * stats_ref[late_row, pl.ds(head, 1), :] + late

    for local in range(share):
        place = slice(local * LANES, (local + 1) * LANES)
        send_ref[place, :] = joined((shard ^ 2) * share + local).astype(BF16)
        kept = joined(shard * share + local)
        own_ref[place, :] = kept
        rest_ref[place, :] = kept.astype(BF16)


def pair(state, log, got, shards):
    head_count, _ = log.shape
    inner, state_size = state.shape
    part = inner // shards
    spans = PARTS * head_count
    return pl.pallas_call(
        functools.partial(pair_kernel, shards=shards),
        in_specs=[VMEM_SPEC] * 3,
        out_specs=[VMEM_SPEC] * 4,
        out_shape=[
            pltpu.VMEM((part, state_size), F32),
            pltpu.VMEM((4, head_count, LANES), F32),
            pltpu.VMEM((part + spans, state_size), BF16),
            pltpu.VMEM((part + spans, state_size), BF16),
        ],
        compiler_params=params(),
        name="pair",
    )(*in_vmem(state, log, got))


def join_kernel(own_ref, stats_ref, got_ref, _, *refs, bit, shards, gathered):
    sources = refs[:gathered]
    if gathered:
        next_stats_ref, send_ref, across_ref = refs[gathered:]
    else:
        next_stats_ref, send_ref, next_ref = refs
    part = own_ref.shape[0]
    head_count = stats_ref.shape[1]
    share = head_count // shards
    index = lax.axis_index("seq")
    is_upper = (index >> bit) % 2 == 1
    mine = stats_ref[0]
    theirs = read_spans(got_ref, part, head_count)
    next_stats_ref[0] = mine + theirs
    next_stats_ref[1] = stats_ref[1] + jnp.where(is_upper, theirs, 0.0)
    next_stats_ref[2] = jnp.exp(jnp.where(is_upper, mine, theirs))
    next_stats_ref[3] = jnp.zeros_like(mine)
    write_spans(send_ref, part, mine + theirs)
    for local in range(share):
        place = slice(local * LANES, (local + 1) * LANES)
        head = (index % shards) * share + local
        own = own_ref[place, :]
        got = got_ref[place, :].astype(F32)
        late = jnp.where(is_upper, own, got)
        early = jnp.where(is_upper, got, own)
        total = early * next_stats_ref[2, pl.ds(head, 1), :] + late
        send_ref[place, :] = total.astype(BF16)
        if not gathered:
            next_ref[place, :] = total
    for slot in range(gathered):
        across_ref[slot * part : (slot + 1) * part, :] = sources[slot][:part, :]


def join(own, stats, got, after, bit, shards, sources):
    operands = [own, stats, got, after, *sources]
    out_shape = [pltpu.VMEM(stats.shape, F32), pltpu.VMEM(got.shape, BF16)]
    if sources:
        out_shape.append(pltpu.VMEM((len(sources) * own.shape[0], own.shape[1]), BF16))
    else:
        out_shape.append(pltpu.VMEM(own.shape, F32))
    return pl.pallas_call(
        functools.partial(join_kernel, bit=bit, shards=shards, gathered=len(sources)),
        in_specs=[VMEM_SPEC] * len(operands),
        out_specs=[VMEM_SPEC] * 3,
        out_shape=out_shape,
        compiler_params=params(),
        name="join",
    )(*in_vmem(*operands))


def bit_length(numbers, limit):
    counted = jnp.zeros(numbers.shape, jnp.int32)
    for power in range(limit):
        counted = counted + (numbers >= 1 << power).astype(jnp.int32)
    return counted


def near_kernel(*refs, first, wide, heads):
    if first:
        acts_ref, maps_ref, log_ref, gains_ref, node_ref, _ = refs[:6]
        near_ref, scores, tails, turned, weights = refs[6:]
    else:
        acts_ref, maps_ref, log_ref, gains_ref, node_ref, _, scores, tails, _ = refs[:9]
        near_ref, turned, weights = refs[9:]
    head_count, rows = log_ref.shape
    inner = head_count * LANES
    state_size = maps_ref.shape[1]
    tiles = rows // LANES
    tile_bits = tiles.bit_length() - 1
    groups = LANES // GROUP
    low_bits = GROUP.bit_length() - 1
    tile_levels = LANES.bit_length() - 1
    queries = acts_ref[inner + state_size :, :]
    middle = LANES // 2 - 1
    if first:
        for start in range(0, rows, wide):
            upto = start + wide
            scores[:upto, start:upto] = product(maps_ref[:upto, :], queries[:, start:upto])
        turned[head_count:, :] = jnp.zeros((LANES - head_count, rows), F32)
        turned[:head_count, :] = log_ref[...]
        columns = [turned[:, tile * LANES : (tile + 1) * LANES].T for tile in range(tiles)]
        for tile in range(tiles):
            place = slice(tile * LANES, (tile + 1) * LANES)
            tails[0, place, :] = jnp.exp(columns[tile][middle : middle + 1] - columns[tile])
            for bit in range(tile_bits):
                if tile >> bit & 1 == 0:
                    edge = ((tile >> bit) + 1 << bit) - 1
                    tails[1 + bit, place, :] = jnp.exp(columns[edge][LANES - 1 :] - columns[tile])
    for late in range(tiles):
        for early in range(tiles):
            if early > late:
                weights[
                    :, early * LANES : (early + 1) * LANES, late * LANES : (late + 1) * LANES
                ] = jnp.zeros((weights.shape[0], LANES, LANES), BF16)
    lane = lax.broadcasted_iota(jnp.int32, (GROUP, LANES), 1)
    row = lax.broadcasted_iota(jnp.int32, (GROUP, LANES), 0)
    inside = bit_length((lane % GROUP) ^ row, low_bits)
    ahead = row <= lane % GROUP
    lane_group = lax.broadcasted_iota(jnp.int32, (groups, LANES), 1) // GROUP
    row_group = lax.broadcasted_iota(jnp.int32, (groups, LANES), 0)
    between = bit_length(lane_group ^ row_group, groups.bit_length() - 1)
    before = row_group < lane_group
    same = (
        lax.broadcasted_iota(jnp.int32, (groups, 1, LANES), 2) // GROUP
        == lax.broadcasted_iota(jnp.int32, (groups, 1, LANES), 0)
    )
    is_upper = lax.axis_index("seq") % 2 == 1

    def spread(kind, place, head):
        chosen = jnp.full((LANES, LANES), head, jnp.int32)
        return jnp.take_along_axis(
            tails[kind, place, :], chosen, axis=1, mode="promise_in_bounds"
        )

    def one_head(head, slot):
        logs = log_ref[pl.ds(head, 1), :]
        gain_rows = [
            gains_ref[pl.ds(level * head_count + head, 1), :]
            for level in range(tile_levels + tile_bits + 2)
        ]
        for late in range(tiles):
            span = slice(late * LANES, (late + 1) * LANES)
            own = logs[:, span]
            start = late * LANES + middle
            grown = jnp.exp(own - logs[:, start : start + 1])
            corner = jnp.zeros((GROUP, LANES), F32)
            for level in range(low_bits + 1):
                gain = gain_rows[level][:, span] * grown
                corner = jnp.where(ahead & (inside == level), gain, corner)
            rest = jnp.zeros((groups, LANES), F32)
            for level in range(low_bits + 1, tile_levels + 1):
                gain = gain_rows[level][:, span] * grown
                rest = jnp.where(before & (between == level - low_bits), gain, rest)
            chosen = jnp.where(same, corner[None], rest[:, None, :]).reshape(LANES, LANES)
            weight = chosen * spread(0, span, head) * scores[span, span]
            weights[slot, span, span] = weight.astype(BF16)
            for bit in range(tile_bits):
                if late >> bit & 1 == 0:
                    continue
                edge = (late >> bit << bit) * LANES - 1
                level = tile_levels + 1 + bit
                factor = gain_rows[level][:, span] * jnp.exp(
                    own - logs[:, edge : edge + 1]
                )
                for early in range(((late >> bit) - 1) << bit, (late >> bit) << bit):
                    place = slice(early * LANES, (early + 1) * LANES)
                    weight = spread(1 + bit, place, head) * factor * scores[place, span]
                    weights[slot, place, span] = weight.astype(BF16)
        at = pl.ds(pl.multiple_of(head * LANES, LANES), LANES)
        level = tile_levels + tile_bits + 1
        factor = gain_rows[level] * jnp.exp(jnp.where(is_upper, logs, -1e30))
        far = product(node_ref[at, :], queries) * factor
        for start in range(0, rows, wide):
            upto = start + wide
            near_ref[at, start:upto] = far[:, start:upto] + product(
                acts_ref[at, :upto], weights[slot, :upto, start:upto]
            )

    def some_heads(step, carry):
        for slot in range(weights.shape[0]):
            one_head(step * weights.shape[0] + slot, slot)
        return carry

    lax.fori_loop(heads[0] // weights.shape[0], heads[1] // weights.shape[0], some_heads, 0)


def near(acts, maps, log, gains, node, after, earlier, heads):
    head_count, rows = log.shape
    wide = min(rows, 2 * LANES)
    tile_bits = (rows // LANES).bit_length() - 1
    first = earlier is None
    out_shape = [pltpu.VMEM((head_count * LANES, rows), F32)]
    operands = [acts, maps, log, gains, node, after]
    aliases = {}
    if first:
        out_shape.append(pltpu.VMEM((rows, rows), F32))
        out_shape.append(pltpu.VMEM((1 + tile_bits, rows, LANES), F32))
    else:
        near_term, scores, tails = earlier
        operands += [scores, tails, near_term]
        aliases = {len(operands) - 1: 0}
    made = pl.pallas_call(
        functools.partial(near_kernel, first=first, wide=wide, heads=heads),
        in_specs=[VMEM_SPEC] * len(operands),
        out_specs=[VMEM_SPEC] * len(out_shape),
        out_shape=out_shape,
        input_output_aliases=aliases,
        scratch_shapes=[
            pltpu.VMEM((LANES, rows), F32),
            pltpu.VMEM((2, rows, rows), BF16),
        ],
        compiler_params=params(),
        cost_estimate=pl.CostEstimate(
            flops=2 * head_count * rows * rows * LANES, bytes_accessed=10 << 20, transcendentals=0
        ),
        name="near",
    )(*in_vmem(*operands))
    return [made[0], *earlier[1:]] if not first else made


def far_product(node_ref, first_row, count, queries):
    return product(node_ref[first_row : first_row + count, :], queries)


def far_factor(gains_ref, log_ref, stats_ref, head, level, base):
    is_upper = (lax.axis_index("seq") >> level) % 2 == 1
    shift = stats_ref[1, pl.ds(head, 1), :][:, :1]
    exponent = jnp.where(is_upper, log_ref[pl.ds(head, 1), :] + shift, -1e30)
    row = (base + level) * log_ref.shape[0] + head
    return gains_ref[pl.ds(row, 1), :] * jnp.exp(exponent)


def middle_kernel(*refs, places, levels, shards):
    count = len(places)
    acts_ref, log_ref, gains_ref = refs[:3]
    stats = refs[3 : 3 + count]
    sources = refs[3 + count : -2]
    total_ref = refs[-1]
    head_count, _ = log_ref.shape
    part = head_count // shards * LANES
    inner = head_count * LANES
    state_size = acts_ref.shape[0] - inner >> 1
    shard = lax.axis_index("seq") % shards
    base = gains_ref.shape[0] // head_count - levels
    queries = acts_ref[inner + state_size :, :]
    for relative in range(shards):
        terms = []
        for slot in range(count):
            source, start = places[slot][relative]
            terms.append(far_product(sources[source], start, part, queries))
        for local in range(head_count // shards):
            head = (relative ^ shard) * (head_count // shards) + local
            at = pl.ds(pl.multiple_of(head * LANES, LANES), LANES)
            total = total_ref[at, :]
            for slot in range(count):
                factor = far_factor(gains_ref, log_ref, stats[slot], head, slot + 1, base)
                total = total + terms[slot][local * LANES : (local + 1) * LANES] * factor
            total_ref[at, :] = total


def middle(near_term, acts, log, gains, stats, sources, places, levels, shards):
    operands = [acts, log, gains, *stats, *sources, near_term]
    return pl.pallas_call(
        functools.partial(middle_kernel, places=places, levels=levels, shards=shards),
        in_specs=[VMEM_SPEC] * len(operands),
        out_specs=VMEM_SPEC,
        out_shape=pltpu.VMEM(near_term.shape, F32),
        input_output_aliases={len(operands) - 1: 0},
        compiler_params=params(),
        name="middle",
    )(*in_vmem(*operands))


def last_kernel(
    total_ref, acts_ref, log_ref, gains_ref, gain_ref, stats_ref, node_a, node_b, *rest,
    starts, level, relatives, shards, base
):
    out_hbm, turned, out_buf, out_sems = rest[-4:]
    head_count, rows = log_ref.shape
    share = head_count // shards
    part = share * LANES
    inner = head_count * LANES
    state_size = acts_ref.shape[0] - inner >> 1
    shard = lax.axis_index("seq") % shards
    turned[...] = jnp.zeros_like(turned)
    turned[:head_count, :] = gain_ref[...]
    gain_columns = turned[...].T
    queries = acts_ref[inner + state_size :, :]
    copies = []
    for relative, node_ref, start in zip(relatives, (node_a, node_b), starts):
        term = far_product(node_ref, start, part, queries)
        for local in range(share):
            head = (relative ^ shard) * share + local
            at = pl.ds(pl.multiple_of(head * LANES, LANES), LANES)
            factor = far_factor(gains_ref, log_ref, stats_ref, head, level, base)
            total = total_ref[at, :] + term[local * LANES : (local + 1) * LANES] * factor
            mean = jnp.mean(total * total, axis=0, keepdims=True)
            scale = lax.rsqrt(mean + 1e-05)
            chosen = jnp.full((LANES, LANES), head, jnp.int32)
            column = jnp.take_along_axis(gain_columns, chosen, axis=1, mode="promise_in_bounds")
            column = jnp.concatenate([column] * (rows // LANES), axis=1)
            slot = len(copies)
            out_buf[slot] = (total * scale * column).astype(BF16).T
            copy = pltpu.make_async_copy(out_buf.at[slot], out_hbm.at[:, at], out_sems.at[slot])
            copy.start()
            copies.append(copy)
    for copy in copies:
        copy.wait()


def last(
    total, acts, log, gains, gain, stats, nodes, starts, level, levels, relatives, shards, mixed
):
    head_count, rows = log.shape
    count = head_count // shards * len(relatives)
    operands = in_vmem(total, acts, log, gains, gain.reshape(head_count, LANES), stats, *nodes)
    specs = [VMEM_SPEC] * len(operands)
    aliases = {}
    if mixed is not None:
        aliases = {len(operands): 0}
        operands.append(mixed)
        specs.append(HBM_SPEC)
    return pl.pallas_call(
        functools.partial(
            last_kernel, starts=starts, level=level, relatives=relatives, shards=shards,
            base=gains.shape[0] // head_count - levels,
        ),
        in_specs=specs,
        out_specs=HBM_SPEC,
        out_shape=jax.ShapeDtypeStruct((rows, head_count * LANES), BF16),
        input_output_aliases=aliases,
        scratch_shapes=[
            pltpu.VMEM((LANES, LANES), F32),
            pltpu.VMEM((count, rows, LANES), BF16),
            pltpu.SemaphoreType.DMA((count,)),
        ],
        compiler_params=params(),
        name="last",
    )(*operands)


def moved(value, apart, chosen=lambda index: True):
    devices = range(lax.axis_size("seq"))
    return lax.ppermute(value, "seq", [(i, i ^ apart) for i in devices if chosen(i)])


def on_device(xbc, conv_weight, log_decay, level_weights, gain):
    taps = conv_weight.shape[0]
    rows = xbc.shape[0]
    head_count = log_decay.shape[0]
    devices = lax.axis_size("seq")
    levels = devices.bit_length() - 1
    shards = 4
    part = head_count * LANES // shards
    gains = level_weights.transpose(1, 0, 2).reshape(-1, rows)
    behind = [(i, i + 1) for i in range(devices - 1)]
    edge = lax.ppermute(xbc[rows - taps + 1 :], "seq", behind)
    acts, maps, state, message, log = front(xbc, edge, conv_weight, log_decay)
    first_node = moved(message, 1)
    own, stats, send, rest = pair(state, log, first_node, shards)
    near_made = None
    all_stats = [stats]
    got = []
    for bit in range(1, levels - 1):
        got.append(moved(send, 1 << bit))
        if bit <= 2:
            half = head_count // 2
            heads = (half * (bit - 1), half * bit)
            near_made = near(acts, maps, log, gains, first_node, stats, near_made, heads)
        sources = [rest, *got[1:]] if bit == levels - 2 else []
        stats, send, own = join(own, stats, got[-1], near_made[0], bit, shards, sources)
        all_stats.append(stats)
    top = levels - 1

    def is_upper(index):
        return index >> top & 1 == 1

    across = moved(own, 2)
    node = moved(send, 1 << top, lambda index: index >> top & 1 == 0)
    node_across = moved(node, 2, is_upper)
    beside = moved(jnp.concatenate([*[kept[:part] for kept in got], across, node[:part]]), 1)
    count = len(got)
    places = [
        [(slot, 0), (count + 1, slot * part), (count, slot * part),
         (count + 1, (count + slot) * part)]
        for slot in range(count)
    ]
    total = middle(
        near_made[0], acts, log, gains, all_stats[:count], [*got, across, beside], places, levels,
        shards,
    )

    common = (acts, log, gains, gain, all_stats[-1])
    mixed = last(
        total, *common, (node, beside), (0, 2 * count * part), top, levels, (0, 1), shards, None
    )
    node_corner = moved(node_across, 1, is_upper)
    return last(
        total, *common, (node_across, node_corner), (0, 0), top, levels, (2, 3), shards, mixed
    )


def solution(mesh):
    in_specs = (
        P(("groups", "seq"), None),
        P(),
        P(None, ("groups", "seq")),
        P(None, None, ("groups", "seq")),
        P(),
    )
    out_specs = P(("groups", "seq"), None)
    return jax.shard_map(
        on_device, mesh=mesh, in_specs=in_specs, out_specs=out_specs, check_vma=False
    )
```

time: 187 us -> 54.3 us (0.29)
  the two profiles are of different devices: /device:TPU:27 before, /device:TPU:25 now
where the time goes in v1:
time: 54.3 us; the launch traced here: 54 us
  Pallas kernels  19.1 us (35%)
  starting transfers between devices  17.7 us (33%)
  waiting for transfers between devices  16.1 us (30%)
  local copies, waits for them, and re-layouts  0.88 us (2%)
    ppermute x8, waiting for transfers between devices, moved(): lax.ppermute(value, 'seq', [(i, i ^ apart) for i in devices if chosen(i)])  15.3 us
    ppermute x8, starting transfers between devices, moved(): lax.ppermute(value, 'seq', [(i, i ^ apart) for i in devices if chosen(i)])  14 us
    pallas_call x1, Pallas kernels, front(): pl.pallas_call(functools.partial(front_kernel, chunk=chunk), in_specs=[HB...  7.75 us
    pallas_call x2, Pallas kernels, near(): pl.pallas_call(functools.partial(near_kernel, first=first, wide=wide, hea...  5.87 us
    pallas_call x2, Pallas kernels, last(): pl.pallas_call(functools.partial(last_kernel, starts=starts, level=level,...  3.75 us
    ppermute x1, starting transfers between devices, on_device(): edge = lax.ppermute(xbc[rows - taps + 1:], 'seq', behind)  3.68 us
    pallas_call x1, Pallas kernels, middle(): pl.pallas_call(functools.partial(middle_kernel, places=places, levels=lev...  1.47 us
  transfers between devices with their start and end apart: 9, of which 6 were waited for; matrix products, arithmetic and copies ran while one was open for 0% of the time, Pallas kernels for 17%

profile of v1, /device:TPU:25, one launch (start us, length us, event | category | flops | bytes accessed | tf_op | source)
XLA Modules:
  0.0 54.0 jit_solution(7240067909110871680)
XLA Ops:
  0.0 0.0 copy-start
  0.0 0.8 %slice.12 = bf16[3,2304]{1,0:T(4,128)(2,1)S(1)} slice(bf16[512,2304]{1,0:T(8,128)(2,1)} %xbc_hbm.1), slice={[509:512], [0:2304]} | slice | bytes 27648 | tf_op jit(solution)/shard_map/slice | solution.py:546
  0.8 3.7 %collective-permute-start = (bf16[3,2304]{1,0:T(4,128)(2,1)S(1)}, bf16[3,2304]{1,0:T(4,128)(2,1)S(1)}, u32[]{:S(2)}, u32[]{:S(2)}) collective-permute-start(bf16[3,2304]{1,0:T(4,128)(2,1)S(1)} %slice.12), channel_id=1, source_target_pairs={{0,1},{1,2},{2,3},{3,4},{4,5},{5,6},{6,7},{7,8},{8,9},{9,10},{10,1... | collective-permute-start | bytes 41480 | tf_op jit(solution)/shard_map/ppermute | solution.py:546
  4.5 0.9 %collective-permute-done.edge_ref = bf16[3,2304]{1,0:T(4,128)(2,1)S(1)} collective-permute-done((bf16[3,2304]{1,0:T(4,128)(2,1)S(1)}, bf16[3,2304]{1,0:T(4,128)(2,1)S(1)}, u32[]{:S(2)}, u32[]{:S(2)}) %collective-permute-start) | collective-permute-done | bytes 13856 | tf_op jit(solution)/shard_map/ppermute | solution.py:546
  5.4 7.8 %front.1 = (bf16[2304,512]{1,0:T(8,128)(2,1)S(1)}, bf16[512,128]{1,0:T(8,128)(2,1)S(1)}, f32[2048,128]{1,0:T(8,128)S(1)}, bf16[2096,128]{1,0:T(8,128)(2,1)S(1)}, f32[16,512]{1,0:T(8,128)S(1)}) custom-call(bf16[512,2304]{1,0:T(8,128)(2,1)} %xbc_hbm.1, bf16[3,2304]{1,0:T(4,128)(2,1)S(1)} %collective-permute-done.edge_ref, f32[4,2304]{1,0:T(4,128)} %taps_hbm.1, ...), custom_call_target="tpu_custom_call" | custom-call | tf_op jit(solution)/shard_map/front/pallas_call | solution.py:133
  13.2 2.2 %collective-permute-start.1 = (bf16[2096,128]{1,0:T(8,128)(2,1)S(1)}, bf16[2096,128]{1,0:T(8,128)(2,1)S(1)}, u32[]{:S(2)}, u32[]{:S(2)}) collective-permute-start(bf16[2096,128]{1,0:T(8,128)(2,1)S(1)} %get-tuple-element.26), channel_id=1, source_target_pairs={{0,1},{1,0},{2,3},{3,2},{4,5},{5,4},{6,7},{7,6},{8,9},{9,8},{10,11... | collective-permute-start | bytes 1609736 | tf_op jit(solution)/shard_map/ppermute | solution.py:533
  15.3 1.6 %collective-permute-done.1.got_ref.refs_4_ = bf16[2096,128]{1,0:T(8,128)(2,1)S(1)} collective-permute-done((bf16[2096,128]{1,0:T(8,128)(2,1)S(1)}, bf16[2096,128]{1,0:T(8,128)(2,1)S(1)}, u32[]{:S(2)}, u32[]{:S(2)}) %collective-permute-start.1) | collective-permute-done | bytes 536608 | tf_op jit(solution)/shard_map/ppermute | solution.py:533
  16.9 0.1 pair.1
  17.0 0.4 collective-permute-start.2
  17.4 0.0 copy-done
  17.4 3.1 %near.2 = (f32[2048,512]{1,0:T(8,128)S(1)}, f32[512,512]{1,0:T(8,128)S(1)}, f32[3,512,128]{2,1,0:T(8,128)S(1)}) custom-call(bf16[2304,512]{1,0:T(8,128)(2,1)S(1)} %get-tuple-element.23.refs_0_.acts_ref, bf16[512,128]{1,0:T(8,128)(2,1)S(1)} %get-tuple-element.30.refs_1_, f32[16,512]{1,0:T(8,128)S(1)} %get-tuple-element.24.log_ref.refs_2_.refs_1_, ...), custom_call_target="tpu_custom_call" | custom-call | flops 1073741824 | bytes 10485760 | tf_op jit(solution)/shard_map/near/pallas_call | solution.py:391
  20.5 1.6 %collective-permute-done.2.got_ref.refs_5_ = bf16[560,128]{1,0:T(8,128)(2,1)S(1)} collective-permute-done((bf16[560,128]{1,0:T(8,128)(2,1)S(1)}, bf16[560,128]{1,0:T(8,128)(2,1)S(1)}, u32[]{:S(2)}, u32[]{:S(2)}) %collective-permute-start.2) | collective-permute-done | bytes 143392 | tf_op jit(solution)/shard_map/ppermute | solution.py:533
  22.1 0.1 join.2
  22.1 0.2 collective-permute-start.3
  22.4 2.8 %near.3._.refs_9_ = f32[2048,512]{1,0:T(8,128)S(1)} custom-call(bf16[2304,512]{1,0:T(8,128)(2,1)S(1)} %get-tuple-element.23.refs_0_.acts_ref, bf16[512,128]{1,0:T(8,128)(2,1)S(1)} %get-tuple-element.30.refs_1_, f32[16,512]{1,0:T(8,128)S(1)} %get-tuple-element.24.log_ref.refs_2_.refs_1_, f32[224,512]{1,0:T(8,128)S(1)} %bitcast.5, ...), custom_call_target="tpu_custom_call", output_to_operand_aliasing={{}: (8, {})} | custom-call | flops 1073741824 | bytes 10485760 | tf_op jit(solution)/shard_map/near/pallas_call | solution.py:391
  25.2 1.0 %collective-permute-done.3.got_ref.refs_1_.refs_6_ = bf16[560,128]{1,0:T(8,128)(2,1)S(1)} collective-permute-done((bf16[560,128]{1,0:T(8,128)(2,1)S(1)}, bf16[560,128]{1,0:T(8,128)(2,1)S(1)}, u32[]{:S(2)}, u32[]{:S(2)}) %collective-permute-start.3) | collective-permute-done | bytes 143392 | tf_op jit(solution)/shard_map/ppermute | solution.py:533
  26.2 0.1 join.3
  26.2 0.4 collective-permute-start.4
  26.6 1.3 %collective-permute-start.5 = (bf16[560,128]{1,0:T(8,128)(2,1)S(1)}, bf16[560,128]{1,0:T(8,128)(2,1)S(1)}, u32[]{:S(2)}, u32[]{:S(2)}) collective-permute-start(bf16[560,128]{1,0:T(8,128)(2,1)S(1)} %get-tuple-element.39), channel_id=1, source_target_pairs={{0,8},{1,9},{2,10},{3,11},{4,12},{5,13},{6,14},{7,15},{16,24},{17,... | collective-permute-start | bytes 430088 | tf_op jit(solution)/shard_map/ppermute | solution.py:533
  28.0 7.0 %collective-permute-done.5.node_a = bf16[560,128]{1,0:T(8,128)(2,1)S(1)} collective-permute-done((bf16[560,128]{1,0:T(8,128)(2,1)S(1)}, bf16[560,128]{1,0:T(8,128)(2,1)S(1)}, u32[]{:S(2)}, u32[]{:S(2)}) %collective-permute-start.5) | collective-permute-done | bytes 143392 | tf_op jit(solution)/shard_map/ppermute | solution.py:533
  34.9 0.0 collective-permute-done.4.refs_7_
  35.0 0.0 copy-start.1
  35.0 3.8 %collective-permute-start.6 = (bf16[2560,128]{1,0:T(8,128)(2,1)S(1)}, bf16[2560,128]{1,0:T(8,128)(2,1)S(1)}, u32[]{:S(2)}, u32[]{:S(2)}) collective-permute-start(bf16[2560,128]{1,0:T(8,128)(2,1)S(1)} %pad_maximum_fusion), channel_id=1, source_target_pairs={{0,1},{1,0},{2,3},{3,2},{4,5},{5,4},{6,7},{7,6},{8,9},{9,8},{10,11... | collective-permute-start | bytes 1966088 | tf_op jit(solution)/shard_map/ppermute | solution.py:533
  38.8 3.0 %collective-permute-start.7 = (bf16[560,128]{1,0:T(8,128)(2,1)S(1)}, bf16[560,128]{1,0:T(8,128)(2,1)S(1)}, u32[]{:S(2)}, u32[]{:S(2)}) collective-permute-start(bf16[560,128]{1,0:T(8,128)(2,1)S(1)} %collective-permute-done.5.node_a), channel_id=1, source_target_pairs={{8,10},{9,11},{10,8},{11,9},{12,14},{13,15},{14,12},{15,13},{24,26... | collective-permute-start | bytes 430088 | tf_op jit(solution)/shard_map/ppermute | solution.py:533
  41.9 4.2 %collective-permute-done.7.node_a = bf16[560,128]{1,0:T(8,128)(2,1)S(1)} collective-permute-done((bf16[560,128]{1,0:T(8,128)(2,1)S(1)}, bf16[560,128]{1,0:T(8,128)(2,1)S(1)}, u32[]{:S(2)}, u32[]{:S(2)}) %collective-permute-start.7) | collective-permute-done | bytes 143392 | tf_op jit(solution)/shard_map/ppermute | solution.py:533
  46.1 2.7 %collective-permute-start.8 = (bf16[560,128]{1,0:T(8,128)(2,1)S(1)}, bf16[560,128]{1,0:T(8,128)(2,1)S(1)}, u32[]{:S(2)}, u32[]{:S(2)}) collective-permute-start(bf16[560,128]{1,0:T(8,128)(2,1)S(1)} %collective-permute-done.7.node_a), channel_id=1, source_target_pairs={{8,9},{9,8},{10,11},{11,10},{12,13},{13,12},{14,15},{15,14},{24,25... | collective-permute-start | bytes 430088 | tf_op jit(solution)/shard_map/ppermute | solution.py:533
  48.8 0.0 collective-permute-done.6.refs_8_.node_b
  48.8 1.5 %middle.1.total_ref = f32[2048,512]{1,0:T(8,128)S(1)} custom-call(bf16[2304,512]{1,0:T(8,128)(2,1)S(1)} %get-tuple-element.23.refs_0_.acts_ref, f32[16,512]{1,0:T(8,128)S(1)} %get-tuple-element.24.log_ref.refs_2_.refs_1_, f32[224,512]{1,0:T(8,128)S(1)} %bitcast.6, ...), custom_call_target="tpu_custom_call", output_to_operand_aliasing={{}: (9, {})} | custom-call | tf_op jit(solution)/shard_map/middle/pallas_call | solution.py:452
  50.3 0.0 copy-done.1
  50.3 1.9 %last.2.rest_0_ = bf16[512,2048]{1,0:T(8,128)(2,1)} custom-call(f32[2048,512]{1,0:T(8,128)S(1)} %middle.1.total_ref, bf16[2304,512]{1,0:T(8,128)(2,1)S(1)} %get-tuple-element.23.refs_0_.acts_ref, f32[16,512]{1,0:T(8,128)S(1)} %get-tuple-element.24.log_ref.refs_2_.refs_1_, f32[224,512]{1,0:T(8,128)S(1)} %bitcast.7, f32[16,128]{1,0:T(8,128)S(1)} %bitcast.9, ...), custom_call_target="tpu_custom_call" | custom-call | tf_op jit(solution)/shard_map/last/pallas_call | solution.py:512
  52.1 0.0 collective-permute-done.8.node_b
  52.2 1.9 %last.3 = bf16[512,2048]{1,0:T(8,128)(2,1)} custom-call(f32[2048,512]{1,0:T(8,128)S(1)} %middle.1.total_ref, bf16[2304,512]{1,0:T(8,128)(2,1)S(1)} %get-tuple-element.23.refs_0_.acts_ref, f32[16,512]{1,0:T(8,128)S(1)} %get-tuple-element.24.log_ref.refs_2_.refs_1_, f32[224,512]{1,0:T(8,128)S(1)} %bitcast.8, ...), custom_call_target="tpu_custom_call", output_to_operand_aliasing={{}: (8, {})} | custom-call | tf_op jit(solution)/shard_map/last/pallas_call | solution.py:512
  (4 shorter events, 0.1 us)
Async XLA Ops:
  0.0 17.4 %copy-start = (f32[16,14,512]{2,0,1:T(8,128)S(1)}, f32[16,14,512]{2,0,1:T(8,128)}, u32[]{:S(2)}) copy-start(f32[16,14,512]{2,0,1:T(8,128)} %param.8) | copy-start | bytes 1376260
  0.8 4.6 %collective-permute-start = (bf16[3,2304]{1,0:T(4,128)(2,1)S(1)}, bf16[3,2304]{1,0:T(4,128)(2,1)S(1)}, u32[]{:S(2)}, u32[]{:S(2)}) collective-permute-start(bf16[3,2304]{1,0:T(4,128)(2,1)S(1)} %slice.12), channel_id=1, source_target_pairs={{0,1},{1,2},{2,3},{3,4},{4,5},{5,6},{6,7},{7,8},{8,9},{9,10},{10,1... | collective-permute-start | bytes 41480 | tf_op jit(solution)/shard_map/ppermute | solution.py:546
  13.2 3.7 %collective-permute-start.1 = (bf16[2096,128]{1,0:T(8,128)(2,1)S(1)}, bf16[2096,128]{1,0:T(8,128)(2,1)S(1)}, u32[]{:S(2)}, u32[]{:S(2)}) collective-permute-start(bf16[2096,128]{1,0:T(8,128)(2,1)S(1)} %get-tuple-element.26), channel_id=1, source_target_pairs={{0,1},{1,0},{2,3},{3,2},{4,5},{5,4},{6,7},{7,6},{8,9},{9,8},{10,11... | collective-permute-start | bytes 1609736 | tf_op jit(solution)/shard_map/ppermute | solution.py:533
  17.0 5.0 %collective-permute-start.2 = (bf16[560,128]{1,0:T(8,128)(2,1)S(1)}, bf16[560,128]{1,0:T(8,128)(2,1)S(1)}, u32[]{:S(2)}, u32[]{:S(2)}) collective-permute-start(bf16[560,128]{1,0:T(8,128)(2,1)S(1)} %get-tuple-element.29), channel_id=1, source_target_pairs={{0,2},{1,3},{2,0},{3,1},{4,6},{5,7},{6,4},{7,5},{8,10},{9,11},{10,... | collective-permute-start | bytes 430088 | tf_op jit(solution)/shard_map/ppermute | solution.py:533
  22.1 4.0 %collective-permute-start.3 = (bf16[560,128]{1,0:T(8,128)(2,1)S(1)}, bf16[560,128]{1,0:T(8,128)(2,1)S(1)}, u32[]{:S(2)}, u32[]{:S(2)}) collective-permute-start(bf16[560,128]{1,0:T(8,128)(2,1)S(1)} %get-tuple-element.33), channel_id=1, source_target_pairs={{0,4},{1,5},{2,6},{3,7},{4,0},{5,1},{6,2},{7,3},{8,12},{9,13},{10,... | collective-permute-start | bytes 430088 | tf_op jit(solution)/shard_map/ppermute | solution.py:533
  26.2 8.7 %collective-permute-start.4 = (bf16[1024,128]{1,0:T(8,128)(2,1)S(1)}, bf16[1024,128]{1,0:T(8,128)(2,1)S(1)}, u32[]{:S(2)}, u32[]{:S(2)}) collective-permute-start(bf16[1024,128]{1,0:T(8,128)(2,1)S(1)} %get-tuple-element.38), channel_id=1, source_target_pairs={{0,2},{1,3},{2,0},{3,1},{4,6},{5,7},{6,4},{7,5},{8,10},{9,11},{10,... | collective-permute-start | bytes 786440 | tf_op jit(solution)/shard_map/ppermute | solution.py:533
  26.6 8.3 %collective-permute-start.5 = (bf16[560,128]{1,0:T(8,128)(2,1)S(1)}, bf16[560,128]{1,0:T(8,128)(2,1)S(1)}, u32[]{:S(2)}, u32[]{:S(2)}) collective-permute-start(bf16[560,128]{1,0:T(8,128)(2,1)S(1)} %get-tuple-element.39), channel_id=1, source_target_pairs={{0,8},{1,9},{2,10},{3,11},{4,12},{5,13},{6,14},{7,15},{16,24},{17,... | collective-permute-start | bytes 430088 | tf_op jit(solution)/shard_map/ppermute | solution.py:533
  35.0 15.3 %copy-start.1 = (f32[2048]{0:T(1024)S(1)}, f32[2048]{0:T(1024)}, u32[]{:S(2)}) copy-start(f32[2048]{0:T(1024)} %param.9) | copy-start | bytes 24580
  35.0 13.8 %collective-permute-start.6 = (bf16[2560,128]{1,0:T(8,128)(2,1)S(1)}, bf16[2560,128]{1,0:T(8,128)(2,1)S(1)}, u32[]{:S(2)}, u32[]{:S(2)}) collective-permute-start(bf16[2560,128]{1,0:T(8,128)(2,1)S(1)} %pad_maximum_fusion), channel_id=1, source_target_pairs={{0,1},{1,0},{2,3},{3,2},{4,5},{5,4},{6,7},{7,6},{8,9},{9,8},{10,11... | collective-permute-start | bytes 1966088 | tf_op jit(solution)/shard_map/ppermute | solution.py:533
  38.8 7.3 %collective-permute-start.7 = (bf16[560,128]{1,0:T(8,128)(2,1)S(1)}, bf16[560,128]{1,0:T(8,128)(2,1)S(1)}, u32[]{:S(2)}, u32[]{:S(2)}) collective-permute-start(bf16[560,128]{1,0:T(8,128)(2,1)S(1)} %collective-permute-done.5.node_a), channel_id=1, source_target_pairs={{8,10},{9,11},{10,8},{11,9},{12,14},{13,15},{14,12},{15,13},{24,26... | collective-permute-start | bytes 430088 | tf_op jit(solution)/shard_map/ppermute | solution.py:533
  46.1 6.1 %collective-permute-start.8 = (bf16[560,128]{1,0:T(8,128)(2,1)S(1)}, bf16[560,128]{1,0:T(8,128)(2,1)S(1)}, u32[]{:S(2)}, u32[]{:S(2)}) collective-permute-start(bf16[560,128]{1,0:T(8,128)(2,1)S(1)} %collective-permute-done.7.node_a), channel_id=1, source_target_pairs={{8,9},{9,8},{10,11},{11,10},{12,13},{13,12},{14,15},{15,14},{24,25... | collective-permute-start | bytes 430088 | tf_op jit(solution)/shard_map/ppermute | solution.py:533

commit v2 on v1

--- a/solution.py
+++ b/solution.py
@@ -11,7 +11,7 @@
 BF16 = jnp.bfloat16
 LANES = 128
 GROUP = 8
-PARTS = 3
+PARTS = 4
 VMEM_LIMIT = 24 << 20
 HBM_SPEC = pl.BlockSpec(memory_space=pltpu.HBM)
 VMEM_SPEC = pl.BlockSpec(memory_space=pltpu.VMEM)
@@ -29,25 +29,31 @@
     return pltpu.CompilerParams(vmem_limit_bytes=VMEM_LIMIT)
 
 
+def small_cost():
+    return pl.CostEstimate(flops=1024, bytes_accessed=1024, transcendentals=0)
+
+
 def product(left, right):
     return jnp.dot(left, right, preferred_element_type=F32)
 
 
 def write_spans(message_ref, first_row, spans):
     head_count = spans.shape[0]
-    for part in range(PARTS):
-        rounded = spans.astype(BF16)
-        start = first_row + part * head_count
-        message_ref[start : start + head_count, :] = rounded
-        spans = spans - rounded.astype(F32)
+    place = lax.broadcasted_iota(jnp.int32, spans.shape, 1) // (LANES // PARTS)
+    packed = jnp.zeros(spans.shape, F32)
+    for part in range(PARTS - 1):
+        rounded = spans.astype(BF16).astype(F32)
+        packed = jnp.where(place == part, rounded, packed)
+        spans = spans - rounded
+    message_ref[first_row : first_row + head_count, :] = packed.astype(BF16)
 
 
 def read_spans(message_ref, first_row, head_count):
-    total = None
-    for part in range(PARTS):
-        start = first_row + part * head_count
-        piece = message_ref[start : start + head_count, :].astype(F32)
-        total = piece if total is None else total + piece
+    total = message_ref[first_row : first_row + head_count, :].astype(F32)
+    width = LANES // PARTS
+    while width < LANES:
+        total = total + pltpu.roll(total, width, 1)
+        width *= 2
     return total
 
 
@@ -60,18 +66,30 @@
     return logs
 
 
+def activated(values, edge, weights, padded):
+    rows = values.shape[0]
+    taps = weights.shape[0]
+    padded[GROUP : GROUP + rows, :] = values
+    if edge is not None:
+        padded[GROUP - taps + 1 : GROUP, :] = edge
+    total = None
+    for tap in range(taps):
+        first = GROUP - taps + 1 + tap
+        shifted = values if tap == taps - 1 else padded[first : first + rows, :]
+        term = shifted * weights[tap : tap + 1]
+        total = term if total is None else total + term
+    return (total * jax.nn.sigmoid(total)).astype(BF16)
+
+
 def front_kernel(
-    xbc_hbm, edge_ref, taps_hbm, decay_hbm, acts_ref, maps_ref, state_ref, message_ref, log_ref,
-    xbc_buf, taps_buf, decay_buf, padded, sems, small_sems, chunk
+    xbc_hbm, taps_hbm, decay_hbm, acts_ref, maps_ref, state_ref, log_ref, taps_ref, top_ref,
+    head_ref, xbc_buf, decay_buf, padded, sems, small_sems, chunk
 ):
     rows, width = xbc_buf.shape
-    taps = taps_buf.shape[0]
-    head_count = decay_buf.shape[0]
-    state_size = maps_ref.shape[1]
     steps = width // chunk
     small = [
         pltpu.make_async_copy(decay_hbm, decay_buf, small_sems.at[0]),
-        pltpu.make_async_copy(taps_hbm, taps_buf, small_sems.at[1]),
+        pltpu.make_async_copy(taps_hbm, taps_ref, small_sems.at[1]),
     ]
     copies = []
     for step in range(steps):
@@ -81,77 +99,123 @@
         )
     for copy in small + copies[-1:] + copies[:-1]:
         copy.start()
-
-    def activated(start):
-        part = pl.ds(start, chunk)
-        weights = taps_buf[:, part]
+    small[0].wait()
+    log_ref[...] = running_sum(decay_buf[...])
+    small[1].wait()
+
+    def some_columns(start, slot):
+        part = slice(start, start + LANES)
+        top_ref[:, part] = xbc_buf[: top_ref.shape[0], part]
         values = xbc_buf[:, part].astype(F32)
-        padded[GROUP : GROUP + rows, :] = values
-        padded[GROUP - taps + 1 : GROUP, :] = edge_ref[:, part].astype(F32)
-        total = None
-        for tap in range(taps):
-            first = GROUP - taps + 1 + tap
-            shifted = values if tap == taps - 1 else padded[first : first + rows, :]
-            term = shifted * weights[tap : tap + 1]
-            total = term if total is None else total + term
-        return (total / (1.0 + jnp.exp(-total))).astype(BF16)
-
-    small[0].wait()
-    local_log = running_sum(decay_buf[...])
-    log_ref[...] = local_log
-    totals = jnp.broadcast_to(local_log[:, rows - 1 : rows], (head_count, LANES))
-    write_spans(message_ref, state_ref.shape[0], totals)
-    small[1].wait()
+        result = activated(values, None, taps_ref[:, part], padded.at[slot])
+        head_ref[:, part] = result[:LANES]
+        turned = result[LANES:].T
+        acts_ref[part, LANES:] = turned
+        return result, turned
+
     copies[-1].wait()
-    last = activated(width - chunk)
-    maps_ref[...] = last[:, :state_size]
-    acts_ref[width - chunk :, :] = last.T
-    per_chunk = chunk // state_size
-
+    some_columns(width - LANES, 0)
+    result, _ = some_columns(width - 2 * LANES, 1)
+    maps_ref[...] = result
     for step in range(steps - 1):
         copies[step].wait()
-        turned = activated(step * chunk).T
-        acts_ref[step * chunk : (step + 1) * chunk, :] = turned
-        for part in range(per_chunk):
-            head = step * per_chunk + part
+        for slot in range(chunk // LANES):
+            head = step * (chunk // LANES) + slot
+            _, turned = some_columns(head * LANES, slot)
             logs = log_ref[head : head + 1, :]
-            tail = jnp.exp(logs[:, rows - 1 : rows] - logs)
-            own = turned[part * LANES : (part + 1) * LANES].astype(F32)
-            decayed = (own * tail).astype(BF16)
-            state = product(decayed, maps_ref[...])
-            state_ref[head * LANES : (head + 1) * LANES, :] = state
-            message_ref[head * LANES : (head + 1) * LANES, :] = state.astype(BF16)
-
-
-def front(xbc, edge, conv_weight, log_decay):
+            tail = jnp.exp(logs[:, rows - 1 : rows] - logs[:, LANES:])
+            decayed = (turned.astype(F32) * tail).astype(BF16)
+            state_ref[head * LANES : (head + 1) * LANES, :] = product(
+                decayed, maps_ref[LANES:, :]
+            )
+
+
+def front(xbc, conv_weight, log_decay):
     rows, width = xbc.shape
     taps = conv_weight.shape[0]
     head_count = log_decay.shape[0]
     inner = head_count * LANES
     state_size = (width - inner) // 2
-    chunk = 2 * state_size
+    chunk = 2 * LANES
     return pl.pallas_call(
         functools.partial(front_kernel, chunk=chunk),
-        in_specs=[HBM_SPEC, VMEM_SPEC, HBM_SPEC, HBM_SPEC],
-        out_specs=[VMEM_SPEC] * 5,
+        in_specs=[HBM_SPEC] * 3,
+        out_specs=[VMEM_SPEC] * 7,
         out_shape=[
             pltpu.VMEM((width, rows), BF16),
             pltpu.VMEM((rows, state_size), BF16),
             pltpu.VMEM((inner, state_size), F32),
-            pltpu.VMEM((inner + PARTS * head_count, state_size), BF16),
             pltpu.VMEM((head_count, rows), F32),
+            pltpu.VMEM((taps, width), F32),
+            pltpu.VMEM((2 * GROUP, width), BF16),
+            pltpu.VMEM((LANES, width), BF16),
         ],
         scratch_shapes=[
             pltpu.VMEM((rows, width), BF16),
-            pltpu.VMEM((taps, width), F32),
             pltpu.VMEM((head_count, rows), F32),
-            pltpu.VMEM((rows + GROUP, chunk), F32),
+            pltpu.VMEM((chunk // LANES, rows + GROUP, LANES), F32),
             pltpu.SemaphoreType.DMA((width // chunk,)),
             pltpu.SemaphoreType.DMA((2,)),
         ],
         compiler_params=params(),
         name="front",
-    )(*in_hbm(xbc), *in_vmem(edge), *in_hbm(conv_weight, log_decay))
+    )(*in_hbm(xbc, conv_weight, log_decay))
+
+
+def edge_kernel(edge_ref, log_ref, taps_ref, top_ref, head_ref, *refs):
+    acts_ref, maps_ref, state_ref, message_ref, padded = refs[-5:]
+    head_count, rows = log_ref.shape
+    width = head_ref.shape[1]
+    inner = head_count * LANES
+    few = top_ref.shape[0]
+    is_first = lax.axis_index("seq") == 0
+
+    def some_columns(start, slot):
+        part = slice(start, start + LANES)
+        edge = jnp.where(is_first, 0.0, edge_ref[:, part].astype(F32))
+        values = top_ref[:, part].astype(F32)
+        result = activated(values, edge, taps_ref[:, part], padded.at[slot])
+        block = jnp.concatenate([result, head_ref[few:, part]], axis=0)
+        turned = block.T
+        acts_ref[part, :LANES] = turned
+        return block, turned
+
+    some_columns(width - LANES, 0)
+    maps, _ = some_columns(width - 2 * LANES, 1)
+    maps_ref[:LANES, :] = maps
+    totals = jnp.broadcast_to(log_ref[:, rows - 1 : rows], (head_count, LANES))
+    write_spans(message_ref, inner, totals)
+    for head in range(head_count):
+        part = slice(head * LANES, (head + 1) * LANES)
+        _, turned = some_columns(head * LANES, head % padded.shape[0])
+        logs = log_ref[head : head + 1, :]
+        tail = jnp.exp(logs[:, rows - 1 : rows] - logs[:, :LANES])
+        decayed = (turned.astype(F32) * tail).astype(BF16)
+        state = state_ref[part, :] + product(decayed, maps)
+        state_ref[part, :] = state
+        message_ref[part, :] = state.astype(BF16)
+
+
+def edge_rows(edge, log, taps, top, head, acts, maps, state):
+    head_count, _ = log.shape
+    inner, state_size = state.shape
+    operands = [edge, log, taps, top, head, acts, maps, state]
+    return pl.pallas_call(
+        edge_kernel,
+        in_specs=[VMEM_SPEC] * len(operands),
+        out_specs=[VMEM_SPEC] * 4,
+        out_shape=[
+            pltpu.VMEM(acts.shape, BF16),
+            pltpu.VMEM(maps.shape, BF16),
+            pltpu.VMEM(state.shape, F32),
+            pltpu.VMEM((inner + head_count, state_size), BF16),
+        ],
+        input_output_aliases={5: 0, 6: 1, 7: 2},
+        scratch_shapes=[pltpu.VMEM((2, top.shape[0] + GROUP, LANES), F32)],
+        compiler_params=params(),
+        cost_estimate=small_cost(),
+        name="edge",
+    )(*in_vmem(*operands))
 
 
 def pair_kernel(state_ref, log_ref, got_ref, own_ref, stats_ref, send_ref, rest_ref, shards):
@@ -191,7 +255,6 @@
     head_count, _ = log.shape
     inner, state_size = state.shape
     part = inner // shards
-    spans = PARTS * head_count
     return pl.pallas_call(
         functools.partial(pair_kernel, shards=shards),
         in_specs=[VMEM_SPEC] * 3,
@@ -199,10 +262,11 @@
         out_shape=[
             pltpu.VMEM((part, state_size), F32),
             pltpu.VMEM((4, head_count, LANES), F32),
-            pltpu.VMEM((part + spans, state_size), BF16),
-            pltpu.VMEM((part + spans, state_size), BF16),
+            pltpu.VMEM((part + head_count, state_size), BF16),
+            pltpu.VMEM((part + head_count, state_size), BF16),
         ],
         compiler_params=params(),
+        cost_estimate=small_cost(),
         name="pair",
     )(*in_vmem(state, log, got))
 
@@ -224,7 +288,8 @@
     next_stats_ref[1] = stats_ref[1] + jnp.where(is_upper, theirs, 0.0)
     next_stats_ref[2] = jnp.exp(jnp.where(is_upper, mine, theirs))
     next_stats_ref[3] = jnp.zeros_like(mine)
-    write_spans(send_ref, part, mine + theirs)
+    if not gathered:
+        write_spans(send_ref, part, mine + theirs)
     for local in range(share):
         place = slice(local * LANES, (local + 1) * LANES)
         head = (index % shards) * share + local
@@ -242,7 +307,8 @@
 
 def join(own, stats, got, after, bit, shards, sources):
     operands = [own, stats, got, after, *sources]
-    out_shape = [pltpu.VMEM(stats.shape, F32), pltpu.VMEM(got.shape, BF16)]
+    message = own.shape if sources else got.shape
+    out_shape = [pltpu.VMEM(stats.shape, F32), pltpu.VMEM(message, BF16)]
     if sources:
         out_shape.append(pltpu.VMEM((len(sources) * own.shape[0], own.shape[1]), BF16))
     else:
@@ -253,6 +319,7 @@
         out_specs=[VMEM_SPEC] * 3,
         out_shape=out_shape,
         compiler_params=params(),
+        cost_estimate=small_cost(),
         name="join",
     )(*in_vmem(*operands))
 
@@ -419,7 +486,7 @@
     return gains_ref[pl.ds(row, 1), :] * jnp.exp(exponent)
 
 
-def middle_kernel(*refs, places, levels, shards):
+def middle_kernel(*refs, places, relatives, levels, shards):
     count = len(places)
     acts_ref, log_ref, gains_ref = refs[:3]
     stats = refs[3 : 3 + count]
@@ -432,7 +499,7 @@
     shard = lax.axis_index("seq") % shards
     base = gains_ref.shape[0] // head_count - levels
     queries = acts_ref[inner + state_size :, :]
-    for relative in range(shards):
+    for relative in relatives:
         terms = []
         for slot in range(count):
             source, start = places[slot][relative]
@@ -447,22 +514,27 @@
             total_ref[at, :] = total
 
 
-def middle(near_term, acts, log, gains, stats, sources, places, levels, shards):
+def middle(
+    near_term, acts, log, gains, stats, sources, places, relatives, levels, shards
+):
     operands = [acts, log, gains, *stats, *sources, near_term]
     return pl.pallas_call(
-        functools.partial(middle_kernel, places=places, levels=levels, shards=shards),
+        functools.partial(
+            middle_kernel, places=places, relatives=relatives, levels=levels, shards=shards
+        ),
         in_specs=[VMEM_SPEC] * len(operands),
         out_specs=VMEM_SPEC,
         out_shape=pltpu.VMEM(near_term.shape, F32),
         input_output_aliases={len(operands) - 1: 0},
         compiler_params=params(),
+        cost_estimate=small_cost(),
         name="middle",
     )(*in_vmem(*operands))
 
 
 def last_kernel(
-    total_ref, acts_ref, log_ref, gains_ref, gain_ref, stats_ref, node_a, node_b, *rest,
-    starts, level, relatives, shards, base
+    total_ref, acts_ref, log_ref, gains_ref, gain_ref, stats_ref, node_ref, *rest,
+    level, relatives, shards, base
 ):
     out_hbm, turned, out_buf, out_sems = rest[-4:]
     head_count, rows = log_ref.shape
@@ -476,8 +548,8 @@
     gain_columns = turned[...].T
     queries = acts_ref[inner + state_size :, :]
     copies = []
-    for relative, node_ref, start in zip(relatives, (node_a, node_b), starts):
-        term = far_product(node_ref, start, part, queries)
+    for place, relative in enumerate(relatives):
+        term = far_product(node_ref, place * part, part, queries)
         for local in range(share):
             head = (relative ^ shard) * share + local
             at = pl.ds(pl.multiple_of(head * LANES, LANES), LANES)
@@ -498,11 +570,11 @@
 
 
 def last(
-    total, acts, log, gains, gain, stats, nodes, starts, level, levels, relatives, shards, mixed
+    total, acts, log, gains, gain, stats, node, level, levels, relatives, shards, mixed
 ):
     head_count, rows = log.shape
     count = head_count // shards * len(relatives)
-    operands = in_vmem(total, acts, log, gains, gain.reshape(head_count, LANES), stats, *nodes)
+    operands = in_vmem(total, acts, log, gains, gain.reshape(head_count, LANES), stats, node)
     specs = [VMEM_SPEC] * len(operands)
     aliases = {}
     if mixed is not None:
@@ -511,7 +583,7 @@
         specs.append(HBM_SPEC)
     return pl.pallas_call(
         functools.partial(
-            last_kernel, starts=starts, level=level, relatives=relatives, shards=shards,
+            last_kernel, level=level, relatives=relatives, shards=shards,
             base=gains.shape[0] // head_count - levels,
         ),
         in_specs=specs,
@@ -524,13 +596,13 @@
             pltpu.SemaphoreType.DMA((count,)),
         ],
         compiler_params=params(),
+        cost_estimate=small_cost(),
         name="last",
     )(*operands)
 
 
-def moved(value, apart, chosen=lambda index: True):
-    devices = range(lax.axis_size("seq"))
-    return lax.ppermute(value, "seq", [(i, i ^ apart) for i in devices if chosen(i)])
+def moved(value, apart):
+    return lax.ppermute(value, "seq", [(i, i ^ apart) for i in range(lax.axis_size("seq"))])
 
 
 def on_device(xbc, conv_weight, log_decay, level_weights, gain):
@@ -542,9 +614,10 @@
     shards = 4
     part = head_count * LANES // shards
     gains = level_weights.transpose(1, 0, 2).reshape(-1, rows)
-    behind = [(i, i + 1) for i in range(devices - 1)]
+    behind = [(i, (i + 1) % devices) for i in range(devices)]
     edge = lax.ppermute(xbc[rows - taps + 1 :], "seq", behind)
-    acts, maps, state, message, log = front(xbc, edge, conv_weight, log_decay)
+    acts, maps, state, log, *kept = front(xbc, conv_weight, log_decay)
+    acts, maps, state, message = edge_rows(edge, log, *kept, acts, maps, state)
     first_node = moved(message, 1)
     own, stats, send, rest = pair(state, log, first_node, shards)
     near_made = None
@@ -561,32 +634,23 @@
         all_stats.append(stats)
     top = levels - 1
 
-    def is_upper(index):
-        return index >> top & 1 == 1
-
     across = moved(own, 2)
-    node = moved(send, 1 << top, lambda index: index >> top & 1 == 0)
-    node_across = moved(node, 2, is_upper)
-    beside = moved(jnp.concatenate([*[kept[:part] for kept in got], across, node[:part]]), 1)
+    node = moved(send, 1 << top)
+    beside = moved(jnp.concatenate([*[kept[:part] for kept in got], across]), 1)
     count = len(got)
-    places = [
-        [(slot, 0), (count + 1, slot * part), (count, slot * part),
-         (count + 1, (count + slot) * part)]
-        for slot in range(count)
-    ]
-    total = middle(
-        near_made[0], acts, log, gains, all_stats[:count], [*got, across, beside], places, levels,
-        shards,
-    )
-
+    shared = (acts, log, gains, all_stats[:count])
+    direct = [{0: (slot, 0), 2: (count, slot * part)} for slot in range(count)]
+    relayed = [{1: (0, slot * part), 3: (0, (count + slot) * part)} for slot in range(count)]
+    total = middle(near_made[0], *shared, [*got, across], direct, (0, 2), levels, shards)
+    node, total = lax.optimization_barrier((node, total))
     common = (acts, log, gains, gain, all_stats[-1])
-    mixed = last(
-        total, *common, (node, beside), (0, 2 * count * part), top, levels, (0, 1), shards, None
-    )
-    node_corner = moved(node_across, 1, is_upper)
-    return last(
-        total, *common, (node_across, node_corner), (0, 0), top, levels, (2, 3), shards, mixed
-    )
+    node_across = moved(node, 2)
+    mixed = last(total, *common, node, top, levels, (0,), shards, None)
+    node_across, mixed, total = lax.optimization_barrier((node_across, mixed, total))
+    node_beside = moved(jnp.concatenate([node, node_across]), 1)
+    total = middle(total, *shared, [beside], relayed, (1, 3), levels, shards)
+    mixed = last(total, *common, node_across, top, levels, (2,), shards, mixed)
+    return last(total, *common, node_beside, top, levels, (1, 3), shards, mixed)
 
 
 def solution(mesh):

time: 54.3 us -> 41.8 us (0.77)
  the two profiles are of different devices: /device:TPU:25 before, /device:TPU:0 now
where the time goes in v2:
time: 41.8 us; the launch traced here: 41.6 us
  Pallas kernels  18.7 us (45%)
  waiting for transfers between devices  11.3 us (27%)
  starting transfers between devices  10.6 us (25%)
  local copies, waits for them, and re-layouts  0.81 us (2%)
    ppermute x8, waiting for transfers between devices, moved(): lax.ppermute(value, 'seq', [(i, i ^ apart) for i in range(lax.axis_size('...  10.5 us
    ppermute x8, starting transfers between devices, moved(): lax.ppermute(value, 'seq', [(i, i ^ apart) for i in range(lax.axis_size('...  10.1 us
    pallas_call x2, Pallas kernels, near(): pl.pallas_call(functools.partial(near_kernel, first=first, wide=wide, hea...  5.97 us
    pallas_call x1, Pallas kernels, front(): pl.pallas_call(functools.partial(front_kernel, chunk=chunk), in_specs=[HB...  5.65 us
    pallas_call x3, Pallas kernels, last(): pl.pallas_call(functools.partial(last_kernel, level=level, relatives=rela...  4.46 us
    pallas_call x2, Pallas kernels, middle(): pl.pallas_call(functools.partial(middle_kernel, places=places, relatives=...  1.57 us
  transfers between devices with their start and end apart: 9, of which 7 were waited for; matrix products, arithmetic and copies ran while one was open for 0% of the time, Pallas kernels for 38%

profile of v2, /device:TPU:0, one launch (start us, length us, event | category | flops | bytes accessed | tf_op | source)
XLA Modules:
  0.0 41.6 jit_solution(12243724881981736829)
XLA Ops:
  0.0 0.8 %slice.9 = bf16[3,2304]{1,0:T(4,128)(2,1)S(1)} slice(bf16[512,2304]{1,0:T(8,128)(2,1)} %xbc_hbm.1), slice={[509:512], [0:2304]} | slice | bytes 27648 | tf_op jit(solution)/shard_map/slice | solution.py:618
  0.8 0.5 %collective-permute-start = (bf16[3,2304]{1,0:T(4,128)(2,1)S(1)}, bf16[3,2304]{1,0:T(4,128)(2,1)S(1)}, u32[]{:S(2)}, u32[]{:S(2)}) collective-permute-start(bf16[3,2304]{1,0:T(4,128)(2,1)S(1)} %slice.9), channel_id=1, source_target_pairs={{0,1},{1,2},{2,3},{3,4},{4,5},{5,6},{6,7},{7,8},{8,9},{9,10},{10,1... | collective-permute-start | bytes 41480 | tf_op jit(solution)/shard_map/ppermute | solution.py:618
  1.3 5.6 %front.1 = (bf16[2304,512]{1,0:T(8,128)(2,1)S(1)}, bf16[512,128]{1,0:T(8,128)(2,1)S(1)}, f32[2048,128]{1,0:T(8,128)S(1)}, f32[16,512]{1,0:T(8,128)S(1)}, f32[4,2...) custom-call(bf16[512,2304]{1,0:T(8,128)(2,1)} %xbc_hbm.1, f32[4,2304]{1,0:T(4,128)} %taps_hbm.1, ...), custom_call_target="tpu_custom_call" | custom-call | tf_op jit(solution)/shard_map/front/pallas_call | solution.py:140
  6.9 0.8 %collective-permute-done.edge_ref = bf16[3,2304]{1,0:T(4,128)(2,1)S(1)} collective-permute-done((bf16[3,2304]{1,0:T(4,128)(2,1)S(1)}, bf16[3,2304]{1,0:T(4,128)(2,1)S(1)}, u32[]{:S(2)}, u32[]{:S(2)}) %collective-permute-start) | collective-permute-done | bytes 13856 | tf_op jit(solution)/shard_map/ppermute | solution.py:618
  7.7 0.0 copy-start
  7.7 0.5 %edge.1 = (bf16[2304,512]{1,0:T(8,128)(2,1)S(1)}, bf16[512,128]{1,0:T(8,128)(2,1)S(1)}, f32[2048,128]{1,0:T(8,128)S(1)}, bf16[2064,128]{1,0:T(8,128)(2,1)S(1)}) custom-call(bf16[3,2304]{1,0:T(4,128)(2,1)S(1)} %collective-permute-done.edge_ref, ...), custom_call_target="tpu_custom_call", output_to_operand_aliasing={{0}: (5, {}), {1}: (6, {}), {2}: (7, {})} | custom-call | flops 1024 | bytes 1024 | tf_op jit(solution)/shard_map/edge/pallas_call | solution.py:203
  8.2 1.9 %collective-permute-start.1 = (bf16[2064,128]{1,0:T(8,128)(2,1)S(1)}, bf16[2064,128]{1,0:T(8,128)(2,1)S(1)}, u32[]{:S(2)}, u32[]{:S(2)}) collective-permute-start(bf16[2064,128]{1,0:T(8,128)(2,1)S(1)} %get-tuple-element.43), channel_id=1, source_target_pairs={{0,1},{1,0},{2,3},{3,2},{4,5},{5,4},{6,7},{7,6},{8,9},{9,8},{10,11... | collective-permute-start | bytes 1585160 | tf_op jit(solution)/shard_map/ppermute | solution.py:605
  10.1 1.5 %collective-permute-done.1.got_ref.refs_4_ = bf16[2064,128]{1,0:T(8,128)(2,1)S(1)} collective-permute-done((bf16[2064,128]{1,0:T(8,128)(2,1)S(1)}, bf16[2064,128]{1,0:T(8,128)(2,1)S(1)}, u32[]{:S(2)}, u32[]{:S(2)}) %collective-permute-start.1) | collective-permute-done | bytes 528416 | tf_op jit(solution)/shard_map/ppermute | solution.py:605
  11.7 0.2 pair.1
  11.9 1.6 %collective-permute-start.2 = (bf16[528,128]{1,0:T(8,128)(2,1)S(1)}, bf16[528,128]{1,0:T(8,128)(2,1)S(1)}, u32[]{:S(2)}, u32[]{:S(2)}) collective-permute-start(bf16[528,128]{1,0:T(8,128)(2,1)S(1)} %get-tuple-element.46), channel_id=1, source_target_pairs={{0,2},{1,3},{2,0},{3,1},{4,6},{5,7},{6,4},{7,5},{8,10},{9,11},{10,... | collective-permute-start | bytes 405512 | tf_op jit(solution)/shard_map/ppermute | solution.py:605
  13.5 0.0 copy-done
  13.5 3.1 %near.2 = (f32[2048,512]{1,0:T(8,128)S(1)}, f32[512,512]{1,0:T(8,128)S(1)}, f32[3,512,128]{2,1,0:T(8,128)S(1)}) custom-call(bf16[2304,512]{1,0:T(8,128)(2,1)S(1)} %get-tuple-element.41.refs_0_.acts_ref, bf16[512,128]{1,0:T(8,128)(2,1)S(1)} %get-tuple-element.47.refs_1_, f32[16,512]{1,0:T(8,128)S(1)} %get-tuple-element.34.log_ref.refs_2_.refs_1_, ...), custom_call_target="tpu_custom_call" | custom-call | flops 1073741824 | bytes 10485760 | tf_op jit(solution)/shard_map/near/pallas_call | solution.py:458
  16.6 1.2 %collective-permute-done.2.got_ref.refs_5_ = bf16[528,128]{1,0:T(8,128)(2,1)S(1)} collective-permute-done((bf16[528,128]{1,0:T(8,128)(2,1)S(1)}, bf16[528,128]{1,0:T(8,128)(2,1)S(1)}, u32[]{:S(2)}, u32[]{:S(2)}) %collective-permute-start.2) | collective-permute-done | bytes 135200 | tf_op jit(solution)/shard_map/ppermute | solution.py:605
  17.8 0.2 join.2
  18.0 1.6 %collective-permute-start.3 = (bf16[528,128]{1,0:T(8,128)(2,1)S(1)}, bf16[528,128]{1,0:T(8,128)(2,1)S(1)}, u32[]{:S(2)}, u32[]{:S(2)}) collective-permute-start(bf16[528,128]{1,0:T(8,128)(2,1)S(1)} %get-tuple-element.50), channel_id=1, source_target_pairs={{0,4},{1,5},{2,6},{3,7},{4,0},{5,1},{6,2},{7,3},{8,12},{9,13},{10,... | collective-permute-start | bytes 405512 | tf_op jit(solution)/shard_map/ppermute | solution.py:605
  19.6 2.9 %near.3._.refs_8_ = f32[2048,512]{1,0:T(8,128)S(1)} custom-call(bf16[2304,512]{1,0:T(8,128)(2,1)S(1)} %get-tuple-element.41.refs_0_.acts_ref, bf16[512,128]{1,0:T(8,128)(2,1)S(1)} %get-tuple-element.47.refs_1_, f32[16,512]{1,0:T(8,128)S(1)} %get-tuple-element.34.log_ref.refs_2_.refs_1_, f32[224,512]{1,0:T(8,128)S(1)} %bitcast.5, ...), custom_call_target="tpu_custom_call", output_to_operand_aliasing={{}: (8, {})} | custom-call | flops 1073741824 | bytes 10485760 | tf_op jit(solution)/shard_map/near/pallas_call | solution.py:458
  22.5 0.6 %collective-permute-done.3.got_ref.refs_1_.refs_6_ = bf16[528,128]{1,0:T(8,128)(2,1)S(1)} collective-permute-done((bf16[528,128]{1,0:T(8,128)(2,1)S(1)}, bf16[528,128]{1,0:T(8,128)(2,1)S(1)}, u32[]{:S(2)}, u32[]{:S(2)}) %collective-permute-start.3) | collective-permute-done | bytes 135200 | tf_op jit(solution)/shard_map/ppermute | solution.py:605
  23.1 0.2 join.3
  23.3 1.6 %collective-permute-start.4 = (bf16[1024,128]{1,0:T(8,128)(2,1)S(1)}, bf16[1024,128]{1,0:T(8,128)(2,1)S(1)}, u32[]{:S(2)}, u32[]{:S(2)}) collective-permute-start(bf16[1024,128]{1,0:T(8,128)(2,1)S(1)} %get-tuple-element.55), channel_id=1, source_target_pairs={{0,2},{1,3},{2,0},{3,1},{4,6},{5,7},{6,4},{7,5},{8,10},{9,11},{10,... | collective-permute-start | bytes 786440 | tf_op jit(solution)/shard_map/ppermute | solution.py:605
  24.9 2.7 %collective-permute-start.6 = (bf16[512,128]{1,0:T(8,128)(2,1)S(1)}, bf16[512,128]{1,0:T(8,128)(2,1)S(1)}, u32[]{:S(2)}, u32[]{:S(2)}) collective-permute-start(bf16[512,128]{1,0:T(8,128)(2,1)S(1)} %get-tuple-element.56), channel_id=1, source_target_pairs={{0,8},{1,9},{2,10},{3,11},{4,12},{5,13},{6,14},{7,15},{8,0},{9,1},... | collective-permute-start | bytes 393224 | tf_op jit(solution)/shard_map/ppermute | solution.py:605
  27.6 2.7 %collective-permute-done.4.refs_7_ = bf16[1024,128]{1,0:T(8,128)(2,1)S(1)} collective-permute-done((bf16[1024,128]{1,0:T(8,128)(2,1)S(1)}, bf16[1024,128]{1,0:T(8,128)(2,1)S(1)}, u32[]{:S(2)}, u32[]{:S(2)}) %collective-permute-start.4) | collective-permute-done | bytes 262176 | tf_op jit(solution)/shard_map/ppermute | solution.py:605
  30.3 0.0 copy-start.1
  30.3 0.1 collective-permute-start.5
  30.4 0.8 %middle.2.total_ref.refs_6_ = f32[2048,512]{1,0:T(8,128)S(1)} custom-call(bf16[2304,512]{1,0:T(8,128)(2,1)S(1)} %get-tuple-element.41.refs_0_.acts_ref, f32[16,512]{1,0:T(8,128)S(1)} %get-tuple-element.34.log_ref.refs_2_.refs_1_, f32[224,512]{1,0:T(8,128)S(1)} %bitcast.6, ...), custom_call_target="tpu_custom_call", output_to_operand_aliasing={{}: (8, {})} | custom-call | flops 1024 | bytes 1024 | tf_op jit(solution)/shard_map/middle/pallas_call | solution.py:521
  31.2 1.3 %collective-permute-done.6.node_ref = bf16[512,128]{1,0:T(8,128)(2,1)S(1)} collective-permute-done((bf16[512,128]{1,0:T(8,128)(2,1)S(1)}, bf16[512,128]{1,0:T(8,128)(2,1)S(1)}, u32[]{:S(2)}, u32[]{:S(2)}) %collective-permute-start.6) | collective-permute-done | bytes 131104 | tf_op jit(solution)/shard_map/ppermute | solution.py:605
  32.5 0.5 %collective-permute-start.7 = (bf16[512,128]{1,0:T(8,128)(2,1)S(1)}, bf16[512,128]{1,0:T(8,128)(2,1)S(1)}, u32[]{:S(2)}, u32[]{:S(2)}) collective-permute-start(bf16[512,128]{1,0:T(8,128)(2,1)S(1)} %collective-permute-done.6.node_ref), channel_id=1, source_target_pairs={{0,2},{1,3},{2,0},{3,1},{4,6},{5,7},{6,4},{7,5},{8,10},{9,11},{10,... | collective-permute-start | bytes 393224 | tf_op jit(solution)/shard_map/ppermute | solution.py:605
  33.0 0.0 copy-done.1
  33.0 1.3 %last.3.rest_0_ = bf16[512,2048]{1,0:T(8,128)(2,1)} custom-call(f32[2048,512]{1,0:T(8,128)S(1)} %middle.2.total_ref.refs_6_, bf16[2304,512]{1,0:T(8,128)(2,1)S(1)} %get-tuple-element.41.refs_0_.acts_ref, f32[16,512]{1,0:T(8,128)S(1)} %get-tuple-element.34.log_ref.refs_2_.refs_1_, f32[224,512]{1,0:T(8,128)S(1)} %bitcast.7, f32[16,128]{1,0:T(8,128)S(1)} %bitcast.11, ...), custom_call_target="tpu_custom_call" | custom-call | flops 1024 | bytes 1024 | tf_op jit(solution)/shard_map/last/pallas_call | solution.py:584
  34.3 3.2 %collective-permute-done.7.node_ref = bf16[512,128]{1,0:T(8,128)(2,1)S(1)} collective-permute-done((bf16[512,128]{1,0:T(8,128)(2,1)S(1)}, bf16[512,128]{1,0:T(8,128)(2,1)S(1)}, u32[]{:S(2)}, u32[]{:S(2)}) %collective-permute-start.7) | collective-permute-done | bytes 131104 | tf_op jit(solution)/shard_map/ppermute | solution.py:605
  37.5 0.1 collective-permute-start.8
  37.6 0.0 collective-permute-done.5.refs_5_
  37.6 0.8 %middle.3.total_ref = f32[2048,512]{1,0:T(8,128)S(1)} custom-call(bf16[2304,512]{1,0:T(8,128)(2,1)S(1)} %get-tuple-element.41.refs_0_.acts_ref, f32[16,512]{1,0:T(8,128)S(1)} %get-tuple-element.34.log_ref.refs_2_.refs_1_, f32[224,512]{1,0:T(8,128)S(1)} %bitcast.8, ...), custom_call_target="tpu_custom_call", output_to_operand_aliasing={{}: (6, {})} | custom-call | flops 1024 | bytes 1024 | tf_op jit(solution)/shard_map/middle/pallas_call | solution.py:521
  38.4 1.3 %last.4.rest_0_ = bf16[512,2048]{1,0:T(8,128)(2,1)} custom-call(f32[2048,512]{1,0:T(8,128)S(1)} %middle.3.total_ref, bf16[2304,512]{1,0:T(8,128)(2,1)S(1)} %get-tuple-element.41.refs_0_.acts_ref, f32[16,512]{1,0:T(8,128)S(1)} %get-tuple-element.34.log_ref.refs_2_.refs_1_, f32[224,512]{1,0:T(8,128)S(1)} %bitcast.9, ...), custom_call_target="tpu_custom_call", output_to_operand_aliasing={{}: (7, {})} | custom-call | flops 1024 | bytes 1024 | tf_op jit(solution)/shard_map/last/pallas_call | solution.py:584
  39.7 0.0 collective-permute-done.8.node_ref
  39.7 1.9 %last.5 = bf16[512,2048]{1,0:T(8,128)(2,1)} custom-call(f32[2048,512]{1,0:T(8,128)S(1)} %middle.3.total_ref, bf16[2304,512]{1,0:T(8,128)(2,1)S(1)} %get-tuple-element.41.refs_0_.acts_ref, f32[16,512]{1,0:T(8,128)S(1)} %get-tuple-element.34.log_ref.refs_2_.refs_1_, f32[224,512]{1,0:T(8,128)S(1)} %bitcast.10, ...), custom_call_target="tpu_custom_call", output_to_operand_aliasing={{}: (7, {})} | custom-call | flops 1024 | bytes 1024 | tf_op jit(solution)/shard_map/last/pallas_call | solution.py:584
  (4 shorter events, 0.1 us)
Async XLA Ops:
  0.8 6.9 %collective-permute-start = (bf16[3,2304]{1,0:T(4,128)(2,1)S(1)}, bf16[3,2304]{1,0:T(4,128)(2,1)S(1)}, u32[]{:S(2)}, u32[]{:S(2)}) collective-permute-start(bf16[3,2304]{1,0:T(4,128)(2,1)S(1)} %slice.9), channel_id=1, source_target_pairs={{0,1},{1,2},{2,3},{3,4},{4,5},{5,6},{6,7},{7,8},{8,9},{9,10},{10,1... | collective-permute-start | bytes 41480 | tf_op jit(solution)/shard_map/ppermute | solution.py:618
  7.7 5.8 %copy-start = (f32[16,14,512]{2,0,1:T(8,128)S(1)}, f32[16,14,512]{2,0,1:T(8,128)}, u32[]{:S(2)}) copy-start(f32[16,14,512]{2,0,1:T(8,128)} %param.8) | copy-start | bytes 1376260
  8.2 3.5 %collective-permute-start.1 = (bf16[2064,128]{1,0:T(8,128)(2,1)S(1)}, bf16[2064,128]{1,0:T(8,128)(2,1)S(1)}, u32[]{:S(2)}, u32[]{:S(2)}) collective-permute-start(bf16[2064,128]{1,0:T(8,128)(2,1)S(1)} %get-tuple-element.43), channel_id=1, source_target_pairs={{0,1},{1,0},{2,3},{3,2},{4,5},{5,4},{6,7},{7,6},{8,9},{9,8},{10,11... | collective-permute-start | bytes 1585160 | tf_op jit(solution)/shard_map/ppermute | solution.py:605
  11.9 5.9 %collective-permute-start.2 = (bf16[528,128]{1,0:T(8,128)(2,1)S(1)}, bf16[528,128]{1,0:T(8,128)(2,1)S(1)}, u32[]{:S(2)}, u32[]{:S(2)}) collective-permute-start(bf16[528,128]{1,0:T(8,128)(2,1)S(1)} %get-tuple-element.46), channel_id=1, source_target_pairs={{0,2},{1,3},{2,0},{3,1},{4,6},{5,7},{6,4},{7,5},{8,10},{9,11},{10,... | collective-permute-start | bytes 405512 | tf_op jit(solution)/shard_map/ppermute | solution.py:605
  18.0 5.1 %collective-permute-start.3 = (bf16[528,128]{1,0:T(8,128)(2,1)S(1)}, bf16[528,128]{1,0:T(8,128)(2,1)S(1)}, u32[]{:S(2)}, u32[]{:S(2)}) collective-permute-start(bf16[528,128]{1,0:T(8,128)(2,1)S(1)} %get-tuple-element.50), channel_id=1, source_target_pairs={{0,4},{1,5},{2,6},{3,7},{4,0},{5,1},{6,2},{7,3},{8,12},{9,13},{10,... | collective-permute-start | bytes 405512 | tf_op jit(solution)/shard_map/ppermute | solution.py:605
  23.3 7.0 %collective-permute-start.4 = (bf16[1024,128]{1,0:T(8,128)(2,1)S(1)}, bf16[1024,128]{1,0:T(8,128)(2,1)S(1)}, u32[]{:S(2)}, u32[]{:S(2)}) collective-permute-start(bf16[1024,128]{1,0:T(8,128)(2,1)S(1)} %get-tuple-element.55), channel_id=1, source_target_pairs={{0,2},{1,3},{2,0},{3,1},{4,6},{5,7},{6,4},{7,5},{8,10},{9,11},{10,... | collective-permute-start | bytes 786440 | tf_op jit(solution)/shard_map/ppermute | solution.py:605
  24.9 7.6 %collective-permute-start.6 = (bf16[512,128]{1,0:T(8,128)(2,1)S(1)}, bf16[512,128]{1,0:T(8,128)(2,1)S(1)}, u32[]{:S(2)}, u32[]{:S(2)}) collective-permute-start(bf16[512,128]{1,0:T(8,128)(2,1)S(1)} %get-tuple-element.56), channel_id=1, source_target_pairs={{0,8},{1,9},{2,10},{3,11},{4,12},{5,13},{6,14},{7,15},{8,0},{9,1},... | collective-permute-start | bytes 393224 | tf_op jit(solution)/shard_map/ppermute | solution.py:605
  30.3 2.7 %copy-start.1 = (f32[2048]{0:T(1024)S(1)}, f32[2048]{0:T(1024)}, u32[]{:S(2)}) copy-start(f32[2048]{0:T(1024)} %param.9) | copy-start | bytes 24580
  30.3 7.3 %collective-permute-start.5 = (bf16[2048,128]{1,0:T(8,128)(2,1)S(1)}, bf16[2048,128]{1,0:T(8,128)(2,1)S(1)}, u32[]{:S(2)}, u32[]{:S(2)}) collective-permute-start(bf16[2048,128]{1,0:T(8,128)(2,1)S(1)} %pad_maximum_fusion), channel_id=1, source_target_pairs={{0,1},{1,0},{2,3},{3,2},{4,5},{5,4},{6,7},{7,6},{8,9},{9,8},{10,11... | collective-permute-start | bytes 1572872 | tf_op jit(solution)/shard_map/ppermute | solution.py:605
  32.5 5.0 %collective-permute-start.7 = (bf16[512,128]{1,0:T(8,128)(2,1)S(1)}, bf16[512,128]{1,0:T(8,128)(2,1)S(1)}, u32[]{:S(2)}, u32[]{:S(2)}) collective-permute-start(bf16[512,128]{1,0:T(8,128)(2,1)S(1)} %collective-permute-done.6.node_ref), channel_id=1, source_target_pairs={{0,2},{1,3},{2,0},{3,1},{4,6},{5,7},{6,4},{7,5},{8,10},{9,11},{10,... | collective-permute-start | bytes 393224 | tf_op jit(solution)/shard_map/ppermute | solution.py:605
  37.5 2.2 %collective-permute-start.8 = (bf16[1024,128]{1,0:T(8,128)(2,1)S(1)}, bf16[1024,128]{1,0:T(8,128)(2,1)S(1)}, u32[]{:S(2)}, u32[]{:S(2)}) collective-permute-start(bf16[1024,128]{1,0:T(8,128)(2,1)S(1)} %pad_maximum_fusion.1), channel_id=1, source_target_pairs={{0,1},{1,0},{2,3},{3,2},{4,5},{5,4},{6,7},{7,6},{8,9},{9,8},{10,11... | collective-permute-start | bytes 786440 | tf_op jit(solution)/shard_map/ppermute | solution.py:605

commit v3 on v2

--- a/solution.py
+++ b/solution.py
@@ -81,113 +81,141 @@
     return (total * jax.nn.sigmoid(total)).astype(BF16)
 
 
-def front_kernel(
-    xbc_hbm, taps_hbm, decay_hbm, acts_ref, maps_ref, state_ref, log_ref, taps_ref, top_ref,
-    head_ref, xbc_buf, decay_buf, padded, sems, small_sems, chunk
+def some_columns(xbc_ref, taps_ref, acts_ref, head_ref, padded, start):
+    part = slice(start, start + LANES)
+    values = xbc_ref[:, part].astype(F32)
+    result = activated(values, None, taps_ref[:, part], padded)
+    head_ref[:, part] = result[:LANES]
+    turned = result[LANES:].T
+    acts_ref[part, LANES:] = turned
+    return result, turned
+
+
+def load_kernel(
+    xbc_hbm, taps_hbm, decay_hbm, xbc_ref, taps_ref, log_ref, edge_ref, acts_ref, head_ref,
+    maps_ref, decay_buf, padded, sems
 ):
-    rows, width = xbc_buf.shape
-    steps = width // chunk
-    small = [
-        pltpu.make_async_copy(decay_hbm, decay_buf, small_sems.at[0]),
-        pltpu.make_async_copy(taps_hbm, taps_ref, small_sems.at[1]),
+    rows, width = xbc_ref.shape
+    pieces = sems.shape[0] - 2
+    maps_width = 2 * maps_ref.shape[1]
+    size = (width - maps_width) // (pieces - 1)
+    starts = [width - maps_width] + [piece * size for piece in range(pieces - 1)]
+    copies = [
+        pltpu.make_async_copy(decay_hbm, decay_buf, sems.at[pieces]),
+        pltpu.make_async_copy(taps_hbm, taps_ref, sems.at[pieces + 1]),
     ]
-    copies = []
-    for step in range(steps):
-        part = pl.ds(step * chunk, chunk)
+    for piece, start in enumerate(starts):
+        part = pl.ds(start, size if piece else maps_width)
         copies.append(
-            pltpu.make_async_copy(xbc_hbm.at[:, part], xbc_buf.at[:, part], sems.at[step])
+            pltpu.make_async_copy(xbc_hbm.at[:, part], xbc_ref.at[:, part], sems.at[piece])
         )
-    for copy in small + copies[-1:] + copies[:-1]:
+    for copy in copies:
         copy.start()
-    small[0].wait()
+    copies[0].wait()
     log_ref[...] = running_sum(decay_buf[...])
-    small[1].wait()
-
-    def some_columns(start, slot):
-        part = slice(start, start + LANES)
-        top_ref[:, part] = xbc_buf[: top_ref.shape[0], part]
-        values = xbc_buf[:, part].astype(F32)
-        result = activated(values, None, taps_ref[:, part], padded.at[slot])
-        head_ref[:, part] = result[:LANES]
-        turned = result[LANES:].T
-        acts_ref[part, LANES:] = turned
-        return result, turned
-
-    copies[-1].wait()
-    some_columns(width - LANES, 0)
-    result, _ = some_columns(width - 2 * LANES, 1)
+    copies[1].wait()
+    copies[2].wait()
+    for slot, start in enumerate(range(width - LANES, width - maps_width - 1, -LANES)):
+        result, _ = some_columns(
+            xbc_ref, taps_ref, acts_ref, head_ref, padded.at[slot % 2], start
+        )
     maps_ref[...] = result
-    for step in range(steps - 1):
-        copies[step].wait()
-        for slot in range(chunk // LANES):
-            head = step * (chunk // LANES) + slot
-            _, turned = some_columns(head * LANES, slot)
-            logs = log_ref[head : head + 1, :]
-            tail = jnp.exp(logs[:, rows - 1 : rows] - logs[:, LANES:])
-            decayed = (turned.astype(F32) * tail).astype(BF16)
-            state_ref[head * LANES : (head + 1) * LANES, :] = product(
-                decayed, maps_ref[LANES:, :]
-            )
-
-
-def front(xbc, conv_weight, log_decay):
+    for copy in copies[3:]:
+        copy.wait()
+    few = edge_ref.shape[0]
+    tail = xbc_ref[rows - 2 * GROUP :, :].astype(F32)
+    edge_ref[...] = tail[2 * GROUP - few :].astype(BF16)
+
+
+def load(xbc, conv_weight, log_decay):
     rows, width = xbc.shape
-    taps = conv_weight.shape[0]
     head_count = log_decay.shape[0]
-    inner = head_count * LANES
-    state_size = (width - inner) // 2
-    chunk = 2 * LANES
+    state_size = (width - head_count * LANES) // 2
+    pieces = 5
     return pl.pallas_call(
-        functools.partial(front_kernel, chunk=chunk),
+        load_kernel,
         in_specs=[HBM_SPEC] * 3,
         out_specs=[VMEM_SPEC] * 7,
         out_shape=[
+            pltpu.VMEM(xbc.shape, BF16),
+            pltpu.VMEM(conv_weight.shape, F32),
+            pltpu.VMEM(log_decay.shape, F32),
+            pltpu.VMEM((conv_weight.shape[0] - 1, width), BF16),
             pltpu.VMEM((width, rows), BF16),
+            pltpu.VMEM((LANES, width), BF16),
             pltpu.VMEM((rows, state_size), BF16),
-            pltpu.VMEM((inner, state_size), F32),
-            pltpu.VMEM((head_count, rows), F32),
-            pltpu.VMEM((taps, width), F32),
-            pltpu.VMEM((2 * GROUP, width), BF16),
-            pltpu.VMEM((LANES, width), BF16),
         ],
         scratch_shapes=[
-            pltpu.VMEM((rows, width), BF16),
-            pltpu.VMEM((head_count, rows), F32),
-            pltpu.VMEM((chunk // LANES, rows + GROUP, LANES), F32),
-            pltpu.SemaphoreType.DMA((width // chunk,)),
-            pltpu.SemaphoreType.DMA((2,)),
+            pltpu.VMEM(log_decay.shape, F32),
+            pltpu.VMEM((2, rows + GROUP, LANES), F32),
+            pltpu.SemaphoreType.DMA((pieces + 2,)),
         ],
         compiler_params=params(),
+        cost_estimate=small_cost(),
+        name="load",
+    )(*in_hbm(xbc, conv_weight, log_decay))
+
+
+def front_kernel(
+    xbc_ref, taps_ref, log_ref, maps_ref, acts_in, head_in, acts_ref, head_ref, state_ref, padded
+):
+    rows, _ = xbc_ref.shape
+    for head in range(log_ref.shape[0]):
+        place = slice(head * LANES, (head + 1) * LANES)
+        _, turned = some_columns(
+            xbc_ref, taps_ref, acts_ref, head_ref, padded.at[head % 2], head * LANES
+        )
+        logs = log_ref[head : head + 1, :]
+        tail = jnp.exp(logs[:, rows - 1 : rows] - logs[:, LANES:])
+        decayed = (turned.astype(F32) * tail).astype(BF16)
+        state_ref[place, :] = product(decayed, maps_ref[LANES:, :])
+
+
+def front(xbc, taps, log, maps, acts, head):
+    rows, _ = xbc.shape
+    operands = [xbc, taps, log, maps, acts, head]
+    return pl.pallas_call(
+        front_kernel,
+        in_specs=[VMEM_SPEC] * len(operands),
+        out_specs=[VMEM_SPEC] * 3,
+        out_shape=[
+            pltpu.VMEM(acts.shape, BF16),
+            pltpu.VMEM(head.shape, BF16),
+            pltpu.VMEM((log.shape[0] * LANES, maps.shape[1]), F32),
+        ],
+        input_output_aliases={4: 0, 5: 1},
+        scratch_shapes=[pltpu.VMEM((2, rows + GROUP, LANES), F32)],
+        compiler_params=params(),
         name="front",
-    )(*in_hbm(xbc, conv_weight, log_decay))
-
-
-def edge_kernel(edge_ref, log_ref, taps_ref, top_ref, head_ref, *refs):
+    )(*in_vmem(*operands))
+
+
+def edge_kernel(edge_ref, log_ref, taps_ref, xbc_ref, head_ref, *refs):
     acts_ref, maps_ref, state_ref, message_ref, padded = refs[-5:]
     head_count, rows = log_ref.shape
     width = head_ref.shape[1]
     inner = head_count * LANES
-    few = top_ref.shape[0]
+    few = 2 * GROUP
     is_first = lax.axis_index("seq") == 0
 
-    def some_columns(start, slot):
+    def first_tile(start, slot):
         part = slice(start, start + LANES)
         edge = jnp.where(is_first, 0.0, edge_ref[:, part].astype(F32))
-        values = top_ref[:, part].astype(F32)
+        values = xbc_ref[:few, part].astype(F32)
         result = activated(values, edge, taps_ref[:, part], padded.at[slot])
         block = jnp.concatenate([result, head_ref[few:, part]], axis=0)
         turned = block.T
         acts_ref[part, :LANES] = turned
         return block, turned
 
-    some_columns(width - LANES, 0)
-    maps, _ = some_columns(width - 2 * LANES, 1)
+    first_tile(width - LANES, 0)
+    maps, _ = first_tile(width - 2 * LANES, 1)
     maps_ref[:LANES, :] = maps
     totals = jnp.broadcast_to(log_ref[:, rows - 1 : rows], (head_count, LANES))
     write_spans(message_ref, inner, totals)
     for head in range(head_count):
         part = slice(head * LANES, (head + 1) * LANES)
-        _, turned = some_columns(head * LANES, head % padded.shape[0])
+        _, turned = first_tile(head * LANES, head % padded.shape[0])
         logs = log_ref[head : head + 1, :]
         tail = jnp.exp(logs[:, rows - 1 : rows] - logs[:, :LANES])
         decayed = (turned.astype(F32) * tail).astype(BF16)
@@ -196,10 +224,10 @@
         message_ref[part, :] = state.astype(BF16)
 
 
-def edge_rows(edge, log, taps, top, head, acts, maps, state):
+def edge_rows(edge, log, taps, xbc, head, acts, maps, state):
     head_count, _ = log.shape
     inner, state_size = state.shape
-    operands = [edge, log, taps, top, head, acts, maps, state]
+    operands = [edge, log, taps, xbc, head, acts, maps, state]
     return pl.pallas_call(
         edge_kernel,
         in_specs=[VMEM_SPEC] * len(operands),
@@ -211,7 +239,7 @@
             pltpu.VMEM((inner + head_count, state_size), BF16),
         ],
         input_output_aliases={5: 0, 6: 1, 7: 2},
-        scratch_shapes=[pltpu.VMEM((2, top.shape[0] + GROUP, LANES), F32)],
+        scratch_shapes=[pltpu.VMEM((2, 3 * GROUP, LANES), F32)],
         compiler_params=params(),
         cost_estimate=small_cost(),
         name="edge",
@@ -333,8 +361,8 @@
 
 def near_kernel(*refs, first, wide, heads):
     if first:
-        acts_ref, maps_ref, log_ref, gains_ref, node_ref, _ = refs[:6]
-        near_ref, scores, tails, turned, weights = refs[6:]
+        acts_ref, maps_ref, log_ref, gains_ref, node_ref, _, gain_ref = refs[:7]
+        near_ref, scores, tails, columns_ref, turned, weights = refs[7:]
     else:
         acts_ref, maps_ref, log_ref, gains_ref, node_ref, _, scores, tails, _ = refs[:9]
         near_ref, turned, weights = refs[9:]
@@ -353,6 +381,8 @@
             upto = start + wide
             scores[:upto, start:upto] = product(maps_ref[:upto, :], queries[:, start:upto])
         turned[head_count:, :] = jnp.zeros((LANES - head_count, rows), F32)
+        turned[:head_count, :LANES] = gain_ref[...]
+        columns_ref[...] = turned[:, :LANES].T
         turned[:head_count, :] = log_ref[...]
         columns = [turned[:, tile * LANES : (tile + 1) * LANES].T for tile in range(tiles)]
         for tile in range(tiles):
@@ -440,7 +470,7 @@
     lax.fori_loop(heads[0] // weights.shape[0], heads[1] // weights.shape[0], some_heads, 0)
 
 
-def near(acts, maps, log, gains, node, after, earlier, heads):
+def near(acts, maps, log, gains, node, after, gain, earlier, heads):
     head_count, rows = log.shape
     wide = min(rows, 2 * LANES)
     tile_bits = (rows // LANES).bit_length() - 1
@@ -451,8 +481,10 @@
     if first:
         out_shape.append(pltpu.VMEM((rows, rows), F32))
         out_shape.append(pltpu.VMEM((1 + tile_bits, rows, LANES), F32))
+        out_shape.append(pltpu.VMEM((LANES, LANES), F32))
+        operands.append(gain.reshape(head_count, LANES))
     else:
-        near_term, scores, tails = earlier
+        near_term, scores, tails, _ = earlier
         operands += [scores, tails, near_term]
         aliases = {len(operands) - 1: 0}
     made = pl.pallas_call(
@@ -471,7 +503,7 @@
         ),
         name="near",
     )(*in_vmem(*operands))
-    return [made[0], *earlier[1:]] if not first else made
+    return made if first else [made[0], *earlier[1:]]
 
 
 def far_product(node_ref, first_row, count, queries):
@@ -533,21 +565,35 @@
 
 
 def last_kernel(
-    total_ref, acts_ref, log_ref, gains_ref, gain_ref, stats_ref, node_ref, *rest,
-    level, relatives, shards, base
+    total_ref, acts_ref, log_ref, gains_ref, columns_ref, stats_ref, node_ref, *refs,
+    level, relatives, done, shards, base
 ):
-    out_hbm, turned, out_buf, out_sems = rest[-4:]
     head_count, rows = log_ref.shape
     share = head_count // shards
     part = share * LANES
     inner = head_count * LANES
     state_size = acts_ref.shape[0] - inner >> 1
     shard = lax.axis_index("seq") % shards
-    turned[...] = jnp.zeros_like(turned)
-    turned[:head_count, :] = gain_ref[...]
-    gain_columns = turned[...].T
     queries = acts_ref[inner + state_size :, :]
     copies = []
+    if done:
+        out_hbm, mixed_ref, sems = refs[-3:]
+
+    def send(source_ref, slot, relative, local):
+        start = pl.multiple_of(((relative ^ shard) * share + local) * LANES, LANES)
+        copies.append(
+            pltpu.make_async_copy(
+                source_ref.at[slot], out_hbm.at[:, pl.ds(start, LANES)], sems.at[len(copies)]
+            )
+        )
+        copies[-1].start()
+
+    if done:
+        for relative, source_ref in zip(done, refs):
+            for local in range(share):
+                send(source_ref, local, relative, local)
+    else:
+        (mixed_ref,) = refs
     for place, relative in enumerate(relatives):
         term = far_product(node_ref, place * part, part, queries)
         for local in range(share):
@@ -558,47 +604,37 @@
             mean = jnp.mean(total * total, axis=0, keepdims=True)
             scale = lax.rsqrt(mean + 1e-05)
             chosen = jnp.full((LANES, LANES), head, jnp.int32)
-            column = jnp.take_along_axis(gain_columns, chosen, axis=1, mode="promise_in_bounds")
+            column = jnp.take_along_axis(
+                columns_ref[...], chosen, axis=1, mode="promise_in_bounds"
+            )
             column = jnp.concatenate([column] * (rows // LANES), axis=1)
-            slot = len(copies)
-            out_buf[slot] = (total * scale * column).astype(BF16).T
-            copy = pltpu.make_async_copy(out_buf.at[slot], out_hbm.at[:, at], out_sems.at[slot])
-            copy.start()
-            copies.append(copy)
+            slot = place * share + local
+            mixed_ref[slot] = (total * scale * column).astype(BF16).T
+            if done:
+                send(mixed_ref, slot, relative, local)
     for copy in copies:
         copy.wait()
 
 
-def last(
-    total, acts, log, gains, gain, stats, node, level, levels, relatives, shards, mixed
-):
+def last(total, acts, log, gains, columns, stats, node, level, levels, relatives, shards, done):
     head_count, rows = log.shape
-    count = head_count // shards * len(relatives)
-    operands = in_vmem(total, acts, log, gains, gain.reshape(head_count, LANES), stats, node)
-    specs = [VMEM_SPEC] * len(operands)
-    aliases = {}
-    if mixed is not None:
-        aliases = {len(operands): 0}
-        operands.append(mixed)
-        specs.append(HBM_SPEC)
+    share = head_count // shards
+    operands = [total, acts, log, gains, columns, stats, node, *done.values()]
+    mixed = pltpu.VMEM((share * len(relatives), rows, LANES), BF16)
+    whole = jax.ShapeDtypeStruct((rows, head_count * LANES), BF16)
     return pl.pallas_call(
         functools.partial(
-            last_kernel, level=level, relatives=relatives, shards=shards,
+            last_kernel, level=level, relatives=relatives, done=tuple(done), shards=shards,
             base=gains.shape[0] // head_count - levels,
         ),
-        in_specs=specs,
-        out_specs=HBM_SPEC,
-        out_shape=jax.ShapeDtypeStruct((rows, head_count * LANES), BF16),
-        input_output_aliases=aliases,
-        scratch_shapes=[
-            pltpu.VMEM((LANES, LANES), F32),
-            pltpu.VMEM((count, rows, LANES), BF16),
-            pltpu.SemaphoreType.DMA((count,)),
-        ],
+        in_specs=[VMEM_SPEC] * len(operands),
+        out_specs=HBM_SPEC if done else VMEM_SPEC,
+        out_shape=whole if done else mixed,
+        scratch_shapes=[mixed, pltpu.SemaphoreType.DMA((head_count,))] if done else [],
         compiler_params=params(),
         cost_estimate=small_cost(),
         name="last",
-    )(*operands)
+    )(*in_vmem(*operands))
 
 
 def moved(value, apart):
@@ -606,7 +642,6 @@
 
 
 def on_device(xbc, conv_weight, log_decay, level_weights, gain):
-    taps = conv_weight.shape[0]
     rows = xbc.shape[0]
     head_count = log_decay.shape[0]
     devices = lax.axis_size("seq")
@@ -615,9 +650,10 @@
     part = head_count * LANES // shards
     gains = level_weights.transpose(1, 0, 2).reshape(-1, rows)
     behind = [(i, (i + 1) % devices) for i in range(devices)]
-    edge = lax.ppermute(xbc[rows - taps + 1 :], "seq", behind)
-    acts, maps, state, log, *kept = front(xbc, conv_weight, log_decay)
-    acts, maps, state, message = edge_rows(edge, log, *kept, acts, maps, state)
+    values, taps, log, edge, acts, head, maps = load(xbc, conv_weight, log_decay)
+    edge = lax.ppermute(edge, "seq", behind)
+    acts, head, state = front(values, taps, log, maps, acts, head)
+    acts, maps, state, message = edge_rows(edge, log, taps, values, head, acts, maps, state)
     first_node = moved(message, 1)
     own, stats, send, rest = pair(state, log, first_node, shards)
     near_made = None
@@ -628,7 +664,9 @@
         if bit <= 2:
             half = head_count // 2
             heads = (half * (bit - 1), half * bit)
-            near_made = near(acts, maps, log, gains, first_node, stats, near_made, heads)
+            near_made = near(
+                acts, maps, log, gains, first_node, stats, gain, near_made, heads
+            )
         sources = [rest, *got[1:]] if bit == levels - 2 else []
         stats, send, own = join(own, stats, got[-1], near_made[0], bit, shards, sources)
         all_stats.append(stats)
@@ -643,14 +681,15 @@
     relayed = [{1: (0, slot * part), 3: (0, (count + slot) * part)} for slot in range(count)]
     total = middle(near_made[0], *shared, [*got, across], direct, (0, 2), levels, shards)
     node, total = lax.optimization_barrier((node, total))
-    common = (acts, log, gains, gain, all_stats[-1])
+    common = (acts, log, gains, near_made[3], all_stats[-1])
     node_across = moved(node, 2)
-    mixed = last(total, *common, node, top, levels, (0,), shards, None)
-    node_across, mixed, total = lax.optimization_barrier((node_across, mixed, total))
+    own_done = last(total, *common, node, top, levels, (0,), shards, {})
+    node_across, own_done, total = lax.optimization_barrier((node_across, own_done, total))
     node_beside = moved(jnp.concatenate([node, node_across]), 1)
     total = middle(total, *shared, [beside], relayed, (1, 3), levels, shards)
-    mixed = last(total, *common, node_across, top, levels, (2,), shards, mixed)
-    return last(total, *common, node_beside, top, levels, (1, 3), shards, mixed)
+    across_done = last(total, *common, node_across, top, levels, (2,), shards, {})
+    done = {0: own_done, 2: across_done}
+    return last(total, *common, node_beside, top, levels, (1, 3), shards, done)
 
 
 def solution(mesh):

time: 41.8 us -> 39.5 us (0.945)
  waiting for transfers between devices: 11.3 us -> 16.8 us
  starting transfers between devices: 10.6 us -> 6.15 us
  Pallas kernels: 18.7 us -> 16.2 us
  local copies, waits for them, and re-layouts: 0.81 us -> 0.03 us
    ppermute x8, starting transfers between devices: 10.1 us -> 5.65 us  [moved(): lax.ppermute(value, 'seq', [(i, i ^ apart) for i in range(lax.axis_size('...]
    ppermute x1, waiting for transfers between devices: 0.76 us -> 3.53 us  [on_device(): edge = lax.ppermute(edge, 'seq', behind)]
    ppermute x8, waiting for transfers between devices: 10.5 us -> 13.2 us  [moved(): lax.ppermute(value, 'seq', [(i, i ^ apart) for i in range(lax.axis_size('...]
    pallas_call x3, Pallas kernels: 4.46 us -> 2.97 us  [last(): pl.pallas_call(functools.partial(last_kernel, level=level, relatives=rela...]
    pallas_call x1 -> x2, Pallas kernels: 5.65 us -> 4.59 us  [the longest x1 2.87 us: front(): pl.pallas_call(front_kernel, in_specs=[VMEM_SPEC] * len(operands), out_sp...]
    slice x1 -> x0, local copies, waits for them, and re-layouts: 0.78 us -> none  [on_device(): edge = lax.ppermute(xbc[rows - taps + 1:], 'seq', behind)]
  transfers between devices with their start and end apart: 9 -> 9, of which waited for: 7 -> 8; matrix products, arithmetic and copies ran while one was open for 0% -> 0% of each run, Pallas kernels for 38% -> 29%
where the time goes in v3:
time: 39.5 us; the launch traced here: 39.4 us
  waiting for transfers between devices  16.8 us (43%)
  Pallas kernels  16.2 us (41%)
  starting transfers between devices  6.15 us (16%)
    ppermute x8, waiting for transfers between devices, moved(): lax.ppermute(value, 'seq', [(i, i ^ apart) for i in range(lax.axis_size('...  13.2 us
    pallas_call x2, Pallas kernels, near(): pl.pallas_call(functools.partial(near_kernel, first=first, wide=wide, hea...  6.01 us
    ppermute x8, starting transfers between devices, moved(): lax.ppermute(value, 'seq', [(i, i ^ apart) for i in range(lax.axis_size('...  5.65 us
    ppermute x1, waiting for transfers between devices, on_device(): edge = lax.ppermute(edge, 'seq', behind)  3.53 us
    pallas_call x3, Pallas kernels, last(): pl.pallas_call(functools.partial(last_kernel, level=level, relatives=rela...  2.97 us
    pallas_call x1, Pallas kernels, front(): pl.pallas_call(front_kernel, in_specs=[VMEM_SPEC] * len(operands), out_sp...  2.87 us
    pallas_call x1, Pallas kernels, load(): pl.pallas_call(load_kernel, in_specs=[HBM_SPEC] * 3, out_specs=[VMEM_SPEC...  1.72 us
    pallas_call x2, Pallas kernels, middle(): pl.pallas_call(functools.partial(middle_kernel, places=places, relatives=...  1.56 us
  transfers between devices with their start and end apart: 9, of which 8 were waited for; matrix products, arithmetic and copies ran while one was open for 0% of the time, Pallas kernels for 29%

profile of v3, /device:TPU:0, one launch (start us, length us, event | category | flops | bytes accessed | tf_op | source)
XLA Modules:
  0.0 39.4 jit_solution(13474128452506755948)
XLA Ops:
  0.0 1.7 %load.1 = (bf16[512,2304]{1,0:T(8,128)(2,1)S(1)}, f32[4,2304]{1,0:T(4,128)S(1)}, f32[16,512]{1,0:T(8,128)S(1)}, bf16[3,2304]{1,0:T(4,128)(2,1)S(1)}, bf16[2304,5...) custom-call(bf16[512,2304]{1,0:T(8,128)(2,1)} %xbc_hbm.1, f32[4,2304]{1,0:T(4,128)} %taps_hbm.1, ...), custom_call_target="tpu_custom_call" | custom-call | flops 1024 | bytes 1024 | tf_op jit(solution)/shard_map/load/pallas_call | solution.py:135
  1.7 0.5 %collective-permute-start = (bf16[3,2304]{1,0:T(4,128)(2,1)S(1)}, bf16[3,2304]{1,0:T(4,128)(2,1)S(1)}, u32[]{:S(2)}, u32[]{:S(2)}) collective-permute-start(bf16[3,2304]{1,0:T(4,128)(2,1)S(1)} %get-tuple-element.38), channel_id=1, source_target_pairs={{0,1},{1,2},{2,3},{3,4},{4,5},{5,6},{6,7},{7,8},{8,9},{9,10},{10,1... | collective-permute-start | bytes 41480 | tf_op jit(solution)/shard_map/ppermute | solution.py:654
  2.2 2.9 %front.1 = (bf16[2304,512]{1,0:T(8,128)(2,1)S(1)}, bf16[128,2304]{1,0:T(8,128)(2,1)S(1)}, f32[2048,128]{1,0:T(8,128)S(1)}) custom-call(bf16[512,2304]{1,0:T(8,128)(2,1)S(1)} %get-tuple-element.41.xbc_ref, f32[4,2304]{1,0:T(4,128)S(1)} %get-tuple-element.40.taps_ref, ...), custom_call_target="tpu_custom_call", output_to_operand_aliasing={{0}: (4, {}), {1}: (5, {})} | custom-call | tf_op jit(solution)/shard_map/front/pallas_call | solution.py:177
  5.1 3.5 %collective-permute-done.edge_ref = bf16[3,2304]{1,0:T(4,128)(2,1)S(1)} collective-permute-done((bf16[3,2304]{1,0:T(4,128)(2,1)S(1)}, bf16[3,2304]{1,0:T(4,128)(2,1)S(1)}, u32[]{:S(2)}, u32[]{:S(2)}) %collective-permute-start) | collective-permute-done | bytes 13856 | tf_op jit(solution)/shard_map/ppermute | solution.py:654
  8.6 0.0 copy-start
  8.6 0.0 copy-start.1
  8.6 0.5 %edge.1 = (bf16[2304,512]{1,0:T(8,128)(2,1)S(1)}, bf16[512,128]{1,0:T(8,128)(2,1)S(1)}, f32[2048,128]{1,0:T(8,128)S(1)}, bf16[2064,128]{1,0:T(8,128)(2,1)S(1)}) custom-call(bf16[3,2304]{1,0:T(4,128)(2,1)S(1)} %collective-permute-done.edge_ref, ...), custom_call_target="tpu_custom_call", output_to_operand_aliasing={{0}: (5, {}), {1}: (6, {}), {2}: (7, {})} | custom-call | flops 1024 | bytes 1024 | tf_op jit(solution)/shard_map/edge/pallas_call | solution.py:231
  9.1 0.1 collective-permute-start.1
  9.2 1.9 %collective-permute-done.1.got_ref.refs_4_ = bf16[2064,128]{1,0:T(8,128)(2,1)S(1)} collective-permute-done((bf16[2064,128]{1,0:T(8,128)(2,1)S(1)}, bf16[2064,128]{1,0:T(8,128)(2,1)S(1)}, u32[]{:S(2)}, u32[]{:S(2)}) %collective-permute-start.1) | collective-permute-done | bytes 528416 | tf_op jit(solution)/shard_map/ppermute | solution.py:641
  11.1 0.2 pair.1
  11.3 0.4 collective-permute-start.2
  11.7 0.0 copy-done
  11.7 0.0 copy-done.1
  11.7 3.1 %near.2 = (f32[2048,512]{1,0:T(8,128)S(1)}, f32[512,512]{1,0:T(8,128)S(1)}, f32[3,512,128]{2,1,0:T(8,128)S(1)}, f32[128,128]{1,0:T(8,128)S(1)}) custom-call(bf16[2304,512]{1,0:T(8,128)(2,1)S(1)} %get-tuple-element.48.refs_0_.acts_ref, bf16[512,128]{1,0:T(8,128)(2,1)S(1)} %get-tuple-element.54.refs_1_, ...), custom_call_target="tpu_custom_call" | custom-call | flops 1073741824 | bytes 10485760 | tf_op jit(solution)/shard_map/near/pallas_call | solution.py:490
  14.8 2.2 %collective-permute-done.2.got_ref.refs_5_ = bf16[528,128]{1,0:T(8,128)(2,1)S(1)} collective-permute-done((bf16[528,128]{1,0:T(8,128)(2,1)S(1)}, bf16[528,128]{1,0:T(8,128)(2,1)S(1)}, u32[]{:S(2)}, u32[]{:S(2)}) %collective-permute-start.2) | collective-permute-done | bytes 135200 | tf_op jit(solution)/shard_map/ppermute | solution.py:641
  17.0 0.2 join.2
  17.2 0.6 %collective-permute-start.3 = (bf16[528,128]{1,0:T(8,128)(2,1)S(1)}, bf16[528,128]{1,0:T(8,128)(2,1)S(1)}, u32[]{:S(2)}, u32[]{:S(2)}) collective-permute-start(bf16[528,128]{1,0:T(8,128)(2,1)S(1)} %get-tuple-element.57), channel_id=1, source_target_pairs={{0,4},{1,5},{2,6},{3,7},{4,0},{5,1},{6,2},{7,3},{8,12},{9,13},{10,... | collective-permute-start | bytes 405512 | tf_op jit(solution)/shard_map/ppermute | solution.py:641
  17.8 2.9 %near.3._.refs_8_ = f32[2048,512]{1,0:T(8,128)S(1)} custom-call(bf16[2304,512]{1,0:T(8,128)(2,1)S(1)} %get-tuple-element.48.refs_0_.acts_ref, bf16[512,128]{1,0:T(8,128)(2,1)S(1)} %get-tuple-element.54.refs_1_, f32[16,512]{1,0:T(8,128)S(1)} %get-tuple-element.39.log_ref.refs_2_.refs_1_, f32[224,512]{1,0:T(8,128)S(1)} %bitcast.5, ...), custom_call_target="tpu_custom_call", output_to_operand_aliasing={{}: (8, {})} | custom-call | flops 1073741824 | bytes 10485760 | tf_op jit(solution)/shard_map/near/pallas_call | solution.py:490
  20.7 1.6 %collective-permute-done.3.got_ref.refs_1_.refs_6_ = bf16[528,128]{1,0:T(8,128)(2,1)S(1)} collective-permute-done((bf16[528,128]{1,0:T(8,128)(2,1)S(1)}, bf16[528,128]{1,0:T(8,128)(2,1)S(1)}, u32[]{:S(2)}, u32[]{:S(2)}) %collective-permute-start.3) | collective-permute-done | bytes 135200 | tf_op jit(solution)/shard_map/ppermute | solution.py:641
  22.3 0.2 join.3
  22.5 0.6 %collective-permute-start.4 = (bf16[1024,128]{1,0:T(8,128)(2,1)S(1)}, bf16[1024,128]{1,0:T(8,128)(2,1)S(1)}, u32[]{:S(2)}, u32[]{:S(2)}) collective-permute-start(bf16[1024,128]{1,0:T(8,128)(2,1)S(1)} %get-tuple-element.62), channel_id=1, source_target_pairs={{0,2},{1,3},{2,0},{3,1},{4,6},{5,7},{6,4},{7,5},{8,10},{9,11},{10,... | collective-permute-start | bytes 786440 | tf_op jit(solution)/shard_map/ppermute | solution.py:641
  23.1 2.7 %collective-permute-start.6 = (bf16[512,128]{1,0:T(8,128)(2,1)S(1)}, bf16[512,128]{1,0:T(8,128)(2,1)S(1)}, u32[]{:S(2)}, u32[]{:S(2)}) collective-permute-start(bf16[512,128]{1,0:T(8,128)(2,1)S(1)} %get-tuple-element.63), channel_id=1, source_target_pairs={{0,8},{1,9},{2,10},{3,11},{4,12},{5,13},{6,14},{7,15},{8,0},{9,1},... | collective-permute-start | bytes 393224 | tf_op jit(solution)/shard_map/ppermute | solution.py:641
  25.8 3.1 %collective-permute-done.4.refs_7_ = bf16[1024,128]{1,0:T(8,128)(2,1)S(1)} collective-permute-done((bf16[1024,128]{1,0:T(8,128)(2,1)S(1)}, bf16[1024,128]{1,0:T(8,128)(2,1)S(1)}, u32[]{:S(2)}, u32[]{:S(2)}) %collective-permute-start.4) | collective-permute-done | bytes 262176 | tf_op jit(solution)/shard_map/ppermute | solution.py:641
  29.0 0.1 collective-permute-start.5
  29.1 0.8 %middle.2.total_ref.refs_6_ = f32[2048,512]{1,0:T(8,128)S(1)} custom-call(bf16[2304,512]{1,0:T(8,128)(2,1)S(1)} %get-tuple-element.48.refs_0_.acts_ref, f32[16,512]{1,0:T(8,128)S(1)} %get-tuple-element.39.log_ref.refs_2_.refs_1_, f32[224,512]{1,0:T(8,128)S(1)} %bitcast.6, ...), custom_call_target="tpu_custom_call", output_to_operand_aliasing={{}: (8, {})} | custom-call | flops 1024 | bytes 1024 | tf_op jit(solution)/shard_map/middle/pallas_call | solution.py:553
  29.8 0.9 %collective-permute-done.6.node_ref = bf16[512,128]{1,0:T(8,128)(2,1)S(1)} collective-permute-done((bf16[512,128]{1,0:T(8,128)(2,1)S(1)}, bf16[512,128]{1,0:T(8,128)(2,1)S(1)}, u32[]{:S(2)}, u32[]{:S(2)}) %collective-permute-start.6) | collective-permute-done | bytes 131104 | tf_op jit(solution)/shard_map/ppermute | solution.py:641
  30.7 1.2 %collective-permute-start.7 = (bf16[512,128]{1,0:T(8,128)(2,1)S(1)}, bf16[512,128]{1,0:T(8,128)(2,1)S(1)}, u32[]{:S(2)}, u32[]{:S(2)}) collective-permute-start(bf16[512,128]{1,0:T(8,128)(2,1)S(1)} %collective-permute-done.6.node_ref), channel_id=1, source_target_pairs={{0,2},{1,3},{2,0},{3,1},{4,6},{5,7},{6,4},{7,5},{8,10},{9,11},{10,... | collective-permute-start | bytes 393224 | tf_op jit(solution)/shard_map/ppermute | solution.py:641
  31.9 0.5 %last.3.refs_0_ = bf16[4,512,128]{2,1,0:T(8,128)(2,1)S(1)} custom-call(f32[2048,512]{1,0:T(8,128)S(1)} %middle.2.total_ref.refs_6_, bf16[2304,512]{1,0:T(8,128)(2,1)S(1)} %get-tuple-element.48.refs_0_.acts_ref, f32[16,512]{1,0:T(8,128)S(1)} %get-tuple-element.39.log_ref.refs_2_.refs_1_, f32[224,512]{1,0:T(8,128)S(1)} %bitcast.7, ...), custom_call_target="tpu_custom_call" | custom-call | flops 1024 | bytes 1024 | tf_op jit(solution)/shard_map/last/pallas_call | solution.py:625
  32.5 3.4 %collective-permute-done.7.node_ref = bf16[512,128]{1,0:T(8,128)(2,1)S(1)} collective-permute-done((bf16[512,128]{1,0:T(8,128)(2,1)S(1)}, bf16[512,128]{1,0:T(8,128)(2,1)S(1)}, u32[]{:S(2)}, u32[]{:S(2)}) %collective-permute-start.7) | collective-permute-done | bytes 131104 | tf_op jit(solution)/shard_map/ppermute | solution.py:641
  35.8 0.1 collective-permute-start.8
  35.9 0.0 collective-permute-done.5.refs_5_
  35.9 0.8 %middle.3.total_ref = f32[2048,512]{1,0:T(8,128)S(1)} custom-call(bf16[2304,512]{1,0:T(8,128)(2,1)S(1)} %get-tuple-element.48.refs_0_.acts_ref, f32[16,512]{1,0:T(8,128)S(1)} %get-tuple-element.39.log_ref.refs_2_.refs_1_, f32[224,512]{1,0:T(8,128)S(1)} %bitcast.8, ...), custom_call_target="tpu_custom_call", output_to_operand_aliasing={{}: (6, {})} | custom-call | flops 1024 | bytes 1024 | tf_op jit(solution)/shard_map/middle/pallas_call | solution.py:553
  36.7 0.5 %last.4.refs_1_ = bf16[4,512,128]{2,1,0:T(8,128)(2,1)S(1)} custom-call(f32[2048,512]{1,0:T(8,128)S(1)} %middle.3.total_ref, bf16[2304,512]{1,0:T(8,128)(2,1)S(1)} %get-tuple-element.48.refs_0_.acts_ref, f32[16,512]{1,0:T(8,128)S(1)} %get-tuple-element.39.log_ref.refs_2_.refs_1_, f32[224,512]{1,0:T(8,128)S(1)} %bitcast.9, ...), custom_call_target="tpu_custom_call" | custom-call | flops 1024 | bytes 1024 | tf_op jit(solution)/shard_map/last/pallas_call | solution.py:625
  37.3 0.2 collective-permute-done.8.node_ref
  37.4 1.9 %last.5 = bf16[512,2048]{1,0:T(8,128)(2,1)} custom-call(f32[2048,512]{1,0:T(8,128)S(1)} %middle.3.total_ref, bf16[2304,512]{1,0:T(8,128)(2,1)S(1)} %get-tuple-element.48.refs_0_.acts_ref, f32[16,512]{1,0:T(8,128)S(1)} %get-tuple-element.39.log_ref.refs_2_.refs_1_, f32[224,512]{1,0:T(8,128)S(1)} %bitcast.10, f32[128,128]{1,0:T(8,128)S(1)} %get-tuple-element.66.columns_ref, ...), custom_call_target="tpu_custom_call" | custom-call | flops 1024 | bytes 1024 | tf_op jit(solution)/shard_map/last/pallas_call | solution.py:625
  (4 shorter events, 0.1 us)
Async XLA Ops:
  1.7 6.9 %collective-permute-start = (bf16[3,2304]{1,0:T(4,128)(2,1)S(1)}, bf16[3,2304]{1,0:T(4,128)(2,1)S(1)}, u32[]{:S(2)}, u32[]{:S(2)}) collective-permute-start(bf16[3,2304]{1,0:T(4,128)(2,1)S(1)} %get-tuple-element.38), channel_id=1, source_target_pairs={{0,1},{1,2},{2,3},{3,4},{4,5},{5,6},{6,7},{7,8},{8,9},{9,10},{10,1... | collective-permute-start | bytes 41480 | tf_op jit(solution)/shard_map/ppermute | solution.py:654
  8.6 3.1 %copy-start = (f32[16,14,512]{2,0,1:T(8,128)S(1)}, f32[16,14,512]{2,0,1:T(8,128)}, u32[]{:S(2)}) copy-start(f32[16,14,512]{2,0,1:T(8,128)} %param.8) | copy-start | bytes 1376260
  8.6 3.1 %copy-start.1 = (f32[2048]{0:T(1024)S(1)}, f32[2048]{0:T(1024)}, u32[]{:S(2)}) copy-start(f32[2048]{0:T(1024)} %param.9) | copy-start | bytes 24580
  9.1 2.0 %collective-permute-start.1 = (bf16[2064,128]{1,0:T(8,128)(2,1)S(1)}, bf16[2064,128]{1,0:T(8,128)(2,1)S(1)}, u32[]{:S(2)}, u32[]{:S(2)}) collective-permute-start(bf16[2064,128]{1,0:T(8,128)(2,1)S(1)} %get-tuple-element.50), channel_id=1, source_target_pairs={{0,1},{1,0},{2,3},{3,2},{4,5},{5,4},{6,7},{7,6},{8,9},{9,8},{10,11... | collective-permute-start | bytes 1585160 | tf_op jit(solution)/shard_map/ppermute | solution.py:641
  11.3 5.7 %collective-permute-start.2 = (bf16[528,128]{1,0:T(8,128)(2,1)S(1)}, bf16[528,128]{1,0:T(8,128)(2,1)S(1)}, u32[]{:S(2)}, u32[]{:S(2)}) collective-permute-start(bf16[528,128]{1,0:T(8,128)(2,1)S(1)} %get-tuple-element.53), channel_id=1, source_target_pairs={{0,2},{1,3},{2,0},{3,1},{4,6},{5,7},{6,4},{7,5},{8,10},{9,11},{10,... | collective-permute-start | bytes 405512 | tf_op jit(solution)/shard_map/ppermute | solution.py:641
  17.2 5.1 %collective-permute-start.3 = (bf16[528,128]{1,0:T(8,128)(2,1)S(1)}, bf16[528,128]{1,0:T(8,128)(2,1)S(1)}, u32[]{:S(2)}, u32[]{:S(2)}) collective-permute-start(bf16[528,128]{1,0:T(8,128)(2,1)S(1)} %get-tuple-element.57), channel_id=1, source_target_pairs={{0,4},{1,5},{2,6},{3,7},{4,0},{5,1},{6,2},{7,3},{8,12},{9,13},{10,... | collective-permute-start | bytes 405512 | tf_op jit(solution)/shard_map/ppermute | solution.py:641
  22.5 6.4 %collective-permute-start.4 = (bf16[1024,128]{1,0:T(8,128)(2,1)S(1)}, bf16[1024,128]{1,0:T(8,128)(2,1)S(1)}, u32[]{:S(2)}, u32[]{:S(2)}) collective-permute-start(bf16[1024,128]{1,0:T(8,128)(2,1)S(1)} %get-tuple-element.62), channel_id=1, source_target_pairs={{0,2},{1,3},{2,0},{3,1},{4,6},{5,7},{6,4},{7,5},{8,10},{9,11},{10,... | collective-permute-start | bytes 786440 | tf_op jit(solution)/shard_map/ppermute | solution.py:641
  23.1 7.6 %collective-permute-start.6 = (bf16[512,128]{1,0:T(8,128)(2,1)S(1)}, bf16[512,128]{1,0:T(8,128)(2,1)S(1)}, u32[]{:S(2)}, u32[]{:S(2)}) collective-permute-start(bf16[512,128]{1,0:T(8,128)(2,1)S(1)} %get-tuple-element.63), channel_id=1, source_target_pairs={{0,8},{1,9},{2,10},{3,11},{4,12},{5,13},{6,14},{7,15},{8,0},{9,1},... | collective-permute-start | bytes 393224 | tf_op jit(solution)/shard_map/ppermute | solution.py:641
  29.0 7.0 %collective-permute-start.5 = (bf16[2048,128]{1,0:T(8,128)(2,1)S(1)}, bf16[2048,128]{1,0:T(8,128)(2,1)S(1)}, u32[]{:S(2)}, u32[]{:S(2)}) collective-permute-start(bf16[2048,128]{1,0:T(8,128)(2,1)S(1)} %pad_maximum_fusion), channel_id=1, source_target_pairs={{0,1},{1,0},{2,3},{3,2},{4,5},{5,4},{6,7},{7,6},{8,9},{9,8},{10,11... | collective-permute-start | bytes 1572872 | tf_op jit(solution)/shard_map/ppermute | solution.py:641
  30.7 5.1 %collective-permute-start.7 = (bf16[512,128]{1,0:T(8,128)(2,1)S(1)}, bf16[512,128]{1,0:T(8,128)(2,1)S(1)}, u32[]{:S(2)}, u32[]{:S(2)}) collective-permute-start(bf16[512,128]{1,0:T(8,128)(2,1)S(1)} %collective-permute-done.6.node_ref), channel_id=1, source_target_pairs={{0,2},{1,3},{2,0},{3,1},{4,6},{5,7},{6,4},{7,5},{8,10},{9,11},{10,... | collective-permute-start | bytes 393224 | tf_op jit(solution)/shard_map/ppermute | solution.py:641
  35.8 1.6 %collective-permute-start.8 = (bf16[1024,128]{1,0:T(8,128)(2,1)S(1)}, bf16[1024,128]{1,0:T(8,128)(2,1)S(1)}, u32[]{:S(2)}, u32[]{:S(2)}) collective-permute-start(bf16[1024,128]{1,0:T(8,128)(2,1)S(1)} %pad_maximum_fusion.1), channel_id=1, source_target_pairs={{0,1},{1,0},{2,3},{3,2},{4,5},{5,4},{6,7},{7,6},{8,9},{9,8},{10,11... | collective-permute-start | bytes 786440 | tf_op jit(solution)/shard_map/ppermute | solution.py:641

commit v4 on v3

--- a/solution.py
+++ b/solution.py
@@ -58,12 +58,28 @@
 
 
 def running_sum(logs):
-    column = lax.broadcasted_iota(jnp.int32, logs.shape, 1)
-    shift = 1
-    while shift < logs.shape[1]:
-        logs = logs + jnp.where(column >= shift, pltpu.roll(logs, shift, 1), 0.0)
-        shift *= 2
-    return logs
+    head_count, rows = logs.shape
+    tiles = rows // LANES
+    row = lax.broadcasted_iota(jnp.int32, (LANES, LANES), 0)
+    column = lax.broadcasted_iota(jnp.int32, (LANES, LANES), 1)
+    upto = (row <= column).astype(BF16)
+    left = jnp.concatenate(
+        [logs[:, tile * LANES : (tile + 1) * LANES] for tile in range(tiles)], axis=0
+    )
+    pieces = []
+    for _ in range(3):
+        pieces.append(left.astype(BF16))
+        left = left - pieces[-1].astype(F32)
+    size = head_count * tiles
+    added = product(jnp.concatenate(pieces, axis=0), upto)
+    within = added[2 * size :] + added[size : 2 * size] + added[:size]
+    sums = []
+    offset = jnp.zeros((head_count, 1), F32)
+    for tile in range(tiles):
+        part = within[tile * head_count : (tile + 1) * head_count]
+        sums.append(part + offset)
+        offset = offset + part[:, LANES - 1 :]
+    return jnp.concatenate(sums, axis=1)
 
 
 def activated(values, edge, weights, padded):
@@ -91,51 +107,74 @@
     return result, turned
 
 
+def head_columns(
+    xbc_ref, taps_ref, log_ref, maps_ref, acts_ref, head_ref, state_ref, padded, heads
+):
+    rows, _ = xbc_ref.shape
+    for head in heads:
+        place = slice(head * LANES, (head + 1) * LANES)
+        _, turned = some_columns(
+            xbc_ref, taps_ref, acts_ref, head_ref, padded.at[head % 2], head * LANES
+        )
+        logs = log_ref[head : head + 1, :]
+        tail = jnp.exp(logs[:, rows - 1 : rows] - logs[:, LANES:])
+        decayed = (turned.astype(F32) * tail).astype(BF16)
+        state_ref[place, :] = product(decayed, maps_ref[LANES:, :])
+
+
 def load_kernel(
     xbc_hbm, taps_hbm, decay_hbm, xbc_ref, taps_ref, log_ref, edge_ref, acts_ref, head_ref,
-    maps_ref, decay_buf, padded, sems
+    maps_ref, state_ref, decay_buf, padded, sems, early
 ):
     rows, width = xbc_ref.shape
     pieces = sems.shape[0] - 2
     maps_width = 2 * maps_ref.shape[1]
-    size = (width - maps_width) // (pieces - 1)
-    starts = [width - maps_width] + [piece * size for piece in range(pieces - 1)]
+    inner = width - maps_width
+    rest = (inner - early * LANES) // (pieces - 2)
+    cuts = [0] + [early * LANES + piece * rest for piece in range(pieces - 1)]
+    spans = [(inner, maps_width)] + [(x, y - x) for x, y in zip(cuts, cuts[1:])]
     copies = [
         pltpu.make_async_copy(decay_hbm, decay_buf, sems.at[pieces]),
         pltpu.make_async_copy(taps_hbm, taps_ref, sems.at[pieces + 1]),
     ]
-    for piece, start in enumerate(starts):
-        part = pl.ds(start, size if piece else maps_width)
+    for piece, (start, size) in enumerate(spans):
+        part = pl.ds(start, size)
         copies.append(
             pltpu.make_async_copy(xbc_hbm.at[:, part], xbc_ref.at[:, part], sems.at[piece])
         )
-    for copy in copies:
+    for copy in copies[:4]:
+        copy.start()
+    for copy in copies[4:]:
         copy.start()
     copies[0].wait()
     log_ref[...] = running_sum(decay_buf[...])
     copies[1].wait()
     copies[2].wait()
-    for slot, start in enumerate(range(width - LANES, width - maps_width - 1, -LANES)):
+    for slot, start in enumerate(range(width - LANES, inner - 1, -LANES)):
         result, _ = some_columns(
             xbc_ref, taps_ref, acts_ref, head_ref, padded.at[slot % 2], start
         )
     maps_ref[...] = result
-    for copy in copies[3:]:
+    copies[3].wait()
+    head_columns(
+        xbc_ref, taps_ref, log_ref, maps_ref, acts_ref, head_ref, state_ref, padded, range(early)
+    )
+    for copy in copies[4:]:
         copy.wait()
     few = edge_ref.shape[0]
     tail = xbc_ref[rows - 2 * GROUP :, :].astype(F32)
     edge_ref[...] = tail[2 * GROUP - few :].astype(BF16)
 
 
-def load(xbc, conv_weight, log_decay):
+def load(xbc, conv_weight, log_decay, early):
     rows, width = xbc.shape
-    head_count = log_decay.shape[0]
-    state_size = (width - head_count * LANES) // 2
-    pieces = 5
+    inner = log_decay.shape[0] * LANES
+    state_size = (width - inner) // 2
+    pieces = 3
     return pl.pallas_call(
-        load_kernel,
+        functools.partial(load_kernel, early=early),
         in_specs=[HBM_SPEC] * 3,
-        out_specs=[VMEM_SPEC] * 7,
+        out_specs=[VMEM_SPEC] * 8,
         out_shape=[
             pltpu.VMEM(xbc.shape, BF16),
             pltpu.VMEM(conv_weight.shape, F32),
@@ -144,6 +183,7 @@
             pltpu.VMEM((width, rows), BF16),
             pltpu.VMEM((LANES, width), BF16),
             pltpu.VMEM((rows, state_size), BF16),
+            pltpu.VMEM((inner, state_size), F32),
         ],
         scratch_shapes=[
             pltpu.VMEM(log_decay.shape, F32),
@@ -157,50 +197,47 @@
 
 
 def front_kernel(
-    xbc_ref, taps_ref, log_ref, maps_ref, acts_in, head_in, acts_ref, head_ref, state_ref, padded
+    xbc_ref, taps_ref, log_ref, maps_ref, acts_in, head_in, state_in, acts_ref, head_ref,
+    state_ref, padded, early
 ):
-    rows, _ = xbc_ref.shape
-    for head in range(log_ref.shape[0]):
-        place = slice(head * LANES, (head + 1) * LANES)
-        _, turned = some_columns(
-            xbc_ref, taps_ref, acts_ref, head_ref, padded.at[head % 2], head * LANES
-        )
-        logs = log_ref[head : head + 1, :]
-        tail = jnp.exp(logs[:, rows - 1 : rows] - logs[:, LANES:])
-        decayed = (turned.astype(F32) * tail).astype(BF16)
-        state_ref[place, :] = product(decayed, maps_ref[LANES:, :])
-
-
-def front(xbc, taps, log, maps, acts, head):
+    head_columns(
+        xbc_ref, taps_ref, log_ref, maps_ref, acts_ref, head_ref, state_ref, padded,
+        range(early, log_ref.shape[0]),
+    )
+
+
+def front(xbc, taps, log, maps, acts, head, state, early):
     rows, _ = xbc.shape
-    operands = [xbc, taps, log, maps, acts, head]
+    operands = [xbc, taps, log, maps, acts, head, state]
     return pl.pallas_call(
-        front_kernel,
+        functools.partial(front_kernel, early=early),
         in_specs=[VMEM_SPEC] * len(operands),
         out_specs=[VMEM_SPEC] * 3,
         out_shape=[
             pltpu.VMEM(acts.shape, BF16),
             pltpu.VMEM(head.shape, BF16),
-            pltpu.VMEM((log.shape[0] * LANES, maps.shape[1]), F32),
+            pltpu.VMEM(state.shape, F32),
         ],
-        input_output_aliases={4: 0, 5: 1},
+        input_output_aliases={4: 0, 5: 1, 6: 2},
         scratch_shapes=[pltpu.VMEM((2, rows + GROUP, LANES), F32)],
         compiler_params=params(),
         name="front",
     )(*in_vmem(*operands))
 
 
-def edge_kernel(edge_ref, log_ref, taps_ref, xbc_ref, head_ref, *refs):
+def edge_kernel(far_edge_ref, near_edge_ref, log_ref, taps_ref, xbc_ref, head_ref, *refs):
     acts_ref, maps_ref, state_ref, message_ref, padded = refs[-5:]
     head_count, rows = log_ref.shape
     width = head_ref.shape[1]
     inner = head_count * LANES
     few = 2 * GROUP
-    is_first = lax.axis_index("seq") == 0
+    index = lax.axis_index("seq")
 
     def first_tile(start, slot):
         part = slice(start, start + LANES)
-        edge = jnp.where(is_first, 0.0, edge_ref[:, part].astype(F32))
+        near_edge = near_edge_ref[:, part].astype(F32)
+        far_edge = far_edge_ref[:, part].astype(F32)
+        edge = jnp.where(index % 2 == 1, near_edge, jnp.where(index == 0, 0.0, far_edge))
         values = xbc_ref[:few, part].astype(F32)
         result = activated(values, edge, taps_ref[:, part], padded.at[slot])
         block = jnp.concatenate([result, head_ref[few:, part]], axis=0)
@@ -224,10 +261,10 @@
         message_ref[part, :] = state.astype(BF16)
 
 
-def edge_rows(edge, log, taps, xbc, head, acts, maps, state):
+def edge_rows(far_edge, near_edge, log, taps, xbc, head, acts, maps, state):
     head_count, _ = log.shape
     inner, state_size = state.shape
-    operands = [edge, log, taps, xbc, head, acts, maps, state]
+    operands = [far_edge, near_edge, log, taps, xbc, head, acts, maps, state]
     return pl.pallas_call(
         edge_kernel,
         in_specs=[VMEM_SPEC] * len(operands),
@@ -238,7 +275,7 @@
             pltpu.VMEM(state.shape, F32),
             pltpu.VMEM((inner + head_count, state_size), BF16),
         ],
-        input_output_aliases={5: 0, 6: 1, 7: 2},
+        input_output_aliases={6: 0, 7: 1, 8: 2},
         scratch_shapes=[pltpu.VMEM((2, 3 * GROUP, LANES), F32)],
         compiler_params=params(),
         cost_estimate=small_cost(),
@@ -579,39 +616,49 @@
     if done:
         out_hbm, mixed_ref, sems = refs[-3:]
 
-    def send(source_ref, slot, relative, local):
-        start = pl.multiple_of(((relative ^ shard) * share + local) * LANES, LANES)
+    def send(source_ref, place, relative, first, count):
+        start = pl.multiple_of((relative ^ shard) * part, part)
         copies.append(
             pltpu.make_async_copy(
-                source_ref.at[slot], out_hbm.at[:, pl.ds(start, LANES)], sems.at[len(copies)]
+                source_ref.at[place, pl.ds(first, count), :],
+                out_hbm.at[pl.ds(first, count), pl.ds(start, part)],
+                sems.at[len(copies)],
             )
         )
         copies[-1].start()
 
     if done:
         for relative, source_ref in zip(done, refs):
-            for local in range(share):
-                send(source_ref, local, relative, local)
+            send(source_ref, 0, relative, 0, rows)
     else:
         (mixed_ref,) = refs
     for place, relative in enumerate(relatives):
         term = far_product(node_ref, place * part, part, queries)
-        for local in range(share):
-            head = (relative ^ shard) * share + local
-            at = pl.ds(pl.multiple_of(head * LANES, LANES), LANES)
-            factor = far_factor(gains_ref, log_ref, stats_ref, head, level, base)
-            total = total_ref[at, :] + term[local * LANES : (local + 1) * LANES] * factor
-            mean = jnp.mean(total * total, axis=0, keepdims=True)
-            scale = lax.rsqrt(mean + 1e-05)
-            chosen = jnp.full((LANES, LANES), head, jnp.int32)
-            column = jnp.take_along_axis(
-                columns_ref[...], chosen, axis=1, mode="promise_in_bounds"
+        heads = [(relative ^ shard) * share + local for local in range(share)]
+        places = [pl.ds(pl.multiple_of(head * LANES, LANES), LANES) for head in heads]
+        factors = [
+            far_factor(gains_ref, log_ref, stats_ref, head, level, base) for head in heads
+        ]
+        gain_columns = [
+            jnp.take_along_axis(
+                columns_ref[...],
+                jnp.full((LANES, LANES), head, jnp.int32),
+                axis=1,
+                mode="promise_in_bounds",
             )
-            column = jnp.concatenate([column] * (rows // LANES), axis=1)
-            slot = place * share + local
-            mixed_ref[slot] = (total * scale * column).astype(BF16).T
+            for head in heads
+        ]
+        for first in range(0, rows, LANES):
+            span = slice(first, first + LANES)
+            for local in range(share):
+                own = term[local * LANES : (local + 1) * LANES, span]
+                total = total_ref[places[local], span] + own * factors[local][:, span]
+                mean = jnp.mean(total * total, axis=0, keepdims=True)
+                scale = lax.rsqrt(mean + 1e-05)
+                mixed = (total * scale * gain_columns[local]).astype(BF16).T
+                mixed_ref[place, span, local * LANES : (local + 1) * LANES] = mixed
             if done:
-                send(mixed_ref, slot, relative, local)
+                send(mixed_ref, place, relative, first, LANES)
     for copy in copies:
         copy.wait()
 
@@ -620,7 +667,8 @@
     head_count, rows = log.shape
     share = head_count // shards
     operands = [total, acts, log, gains, columns, stats, node, *done.values()]
-    mixed = pltpu.VMEM((share * len(relatives), rows, LANES), BF16)
+    mixed = pltpu.VMEM((len(relatives), rows, share * LANES), BF16)
+    copies = len(done) + len(relatives) * rows // LANES
     whole = jax.ShapeDtypeStruct((rows, head_count * LANES), BF16)
     return pl.pallas_call(
         functools.partial(
@@ -630,7 +678,7 @@
         in_specs=[VMEM_SPEC] * len(operands),
         out_specs=HBM_SPEC if done else VMEM_SPEC,
         out_shape=whole if done else mixed,
-        scratch_shapes=[mixed, pltpu.SemaphoreType.DMA((head_count,))] if done else [],
+        scratch_shapes=[mixed, pltpu.SemaphoreType.DMA((copies,))] if done else [],
         compiler_params=params(),
         cost_estimate=small_cost(),
         name="last",
@@ -639,6 +687,17 @@
 
 def moved(value, apart):
     return lax.ppermute(value, "seq", [(i, i ^ apart) for i in range(lax.axis_size("seq"))])
+
+
+def onward(devices):
+    route = {index: index + 1 for index in range(devices)}
+    planes = devices // 4
+    target = 0
+    for plane in range(1, planes - 1):
+        route[4 * plane + 2] = target
+        target = 4 * plane + 3
+    route[devices - 1] = target
+    return list(route.items())
 
 
 def on_device(xbc, conv_weight, log_decay, level_weights, gain):
@@ -649,11 +708,15 @@
     shards = 4
     part = head_count * LANES // shards
     gains = level_weights.transpose(1, 0, 2).reshape(-1, rows)
-    behind = [(i, (i + 1) % devices) for i in range(devices)]
-    values, taps, log, edge, acts, head, maps = load(xbc, conv_weight, log_decay)
-    edge = lax.ppermute(edge, "seq", behind)
-    acts, head, state = front(values, taps, log, maps, acts, head)
-    acts, maps, state, message = edge_rows(edge, log, taps, values, head, acts, maps, state)
+    beyond = onward(devices)
+    early = head_count // 4
+    values, taps, log, edge, acts, head, maps, state = load(xbc, conv_weight, log_decay, early)
+    far_edge = lax.ppermute(edge, "seq", beyond)
+    near_edge = moved(edge, 1)
+    acts, head, state = front(values, taps, log, maps, acts, head, state, early)
+    acts, maps, state, message = edge_rows(
+        far_edge, near_edge, log, taps, values, head, acts, maps, state
+    )
     first_node = moved(message, 1)
     own, stats, send, rest = pair(state, log, first_node, shards)
     near_made = None
@@ -674,19 +737,22 @@
 
     across = moved(own, 2)
     node = moved(send, 1 << top)
-    beside = moved(jnp.concatenate([*[kept[:part] for kept in got], across]), 1)
     count = len(got)
     shared = (acts, log, gains, all_stats[:count])
     direct = [{0: (slot, 0), 2: (count, slot * part)} for slot in range(count)]
-    relayed = [{1: (0, slot * part), 3: (0, (count + slot) * part)} for slot in range(count)]
+    relayed = [{1: (slot, 0), 3: (count + slot, 0)} for slot in range(count)]
     total = middle(near_made[0], *shared, [*got, across], direct, (0, 2), levels, shards)
     node, total = lax.optimization_barrier((node, total))
     common = (acts, log, gains, near_made[3], all_stats[-1])
     node_across = moved(node, 2)
     own_done = last(total, *common, node, top, levels, (0,), shards, {})
-    node_across, own_done, total = lax.optimization_barrier((node_across, own_done, total))
+    shares = [kept[:part] for kept in got]
+    shares += [across[slot * part : (slot + 1) * part] for slot in range(count)]
+    own_done, shares = lax.optimization_barrier((own_done, shares))
+    beside = [moved(kept, 1) for kept in shares]
+    node_across, beside, total = lax.optimization_barrier((node_across, beside, total))
     node_beside = moved(jnp.concatenate([node, node_across]), 1)
-    total = middle(total, *shared, [beside], relayed, (1, 3), levels, shards)
+    total = middle(total, *shared, beside, relayed, (1, 3), levels, shards)
     across_done = last(total, *common, node_across, top, levels, (2,), shards, {})
     done = {0: own_done, 2: across_done}
     return last(total, *common, node_beside, top, levels, (1, 3), shards, done)

time: 39.5 us -> 38.7 us (0.980)
  waiting for transfers between devices: 16.8 us -> 11.1 us
  starting transfers between devices: 6.15 us -> 11.6 us
  Pallas kernels: 16.2 us -> 15.7 us
    ppermute x8 -> x12, starting transfers between devices: 5.65 us -> 11 us  [moved(): lax.ppermute(value, 'seq', [(i, i ^ apart) for i in range(lax.axis_size('...]
    ppermute x1, waiting for transfers between devices: 3.53 us -> 0.53 us  [on_device(): far_edge = lax.ppermute(edge, 'seq', beyond)]
    ppermute x8 -> x12, waiting for transfers between devices: 13.2 us -> 10.5 us  [moved(): lax.ppermute(value, 'seq', [(i, i ^ apart) for i in range(lax.axis_size('...]
    pallas_call x2, Pallas kernels: 4.59 us -> 4.19 us  [the longest x1 2.1 us: front(): pl.pallas_call(functools.partial(front_kernel, early=early), in_specs=[VM...]
  transfers between devices with their start and end apart: 9 -> 13, of which waited for: 8 -> 8; matrix products, arithmetic and copies ran while one was open for 0% -> 0% of each run, Pallas kernels for 29% -> 28%
where the time goes in v4:
time: 38.7 us; the launch traced here: 38.5 us
  Pallas kernels  15.7 us (41%)
  starting transfers between devices  11.6 us (30%)
  waiting for transfers between devices  11.1 us (29%)
    ppermute x12, starting transfers between devices, moved(): lax.ppermute(value, 'seq', [(i, i ^ apart) for i in range(lax.axis_size('...  11 us
    ppermute x12, waiting for transfers between devices, moved(): lax.ppermute(value, 'seq', [(i, i ^ apart) for i in range(lax.axis_size('...  10.5 us
    pallas_call x2, Pallas kernels, near(): pl.pallas_call(functools.partial(near_kernel, first=first, wide=wide, hea...  6.01 us
    pallas_call x3, Pallas kernels, last(): pl.pallas_call(functools.partial(last_kernel, level=level, relatives=rela...  2.85 us
    pallas_call x1, Pallas kernels, front(): pl.pallas_call(functools.partial(front_kernel, early=early), in_specs=[VM...  2.1 us
    pallas_call x1, Pallas kernels, load(): pl.pallas_call(functools.partial(load_kernel, early=early), in_specs=[HBM...  2.09 us
    pallas_call x2, Pallas kernels, middle(): pl.pallas_call(functools.partial(middle_kernel, places=places, relatives=...  1.57 us
  transfers between devices with their start and end apart: 13, of which 8 were waited for; matrix products, arithmetic and copies ran while one was open for 0% of the time, Pallas kernels for 28%

profile of v4, /device:TPU:0, one launch (start us, length us, event | category | flops | bytes accessed | tf_op | source)
XLA Modules:
  0.0 38.5 jit_solution(337615690323443019)
XLA Ops:
  0.0 2.1 %load.1 = (bf16[512,2304]{1,0:T(8,128)(2,1)S(1)}, f32[4,2304]{1,0:T(4,128)S(1)}, f32[16,512]{1,0:T(8,128)S(1)}, bf16[3,2304]{1,0:T(4,128)(2,1)S(1)}, bf16[2304,5...) custom-call(bf16[512,2304]{1,0:T(8,128)(2,1)} %xbc_hbm.1, ...), custom_call_target="tpu_custom_call" | custom-call | flops 1024 | bytes 1024 | tf_op jit(solution)/shard_map/load/pallas_call | solution.py:174
  2.1 0.5 %collective-permute-start = (bf16[3,2304]{1,0:T(4,128)(2,1)S(1)}, bf16[3,2304]{1,0:T(4,128)(2,1)S(1)}, u32[]{:S(2)}, u32[]{:S(2)}) collective-permute-start(bf16[3,2304]{1,0:T(4,128)(2,1)S(1)} %get-tuple-element.47), channel_id=1, source_target_pairs={{0,1},{1,2},{2,3},{3,4},{4,5},{5,6},{6,0},{7,8},{8,9},{9,10},{10,7... | collective-permute-start | bytes 41480 | tf_op jit(solution)/shard_map/ppermute | solution.py:714
  2.6 2.6 %collective-permute-start.1 = (bf16[3,2304]{1,0:T(4,128)(2,1)S(1)}, bf16[3,2304]{1,0:T(4,128)(2,1)S(1)}, u32[]{:S(2)}, u32[]{:S(2)}) collective-permute-start(bf16[3,2304]{1,0:T(4,128)(2,1)S(1)} %get-tuple-element.47), channel_id=1, source_target_pairs={{0,1},{1,0},{2,3},{3,2},{4,5},{5,4},{6,7},{7,6},{8,9},{9,8},{10,11... | collective-permute-start | bytes 41480 | tf_op jit(solution)/shard_map/ppermute | solution.py:689
  5.2 2.1 %front.1 = (bf16[2304,512]{1,0:T(8,128)(2,1)S(1)}, bf16[128,2304]{1,0:T(8,128)(2,1)S(1)}, f32[2048,128]{1,0:T(8,128)S(1)}) custom-call(bf16[512,2304]{1,0:T(8,128)(2,1)S(1)} %get-tuple-element.50.xbc_ref, f32[4,2304]{1,0:T(4,128)S(1)} %get-tuple-element.49.taps_ref, ...), custom_call_target="tpu_custom_call", output_to_operand_aliasing={{0}: (4, {}), {1}: (5, {}), {2}: (6, {})} | custom-call | tf_op jit(solution)/shard_map/front/pallas_call | solution.py:212
  7.3 0.5 %collective-permute-done.far_edge_ref = bf16[3,2304]{1,0:T(4,128)(2,1)S(1)} collective-permute-done((bf16[3,2304]{1,0:T(4,128)(2,1)S(1)}, bf16[3,2304]{1,0:T(4,128)(2,1)S(1)}, u32[]{:S(2)}, u32[]{:S(2)}) %collective-permute-start) | collective-permute-done | bytes 13856 | tf_op jit(solution)/shard_map/ppermute | solution.py:714
  7.8 0.0 collective-permute-done.1.near_edge_ref
  7.9 0.0 copy-start
  7.9 0.0 copy-start.1
  7.9 0.5 %edge.1 = (bf16[2304,512]{1,0:T(8,128)(2,1)S(1)}, bf16[512,128]{1,0:T(8,128)(2,1)S(1)}, f32[2048,128]{1,0:T(8,128)S(1)}, bf16[2064,128]{1,0:T(8,128)(2,1)S(1)}) custom-call(bf16[3,2304]{1,0:T(4,128)(2,1)S(1)} %collective-permute-done.far_edge_ref, ...), custom_call_target="tpu_custom_call", output_to_operand_aliasing={{0}: (6, {}), {1}: (7, {}), {2}: (8, {})} | custom-call | flops 1024 | bytes 1024 | tf_op jit(solution)/shard_map/edge/pallas_call | solution.py:268
  8.3 0.1 collective-permute-start.2
  8.4 1.9 %collective-permute-done.2.got_ref.refs_4_ = bf16[2064,128]{1,0:T(8,128)(2,1)S(1)} collective-permute-done((bf16[2064,128]{1,0:T(8,128)(2,1)S(1)}, bf16[2064,128]{1,0:T(8,128)(2,1)S(1)}, u32[]{:S(2)}, u32[]{:S(2)}) %collective-permute-start.2) | collective-permute-done | bytes 528416 | tf_op jit(solution)/shard_map/ppermute | solution.py:689
  10.3 0.2 pair.1
  10.5 1.1 %collective-permute-start.3 = (bf16[528,128]{1,0:T(8,128)(2,1)S(1)}, bf16[528,128]{1,0:T(8,128)(2,1)S(1)}, u32[]{:S(2)}, u32[]{:S(2)}) collective-permute-start(bf16[528,128]{1,0:T(8,128)(2,1)S(1)} %get-tuple-element.63), channel_id=1, source_target_pairs={{0,2},{1,3},{2,0},{3,1},{4,6},{5,7},{6,4},{7,5},{8,10},{9,11},{10,... | collective-permute-start | bytes 405512 | tf_op jit(solution)/shard_map/ppermute | solution.py:689
  11.7 0.0 copy-done
  11.7 0.0 copy-done.1
  11.7 3.1 %near.2 = (f32[2048,512]{1,0:T(8,128)S(1)}, f32[512,512]{1,0:T(8,128)S(1)}, f32[3,512,128]{2,1,0:T(8,128)S(1)}, f32[128,128]{1,0:T(8,128)S(1)}) custom-call(bf16[2304,512]{1,0:T(8,128)(2,1)S(1)} %get-tuple-element.58.refs_0_.acts_ref, bf16[512,128]{1,0:T(8,128)(2,1)S(1)} %get-tuple-element.64.refs_1_, ...), custom_call_target="tpu_custom_call" | custom-call | flops 1073741824 | bytes 10485760 | tf_op jit(solution)/shard_map/near/pallas_call | solution.py:527
  14.8 1.4 %collective-permute-done.3.got_ref.refs_5_ = bf16[528,128]{1,0:T(8,128)(2,1)S(1)} collective-permute-done((bf16[528,128]{1,0:T(8,128)(2,1)S(1)}, bf16[528,128]{1,0:T(8,128)(2,1)S(1)}, u32[]{:S(2)}, u32[]{:S(2)}) %collective-permute-start.3) | collective-permute-done | bytes 135200 | tf_op jit(solution)/shard_map/ppermute | solution.py:689
  16.2 0.2 join.2
  16.4 1.5 %collective-permute-start.4 = (bf16[528,128]{1,0:T(8,128)(2,1)S(1)}, bf16[528,128]{1,0:T(8,128)(2,1)S(1)}, u32[]{:S(2)}, u32[]{:S(2)}) collective-permute-start(bf16[528,128]{1,0:T(8,128)(2,1)S(1)} %get-tuple-element.68), channel_id=1, source_target_pairs={{0,4},{1,5},{2,6},{3,7},{4,0},{5,1},{6,2},{7,3},{8,12},{9,13},{10,... | collective-permute-start | bytes 405512 | tf_op jit(solution)/shard_map/ppermute | solution.py:689
  17.9 2.9 %near.3._.refs_8_ = f32[2048,512]{1,0:T(8,128)S(1)} custom-call(bf16[2304,512]{1,0:T(8,128)(2,1)S(1)} %get-tuple-element.58.refs_0_.acts_ref, bf16[512,128]{1,0:T(8,128)(2,1)S(1)} %get-tuple-element.64.refs_1_, f32[16,512]{1,0:T(8,128)S(1)} %get-tuple-element.48.log_ref.refs_2_.refs_1_, f32[224,512]{1,0:T(8,128)S(1)} %bitcast.5, ...), custom_call_target="tpu_custom_call", output_to_operand_aliasing={{}: (8, {})} | custom-call | flops 1073741824 | bytes 10485760 | tf_op jit(solution)/shard_map/near/pallas_call | solution.py:527
  20.8 0.7 %collective-permute-done.4.got_ref.refs_1_.refs_6_ = bf16[528,128]{1,0:T(8,128)(2,1)S(1)} collective-permute-done((bf16[528,128]{1,0:T(8,128)(2,1)S(1)}, bf16[528,128]{1,0:T(8,128)(2,1)S(1)}, u32[]{:S(2)}, u32[]{:S(2)}) %collective-permute-start.4) | collective-permute-done | bytes 135200 | tf_op jit(solution)/shard_map/ppermute | solution.py:689
  21.5 0.2 join.3
  21.7 1.1 %collective-permute-start.6 = (bf16[1024,128]{1,0:T(8,128)(2,1)S(1)}, bf16[1024,128]{1,0:T(8,128)(2,1)S(1)}, u32[]{:S(2)}, u32[]{:S(2)}) collective-permute-start(bf16[1024,128]{1,0:T(8,128)(2,1)S(1)} %get-tuple-element.73), channel_id=1, source_target_pairs={{0,2},{1,3},{2,0},{3,1},{4,6},{5,7},{6,4},{7,5},{8,10},{9,11},{10,... | collective-permute-start | bytes 786440 | tf_op jit(solution)/shard_map/ppermute | solution.py:689
  22.8 2.6 %collective-permute-start.5 = (bf16[512,128]{1,0:T(8,128)(2,1)S(1)}, bf16[512,128]{1,0:T(8,128)(2,1)S(1)}, u32[]{:S(2)}, u32[]{:S(2)}) collective-permute-start(bf16[512,128]{1,0:T(8,128)(2,1)S(1)} %get-tuple-element.72), channel_id=1, source_target_pairs={{0,8},{1,9},{2,10},{3,11},{4,12},{5,13},{6,14},{7,15},{8,0},{9,1},... | collective-permute-start | bytes 393224 | tf_op jit(solution)/shard_map/ppermute | solution.py:689
  25.4 2.9 %collective-permute-done.6.refs_7_ = bf16[1024,128]{1,0:T(8,128)(2,1)S(1)} collective-permute-done((bf16[1024,128]{1,0:T(8,128)(2,1)S(1)}, bf16[1024,128]{1,0:T(8,128)(2,1)S(1)}, u32[]{:S(2)}, u32[]{:S(2)}) %collective-permute-start.6) | collective-permute-done | bytes 262176 | tf_op jit(solution)/shard_map/ppermute | solution.py:689
  28.3 0.8 %middle.2.total_ref.refs_9_ = f32[2048,512]{1,0:T(8,128)S(1)} custom-call(bf16[2304,512]{1,0:T(8,128)(2,1)S(1)} %get-tuple-element.58.refs_0_.acts_ref, f32[16,512]{1,0:T(8,128)S(1)} %get-tuple-element.48.log_ref.refs_2_.refs_1_, f32[224,512]{1,0:T(8,128)S(1)} %bitcast.6, ...), custom_call_target="tpu_custom_call", output_to_operand_aliasing={{}: (8, {})} | custom-call | flops 1024 | bytes 1024 | tf_op jit(solution)/shard_map/middle/pallas_call | solution.py:590
  29.1 1.0 %collective-permute-done.5.node_ref = bf16[512,128]{1,0:T(8,128)(2,1)S(1)} collective-permute-done((bf16[512,128]{1,0:T(8,128)(2,1)S(1)}, bf16[512,128]{1,0:T(8,128)(2,1)S(1)}, u32[]{:S(2)}, u32[]{:S(2)}) %collective-permute-start.5) | collective-permute-done | bytes 131104 | tf_op jit(solution)/shard_map/ppermute | solution.py:689
  30.1 0.9 %collective-permute-start.7 = (bf16[512,128]{1,0:T(8,128)(2,1)S(1)}, bf16[512,128]{1,0:T(8,128)(2,1)S(1)}, u32[]{:S(2)}, u32[]{:S(2)}) collective-permute-start(bf16[512,128]{1,0:T(8,128)(2,1)S(1)} %collective-permute-done.5.node_ref), channel_id=1, source_target_pairs={{0,2},{1,3},{2,0},{3,1},{4,6},{5,7},{6,4},{7,5},{8,10},{9,11},{10,... | collective-permute-start | bytes 393224 | tf_op jit(solution)/shard_map/ppermute | solution.py:689
  31.1 0.5 %last.3.refs_0_ = bf16[1,512,512]{2,1,0:T(8,128)(2,1)S(1)} custom-call(f32[2048,512]{1,0:T(8,128)S(1)} %middle.2.total_ref.refs_9_, bf16[2304,512]{1,0:T(8,128)(2,1)S(1)} %get-tuple-element.58.refs_0_.acts_ref, f32[16,512]{1,0:T(8,128)S(1)} %get-tuple-element.48.log_ref.refs_2_.refs_1_, f32[224,512]{1,0:T(8,128)S(1)} %bitcast.7, ...), custom_call_target="tpu_custom_call" | custom-call | flops 1024 | bytes 1024 | tf_op jit(solution)/shard_map/last/pallas_call | solution.py:673
  31.6 0.1 collective-permute-start.8
  31.7 0.5 %collective-permute-start.9 = (bf16[512,128]{1,0:T(8,128)(2,1)S(1)}, bf16[512,128]{1,0:T(8,128)(2,1)S(1)}, u32[]{:S(2)}, u32[]{:S(2)}) collective-permute-start(bf16[512,128]{1,0:T(8,128)(2,1)S(1)} %slice.17), channel_id=1, source_target_pairs={{0,1},{1,0},{2,3},{3,2},{4,5},{5,4},{6,7},{7,6},{8,9},{9,8},{10,11... | collective-permute-start | bytes 393224 | tf_op jit(solution)/shard_map/ppermute | solution.py:689
  32.2 0.1 collective-permute-start.10
  32.3 0.4 %collective-permute-start.11 = (bf16[512,128]{1,0:T(8,128)(2,1)S(1)}, bf16[512,128]{1,0:T(8,128)(2,1)S(1)}, u32[]{:S(2)}, u32[]{:S(2)}) collective-permute-start(bf16[512,128]{1,0:T(8,128)(2,1)S(1)} %get-tuple-element.81), channel_id=1, source_target_pairs={{0,1},{1,0},{2,3},{3,2},{4,5},{5,4},{6,7},{7,6},{8,9},{9,8},{10,11... | collective-permute-start | bytes 393224 | tf_op jit(solution)/shard_map/ppermute | solution.py:689
  32.7 2.4 %collective-permute-done.7.node_ref = bf16[512,128]{1,0:T(8,128)(2,1)S(1)} collective-permute-done((bf16[512,128]{1,0:T(8,128)(2,1)S(1)}, bf16[512,128]{1,0:T(8,128)(2,1)S(1)}, u32[]{:S(2)}, u32[]{:S(2)}) %collective-permute-start.7) | collective-permute-done | bytes 131104 | tf_op jit(solution)/shard_map/ppermute | solution.py:689
  35.1 0.0 collective-permute-done.8.refs_5_
  35.1 0.0 collective-permute-done.9.refs_6_
  35.1 0.0 collective-permute-done.10.refs_7_
  35.1 0.0 collective-permute-done.11.refs_8_
  35.2 0.1 collective-permute-start.12
  35.2 0.8 %middle.3.total_ref = f32[2048,512]{1,0:T(8,128)S(1)} custom-call(bf16[2304,512]{1,0:T(8,128)(2,1)S(1)} %get-tuple-element.58.refs_0_.acts_ref, f32[16,512]{1,0:T(8,128)S(1)} %get-tuple-element.48.log_ref.refs_2_.refs_1_, f32[224,512]{1,0:T(8,128)S(1)} %bitcast.8, ...), custom_call_target="tpu_custom_call", output_to_operand_aliasing={{}: (9, {})} | custom-call | flops 1024 | bytes 1024 | tf_op jit(solution)/shard_map/middle/pallas_call | solution.py:590
  36.0 0.5 %last.4.refs_1_ = bf16[1,512,512]{2,1,0:T(8,128)(2,1)S(1)} custom-call(f32[2048,512]{1,0:T(8,128)S(1)} %middle.3.total_ref, bf16[2304,512]{1,0:T(8,128)(2,1)S(1)} %get-tuple-element.58.refs_0_.acts_ref, f32[16,512]{1,0:T(8,128)S(1)} %get-tuple-element.48.log_ref.refs_2_.refs_1_, f32[224,512]{1,0:T(8,128)S(1)} %bitcast.9, ...), custom_call_target="tpu_custom_call" | custom-call | flops 1024 | bytes 1024 | tf_op jit(solution)/shard_map/last/pallas_call | solution.py:673
  36.6 0.2 collective-permute-done.12.node_ref
  36.8 1.8 %last.5 = bf16[512,2048]{1,0:T(8,128)(2,1)} custom-call(f32[2048,512]{1,0:T(8,128)S(1)} %middle.3.total_ref, bf16[2304,512]{1,0:T(8,128)(2,1)S(1)} %get-tuple-element.58.refs_0_.acts_ref, f32[16,512]{1,0:T(8,128)S(1)} %get-tuple-element.48.log_ref.refs_2_.refs_1_, f32[224,512]{1,0:T(8,128)S(1)} %bitcast.10, f32[128,128]{1,0:T(8,128)S(1)} %get-tuple-element.76.columns_ref, ...), custom_call_target="tpu_custom_call" | custom-call | flops 1024 | bytes 1024 | tf_op jit(solution)/shard_map/last/pallas_call | solution.py:673
  (4 shorter events, 0.1 us)
Async XLA Ops:
  2.1 5.8 %collective-permute-start = (bf16[3,2304]{1,0:T(4,128)(2,1)S(1)}, bf16[3,2304]{1,0:T(4,128)(2,1)S(1)}, u32[]{:S(2)}, u32[]{:S(2)}) collective-permute-start(bf16[3,2304]{1,0:T(4,128)(2,1)S(1)} %get-tuple-element.47), channel_id=1, source_target_pairs={{0,1},{1,2},{2,3},{3,4},{4,5},{5,6},{6,0},{7,8},{8,9},{9,10},{10,7... | collective-permute-start | bytes 41480 | tf_op jit(solution)/shard_map/ppermute | solution.py:714
  2.6 5.2 %collective-permute-start.1 = (bf16[3,2304]{1,0:T(4,128)(2,1)S(1)}, bf16[3,2304]{1,0:T(4,128)(2,1)S(1)}, u32[]{:S(2)}, u32[]{:S(2)}) collective-permute-start(bf16[3,2304]{1,0:T(4,128)(2,1)S(1)} %get-tuple-element.47), channel_id=1, source_target_pairs={{0,1},{1,0},{2,3},{3,2},{4,5},{5,4},{6,7},{7,6},{8,9},{9,8},{10,11... | collective-permute-start | bytes 41480 | tf_op jit(solution)/shard_map/ppermute | solution.py:689
  7.9 3.8 %copy-start = (f32[16,14,512]{2,0,1:T(8,128)S(1)}, f32[16,14,512]{2,0,1:T(8,128)}, u32[]{:S(2)}) copy-start(f32[16,14,512]{2,0,1:T(8,128)} %param.8) | copy-start | bytes 1376260
  7.9 3.8 %copy-start.1 = (f32[2048]{0:T(1024)S(1)}, f32[2048]{0:T(1024)}, u32[]{:S(2)}) copy-start(f32[2048]{0:T(1024)} %param.9) | copy-start | bytes 24580
  8.3 2.0 %collective-permute-start.2 = (bf16[2064,128]{1,0:T(8,128)(2,1)S(1)}, bf16[2064,128]{1,0:T(8,128)(2,1)S(1)}, u32[]{:S(2)}, u32[]{:S(2)}) collective-permute-start(bf16[2064,128]{1,0:T(8,128)(2,1)S(1)} %get-tuple-element.60), channel_id=1, source_target_pairs={{0,1},{1,0},{2,3},{3,2},{4,5},{5,4},{6,7},{7,6},{8,9},{9,8},{10,11... | collective-permute-start | bytes 1585160 | tf_op jit(solution)/shard_map/ppermute | solution.py:689
  10.5 5.7 %collective-permute-start.3 = (bf16[528,128]{1,0:T(8,128)(2,1)S(1)}, bf16[528,128]{1,0:T(8,128)(2,1)S(1)}, u32[]{:S(2)}, u32[]{:S(2)}) collective-permute-start(bf16[528,128]{1,0:T(8,128)(2,1)S(1)} %get-tuple-element.63), channel_id=1, source_target_pairs={{0,2},{1,3},{2,0},{3,1},{4,6},{5,7},{6,4},{7,5},{8,10},{9,11},{10,... | collective-permute-start | bytes 405512 | tf_op jit(solution)/shard_map/ppermute | solution.py:689
  16.4 5.1 %collective-permute-start.4 = (bf16[528,128]{1,0:T(8,128)(2,1)S(1)}, bf16[528,128]{1,0:T(8,128)(2,1)S(1)}, u32[]{:S(2)}, u32[]{:S(2)}) collective-permute-start(bf16[528,128]{1,0:T(8,128)(2,1)S(1)} %get-tuple-element.68), channel_id=1, source_target_pairs={{0,4},{1,5},{2,6},{3,7},{4,0},{5,1},{6,2},{7,3},{8,12},{9,13},{10,... | collective-permute-start | bytes 405512 | tf_op jit(solution)/shard_map/ppermute | solution.py:689
  21.7 6.6 %collective-permute-start.6 = (bf16[1024,128]{1,0:T(8,128)(2,1)S(1)}, bf16[1024,128]{1,0:T(8,128)(2,1)S(1)}, u32[]{:S(2)}, u32[]{:S(2)}) collective-permute-start(bf16[1024,128]{1,0:T(8,128)(2,1)S(1)} %get-tuple-element.73), channel_id=1, source_target_pairs={{0,2},{1,3},{2,0},{3,1},{4,6},{5,7},{6,4},{7,5},{8,10},{9,11},{10,... | collective-permute-start | bytes 786440 | tf_op jit(solution)/shard_map/ppermute | solution.py:689
  22.8 7.3 %collective-permute-start.5 = (bf16[512,128]{1,0:T(8,128)(2,1)S(1)}, bf16[512,128]{1,0:T(8,128)(2,1)S(1)}, u32[]{:S(2)}, u32[]{:S(2)}) collective-permute-start(bf16[512,128]{1,0:T(8,128)(2,1)S(1)} %get-tuple-element.72), channel_id=1, source_target_pairs={{0,8},{1,9},{2,10},{3,11},{4,12},{5,13},{6,14},{7,15},{8,0},{9,1},... | collective-permute-start | bytes 393224 | tf_op jit(solution)/shard_map/ppermute | solution.py:689
  30.1 5.0 %collective-permute-start.7 = (bf16[512,128]{1,0:T(8,128)(2,1)S(1)}, bf16[512,128]{1,0:T(8,128)(2,1)S(1)}, u32[]{:S(2)}, u32[]{:S(2)}) collective-permute-start(bf16[512,128]{1,0:T(8,128)(2,1)S(1)} %collective-permute-done.5.node_ref), channel_id=1, source_target_pairs={{0,2},{1,3},{2,0},{3,1},{4,6},{5,7},{6,4},{7,5},{8,10},{9,11},{10,... | collective-permute-start | bytes 393224 | tf_op jit(solution)/shard_map/ppermute | solution.py:689
  31.6 3.5 %collective-permute-start.8 = (bf16[512,128]{1,0:T(8,128)(2,1)S(1)}, bf16[512,128]{1,0:T(8,128)(2,1)S(1)}, u32[]{:S(2)}, u32[]{:S(2)}) collective-permute-start(bf16[512,128]{1,0:T(8,128)(2,1)S(1)} %slice.16), channel_id=1, source_target_pairs={{0,1},{1,0},{2,3},{3,2},{4,5},{5,4},{6,7},{7,6},{8,9},{9,8},{10,11... | collective-permute-start | bytes 393224 | tf_op jit(solution)/shard_map/ppermute | solution.py:689
  31.7 3.4 %collective-permute-start.9 = (bf16[512,128]{1,0:T(8,128)(2,1)S(1)}, bf16[512,128]{1,0:T(8,128)(2,1)S(1)}, u32[]{:S(2)}, u32[]{:S(2)}) collective-permute-start(bf16[512,128]{1,0:T(8,128)(2,1)S(1)} %slice.17), channel_id=1, source_target_pairs={{0,1},{1,0},{2,3},{3,2},{4,5},{5,4},{6,7},{7,6},{8,9},{9,8},{10,11... | collective-permute-start | bytes 393224 | tf_op jit(solution)/shard_map/ppermute | solution.py:689
  32.2 2.9 %collective-permute-start.10 = (bf16[512,128]{1,0:T(8,128)(2,1)S(1)}, bf16[512,128]{1,0:T(8,128)(2,1)S(1)}, u32[]{:S(2)}, u32[]{:S(2)}) collective-permute-start(bf16[512,128]{1,0:T(8,128)(2,1)S(1)} %get-tuple-element.80), channel_id=1, source_target_pairs={{0,1},{1,0},{2,3},{3,2},{4,5},{5,4},{6,7},{7,6},{8,9},{9,8},{10,11... | collective-permute-start | bytes 393224 | tf_op jit(solution)/shard_map/ppermute | solution.py:689
  32.3 2.8 %collective-permute-start.11 = (bf16[512,128]{1,0:T(8,128)(2,1)S(1)}, bf16[512,128]{1,0:T(8,128)(2,1)S(1)}, u32[]{:S(2)}, u32[]{:S(2)}) collective-permute-start(bf16[512,128]{1,0:T(8,128)(2,1)S(1)} %get-tuple-element.81), channel_id=1, source_target_pairs={{0,1},{1,0},{2,3},{3,2},{4,5},{5,4},{6,7},{7,6},{8,9},{9,8},{10,11... | collective-permute-start | bytes 393224 | tf_op jit(solution)/shard_map/ppermute | solution.py:689
  35.2 1.6 %collective-permute-start.12 = (bf16[1024,128]{1,0:T(8,128)(2,1)S(1)}, bf16[1024,128]{1,0:T(8,128)(2,1)S(1)}, u32[]{:S(2)}, u32[]{:S(2)}) collective-permute-start(bf16[1024,128]{1,0:T(8,128)(2,1)S(1)} %pad_maximum_fusion), channel_id=1, source_target_pairs={{0,1},{1,0},{2,3},{3,2},{4,5},{5,4},{6,7},{7,6},{8,9},{9,8},{10,11... | collective-permute-start | bytes 786440 | tf_op jit(solution)/shard_map/ppermute | solution.py:689

commit v5 on v4

--- a/solution.py
+++ b/solution.py
@@ -225,8 +225,10 @@
     )(*in_vmem(*operands))
 
 
-def edge_kernel(far_edge_ref, near_edge_ref, log_ref, taps_ref, xbc_ref, head_ref, *refs):
-    acts_ref, maps_ref, state_ref, message_ref, padded = refs[-5:]
+def edge_kernel(
+    far_edge_ref, near_edge_ref, log_ref, taps_ref, xbc_ref, head_ref, *refs, shards
+):
+    acts_ref, maps_ref, state_ref, away_ref, home_ref, padded = refs[-6:]
     head_count, rows = log_ref.shape
     width = head_ref.shape[1]
     inner = head_count * LANES
@@ -249,7 +251,8 @@
     maps, _ = first_tile(width - 2 * LANES, 1)
     maps_ref[:LANES, :] = maps
     totals = jnp.broadcast_to(log_ref[:, rows - 1 : rows], (head_count, LANES))
-    write_spans(message_ref, inner, totals)
+    write_spans(away_ref, inner // 2, totals)
+    parity = index % 2
     for head in range(head_count):
         part = slice(head * LANES, (head + 1) * LANES)
         _, turned = first_tile(head * LANES, head % padded.shape[0])
@@ -258,22 +261,29 @@
         decayed = (turned.astype(F32) * tail).astype(BF16)
         state = state_ref[part, :] + product(decayed, maps)
         state_ref[part, :] = state
-        message_ref[part, :] = state.astype(BF16)
-
-
-def edge_rows(far_edge, near_edge, log, taps, xbc, head, acts, maps, state):
+    part = inner // shards
+    for slot in range(shards // 2):
+        place = slice(slot * part, (slot + 1) * part)
+        kept = pl.multiple_of((2 * slot + parity) * part, part)
+        given = pl.multiple_of((2 * slot + 1 - parity) * part, part)
+        away_ref[place, :] = state_ref[pl.ds(given, part), :].astype(BF16)
+        home_ref[place, :] = state_ref[pl.ds(kept, part), :].astype(BF16)
+
+
+def edge_rows(far_edge, near_edge, log, taps, xbc, head, acts, maps, state, shards):
     head_count, _ = log.shape
     inner, state_size = state.shape
     operands = [far_edge, near_edge, log, taps, xbc, head, acts, maps, state]
     return pl.pallas_call(
-        edge_kernel,
+        functools.partial(edge_kernel, shards=shards),
         in_specs=[VMEM_SPEC] * len(operands),
-        out_specs=[VMEM_SPEC] * 4,
+        out_specs=[VMEM_SPEC] * 5,
         out_shape=[
             pltpu.VMEM(acts.shape, BF16),
             pltpu.VMEM(maps.shape, BF16),
             pltpu.VMEM(state.shape, F32),
-            pltpu.VMEM((inner + head_count, state_size), BF16),
+            pltpu.VMEM((inner // 2 + head_count, state_size), BF16),
+            pltpu.VMEM((inner // 2, state_size), BF16),
         ],
         input_output_aliases={6: 0, 7: 1, 8: 2},
         scratch_shapes=[pltpu.VMEM((2, 3 * GROUP, LANES), F32)],
@@ -289,20 +299,21 @@
     index = lax.axis_index("seq")
     is_upper = index % 2 == 1
     mine = jnp.broadcast_to(log_ref[:, rows - 1 : rows], (head_count, LANES))
-    theirs = read_spans(got_ref, inner, head_count)
+    theirs = read_spans(got_ref, inner // 2, head_count)
     stats_ref[0] = mine + theirs
     stats_ref[1] = jnp.where(is_upper, theirs, 0.0)
     write_spans(send_ref, inner // shards, mine + theirs)
-    write_spans(rest_ref, inner // shards, mine + theirs)
     stats_ref[2] = jnp.exp(mine)
     stats_ref[3] = jnp.exp(theirs)
     shard = index % shards
     share = head_count // shards
 
-    def joined(head):
+    def joined(owner, local):
+        head = owner * share + local
         at = pl.ds(pl.multiple_of(head * LANES, LANES), LANES)
         own = state_ref[at, :]
-        got = got_ref[at, :].astype(F32)
+        start = pl.multiple_of((owner // 2 * share + local) * LANES, LANES)
+        got = got_ref[pl.ds(start, LANES), :].astype(F32)
         late = jnp.where(is_upper, own, got)
         early = jnp.where(is_upper, got, own)
         late_row = jnp.where(is_upper, 2, 3)
@@ -310,8 +321,8 @@
 
     for local in range(share):
         place = slice(local * LANES, (local + 1) * LANES)
-        send_ref[place, :] = joined((shard ^ 2) * share + local).astype(BF16)
-        kept = joined(shard * share + local)
+        send_ref[place, :] = joined(shard ^ 2, local).astype(BF16)
+        kept = joined(shard, local)
         own_ref[place, :] = kept
         rest_ref[place, :] = kept.astype(BF16)
 
@@ -328,7 +339,7 @@
             pltpu.VMEM((part, state_size), F32),
             pltpu.VMEM((4, head_count, LANES), F32),
             pltpu.VMEM((part + head_count, state_size), BF16),
-            pltpu.VMEM((part + head_count, state_size), BF16),
+            pltpu.VMEM((part, state_size), BF16),
         ],
         compiler_params=params(),
         cost_estimate=small_cost(),
@@ -396,7 +407,7 @@
     return counted
 
 
-def near_kernel(*refs, first, wide, heads):
+def near_kernel(*refs, first, wide, heads, shards):
     if first:
         acts_ref, maps_ref, log_ref, gains_ref, node_ref, _, gain_ref = refs[:7]
         near_ref, scores, tails, columns_ref, turned, weights = refs[7:]
@@ -447,7 +458,9 @@
         lax.broadcasted_iota(jnp.int32, (groups, 1, LANES), 2) // GROUP
         == lax.broadcasted_iota(jnp.int32, (groups, 1, LANES), 0)
     )
-    is_upper = lax.axis_index("seq") % 2 == 1
+    index = lax.axis_index("seq")
+    is_upper = index % 2 == 1
+    share = head_count // shards
 
     def spread(kind, place, head):
         chosen = jnp.full((LANES, LANES), head, jnp.int32)
@@ -492,7 +505,11 @@
         at = pl.ds(pl.multiple_of(head * LANES, LANES), LANES)
         level = tile_levels + tile_bits + 1
         factor = gain_rows[level] * jnp.exp(jnp.where(is_upper, logs, -1e30))
-        far = product(node_ref[at, :], queries) * factor
+        owner, local = head // share, head % share
+        start = jnp.where(owner % 2 == index % 2, 0, inner // 2)
+        start = start + (owner // 2 * share + local) * LANES
+        node = node_ref[pl.ds(pl.multiple_of(start, LANES), LANES), :]
+        far = product(node, queries) * factor
         for start in range(0, rows, wide):
             upto = start + wide
             near_ref[at, start:upto] = far[:, start:upto] + product(
@@ -507,7 +524,7 @@
     lax.fori_loop(heads[0] // weights.shape[0], heads[1] // weights.shape[0], some_heads, 0)
 
 
-def near(acts, maps, log, gains, node, after, gain, earlier, heads):
+def near(acts, maps, log, gains, node, after, gain, earlier, heads, shards):
     head_count, rows = log.shape
     wide = min(rows, 2 * LANES)
     tile_bits = (rows // LANES).bit_length() - 1
@@ -525,7 +542,7 @@
         operands += [scores, tails, near_term]
         aliases = {len(operands) - 1: 0}
     made = pl.pallas_call(
-        functools.partial(near_kernel, first=first, wide=wide, heads=heads),
+        functools.partial(near_kernel, first=first, wide=wide, heads=heads, shards=shards),
         in_specs=[VMEM_SPEC] * len(operands),
         out_specs=[VMEM_SPEC] * len(out_shape),
         out_shape=out_shape,
@@ -714,11 +731,12 @@
     far_edge = lax.ppermute(edge, "seq", beyond)
     near_edge = moved(edge, 1)
     acts, head, state = front(values, taps, log, maps, acts, head, state, early)
-    acts, maps, state, message = edge_rows(
-        far_edge, near_edge, log, taps, values, head, acts, maps, state
+    acts, maps, state, away, home = edge_rows(
+        far_edge, near_edge, log, taps, values, head, acts, maps, state, shards
     )
-    first_node = moved(message, 1)
-    own, stats, send, rest = pair(state, log, first_node, shards)
+    joined = moved(away, 1)
+    first_node = jnp.concatenate([joined[: home.shape[0]], moved(home, 1)])
+    own, stats, send, rest = pair(state, log, joined, shards)
     near_made = None
     all_stats = [stats]
     got = []
@@ -728,7 +746,7 @@
             half = head_count // 2
             heads = (half * (bit - 1), half * bit)
             near_made = near(
-                acts, maps, log, gains, first_node, stats, gain, near_made, heads
+                acts, maps, log, gains, first_node, stats, gain, near_made, heads, shards
             )
         sources = [rest, *got[1:]] if bit == levels - 2 else []
         stats, send, own = join(own, stats, got[-1], near_made[0], bit, shards, sources)

time: 38.7 us -> 38.4 us (level)
  waiting for transfers between devices: 11.1 us -> 10.1 us
  starting transfers between devices: 11.6 us -> 12 us
    ppermute x12 -> x13, waiting for transfers between devices: 10.5 us -> 9.6 us  [moved(): lax.ppermute(value, 'seq', [(i, i ^ apart) for i in range(lax.axis_size('...]
    ppermute x12 -> x13, starting transfers between devices: 11 us -> 11.5 us  [moved(): lax.ppermute(value, 'seq', [(i, i ^ apart) for i in range(lax.axis_size('...]
  transfers between devices with their start and end apart: 13 -> 14, of which waited for: 8 -> 8; matrix products, arithmetic and copies ran while one was open for 0% -> 0% of each run, Pallas kernels for 28% -> 29%
where the time goes in v5:
time: 38.4 us; the launch traced here: 38.3 us
  Pallas kernels  15.8 us (41%)
  starting transfers between devices  12 us (31%)
  waiting for transfers between devices  10.1 us (26%)
    ppermute x13, starting transfers between devices, moved(): lax.ppermute(value, 'seq', [(i, i ^ apart) for i in range(lax.axis_size('...  11.5 us
    ppermute x13, waiting for transfers between devices, moved(): lax.ppermute(value, 'seq', [(i, i ^ apart) for i in range(lax.axis_size('...  9.6 us
    pallas_call x2, Pallas kernels, near(): pl.pallas_call(functools.partial(near_kernel, first=first, wide=wide, hea...  6.01 us
    pallas_call x3, Pallas kernels, last(): pl.pallas_call(functools.partial(last_kernel, level=level, relatives=rela...  2.85 us
    pallas_call x1, Pallas kernels, front(): pl.pallas_call(functools.partial(front_kernel, early=early), in_specs=[VM...  2.1 us
    pallas_call x1, Pallas kernels, load(): pl.pallas_call(functools.partial(load_kernel, early=early), in_specs=[HBM...  2.09 us
    pallas_call x2, Pallas kernels, middle(): pl.pallas_call(functools.partial(middle_kernel, places=places, relatives=...  1.55 us
  transfers between devices with their start and end apart: 14, of which 8 were waited for; matrix products, arithmetic and copies ran while one was open for 0% of the time, Pallas kernels for 29%

profile of v5, /device:TPU:0, one launch (start us, length us, event | category | flops | bytes accessed | tf_op | source)
XLA Modules:
  0.0 38.3 jit_solution(4624937154065905014)
XLA Ops:
  0.0 2.1 %load.1 = (bf16[512,2304]{1,0:T(8,128)(2,1)S(1)}, f32[4,2304]{1,0:T(4,128)S(1)}, f32[16,512]{1,0:T(8,128)S(1)}, bf16[3,2304]{1,0:T(4,128)(2,1)S(1)}, bf16[2304,5...) custom-call(bf16[512,2304]{1,0:T(8,128)(2,1)} %xbc_hbm.1, ...), custom_call_target="tpu_custom_call" | custom-call | flops 1024 | bytes 1024 | tf_op jit(solution)/shard_map/load/pallas_call | solution.py:174
  2.1 0.5 %collective-permute-start = (bf16[3,2304]{1,0:T(4,128)(2,1)S(1)}, bf16[3,2304]{1,0:T(4,128)(2,1)S(1)}, u32[]{:S(2)}, u32[]{:S(2)}) collective-permute-start(bf16[3,2304]{1,0:T(4,128)(2,1)S(1)} %get-tuple-element.48), channel_id=1, source_target_pairs={{0,1},{1,2},{2,3},{3,4},{4,5},{5,6},{6,0},{7,8},{8,9},{9,10},{10,7... | collective-permute-start | bytes 41480 | tf_op jit(solution)/shard_map/ppermute | solution.py:731
  2.6 2.6 %collective-permute-start.1 = (bf16[3,2304]{1,0:T(4,128)(2,1)S(1)}, bf16[3,2304]{1,0:T(4,128)(2,1)S(1)}, u32[]{:S(2)}, u32[]{:S(2)}) collective-permute-start(bf16[3,2304]{1,0:T(4,128)(2,1)S(1)} %get-tuple-element.48), channel_id=1, source_target_pairs={{0,1},{1,0},{2,3},{3,2},{4,5},{5,4},{6,7},{7,6},{8,9},{9,8},{10,11... | collective-permute-start | bytes 41480 | tf_op jit(solution)/shard_map/ppermute | solution.py:706
  5.2 2.1 %front.1 = (bf16[2304,512]{1,0:T(8,128)(2,1)S(1)}, bf16[128,2304]{1,0:T(8,128)(2,1)S(1)}, f32[2048,128]{1,0:T(8,128)S(1)}) custom-call(bf16[512,2304]{1,0:T(8,128)(2,1)S(1)} %get-tuple-element.51.xbc_ref, f32[4,2304]{1,0:T(4,128)S(1)} %get-tuple-element.50.taps_ref, ...), custom_call_target="tpu_custom_call", output_to_operand_aliasing={{0}: (4, {}), {1}: (5, {}), {2}: (6, {})} | custom-call | tf_op jit(solution)/shard_map/front/pallas_call | solution.py:212
  7.3 0.5 %collective-permute-done.far_edge_ref = bf16[3,2304]{1,0:T(4,128)(2,1)S(1)} collective-permute-done((bf16[3,2304]{1,0:T(4,128)(2,1)S(1)}, bf16[3,2304]{1,0:T(4,128)(2,1)S(1)}, u32[]{:S(2)}, u32[]{:S(2)}) %collective-permute-start) | collective-permute-done | bytes 13856 | tf_op jit(solution)/shard_map/ppermute | solution.py:731
  7.8 0.0 collective-permute-done.1.near_edge_ref
  7.8 0.6 %edge.1 = (bf16[2304,512]{1,0:T(8,128)(2,1)S(1)}, bf16[512,128]{1,0:T(8,128)(2,1)S(1)}, f32[2048,128]{1,0:T(8,128)S(1)}, bf16[1040,128]{1,0:T(8,128)(2,1)S(1)}, bf16[1024,128]{1,0:T(8,128)(2,1)S(1)}) custom-call(bf16[3,2304]{1,0:T(4,128)(2,1)S(1)} %collective-permute-done.far_edge_ref, ...), custom_call_target="tpu_custom_call", output_to_operand_aliasing={{0}: (6, {}), {1}: (7, {}), {2}: (8, {})} | custom-call | flops 1024 | bytes 1024 | tf_op jit(solution)/shard_map/edge/pallas_call | solution.py:277
  8.5 0.0 copy-start
  8.5 0.0 copy-start.1
  8.5 0.1 collective-permute-start.2
  8.6 0.5 %collective-permute-start.4 = (bf16[1024,128]{1,0:T(8,128)(2,1)S(1)}, bf16[1024,128]{1,0:T(8,128)(2,1)S(1)}, u32[]{:S(2)}, u32[]{:S(2)}) collective-permute-start(bf16[1024,128]{1,0:T(8,128)(2,1)S(1)} %get-tuple-element.66), channel_id=1, source_target_pairs={{0,1},{1,0},{2,3},{3,2},{4,5},{5,4},{6,7},{7,6},{8,9},{9,8},{10,11... | collective-permute-start | bytes 786440 | tf_op jit(solution)/shard_map/ppermute | solution.py:706
  9.1 1.0 %collective-permute-done.2.got_ref = bf16[1040,128]{1,0:T(8,128)(2,1)S(1)} collective-permute-done((bf16[1040,128]{1,0:T(8,128)(2,1)S(1)}, bf16[1040,128]{1,0:T(8,128)(2,1)S(1)}, u32[]{:S(2)}, u32[]{:S(2)}) %collective-permute-start.2) | collective-permute-done | bytes 266272 | tf_op jit(solution)/shard_map/ppermute | solution.py:706
  10.1 0.2 pair.1
  10.3 1.1 %collective-permute-start.3 = (bf16[528,128]{1,0:T(8,128)(2,1)S(1)}, bf16[528,128]{1,0:T(8,128)(2,1)S(1)}, u32[]{:S(2)}, u32[]{:S(2)}) collective-permute-start(bf16[528,128]{1,0:T(8,128)(2,1)S(1)} %get-tuple-element.64), channel_id=1, source_target_pairs={{0,2},{1,3},{2,0},{3,1},{4,6},{5,7},{6,4},{7,5},{8,10},{9,11},{10,... | collective-permute-start | bytes 405512 | tf_op jit(solution)/shard_map/ppermute | solution.py:706
  11.4 0.0 collective-permute-done.4
  11.5 0.0 copy-done
  11.5 0.0 copy-done.1
  11.5 3.1 %near.2 = (f32[2048,512]{1,0:T(8,128)S(1)}, f32[512,512]{1,0:T(8,128)S(1)}, f32[3,512,128]{2,1,0:T(8,128)S(1)}, f32[128,128]{1,0:T(8,128)S(1)}) custom-call(bf16[2304,512]{1,0:T(8,128)(2,1)S(1)} %get-tuple-element.59.refs_0_.acts_ref, bf16[512,128]{1,0:T(8,128)(2,1)S(1)} %get-tuple-element.65.refs_1_, ...), custom_call_target="tpu_custom_call" | custom-call | flops 1073741824 | bytes 10485760 | tf_op jit(solution)/shard_map/near/pallas_call | solution.py:544
  14.6 1.4 %collective-permute-done.3.got_ref.refs_5_ = bf16[528,128]{1,0:T(8,128)(2,1)S(1)} collective-permute-done((bf16[528,128]{1,0:T(8,128)(2,1)S(1)}, bf16[528,128]{1,0:T(8,128)(2,1)S(1)}, u32[]{:S(2)}, u32[]{:S(2)}) %collective-permute-start.3) | collective-permute-done | bytes 135200 | tf_op jit(solution)/shard_map/ppermute | solution.py:706
  16.0 0.2 join.2
  16.2 1.5 %collective-permute-start.5 = (bf16[528,128]{1,0:T(8,128)(2,1)S(1)}, bf16[528,128]{1,0:T(8,128)(2,1)S(1)}, u32[]{:S(2)}, u32[]{:S(2)}) collective-permute-start(bf16[528,128]{1,0:T(8,128)(2,1)S(1)} %get-tuple-element.70), channel_id=1, source_target_pairs={{0,4},{1,5},{2,6},{3,7},{4,0},{5,1},{6,2},{7,3},{8,12},{9,13},{10,... | collective-permute-start | bytes 405512 | tf_op jit(solution)/shard_map/ppermute | solution.py:706
  17.7 2.9 %near.3._.refs_8_ = f32[2048,512]{1,0:T(8,128)S(1)} custom-call(bf16[2304,512]{1,0:T(8,128)(2,1)S(1)} %get-tuple-element.59.refs_0_.acts_ref, bf16[512,128]{1,0:T(8,128)(2,1)S(1)} %get-tuple-element.65.refs_1_, f32[16,512]{1,0:T(8,128)S(1)} %get-tuple-element.49.log_ref.refs_2_.refs_1_, f32[224,512]{1,0:T(8,128)S(1)} %bitcast.5, ...), custom_call_target="tpu_custom_call", output_to_operand_aliasing={{}: (8, {})} | custom-call | flops 1073741824 | bytes 10485760 | tf_op jit(solution)/shard_map/near/pallas_call | solution.py:544
  20.6 0.7 %collective-permute-done.5.got_ref.refs_1_.refs_6_ = bf16[528,128]{1,0:T(8,128)(2,1)S(1)} collective-permute-done((bf16[528,128]{1,0:T(8,128)(2,1)S(1)}, bf16[528,128]{1,0:T(8,128)(2,1)S(1)}, u32[]{:S(2)}, u32[]{:S(2)}) %collective-permute-start.5) | collective-permute-done | bytes 135200 | tf_op jit(solution)/shard_map/ppermute | solution.py:706
  21.3 0.2 join.3
  21.5 1.1 %collective-permute-start.7 = (bf16[1024,128]{1,0:T(8,128)(2,1)S(1)}, bf16[1024,128]{1,0:T(8,128)(2,1)S(1)}, u32[]{:S(2)}, u32[]{:S(2)}) collective-permute-start(bf16[1024,128]{1,0:T(8,128)(2,1)S(1)} %get-tuple-element.75), channel_id=1, source_target_pairs={{0,2},{1,3},{2,0},{3,1},{4,6},{5,7},{6,4},{7,5},{8,10},{9,11},{10,... | collective-permute-start | bytes 786440 | tf_op jit(solution)/shard_map/ppermute | solution.py:706
  22.6 2.6 %collective-permute-start.6 = (bf16[512,128]{1,0:T(8,128)(2,1)S(1)}, bf16[512,128]{1,0:T(8,128)(2,1)S(1)}, u32[]{:S(2)}, u32[]{:S(2)}) collective-permute-start(bf16[512,128]{1,0:T(8,128)(2,1)S(1)} %get-tuple-element.74), channel_id=1, source_target_pairs={{0,8},{1,9},{2,10},{3,11},{4,12},{5,13},{6,14},{7,15},{8,0},{9,1},... | collective-permute-start | bytes 393224 | tf_op jit(solution)/shard_map/ppermute | solution.py:706
  25.2 2.9 %collective-permute-done.7.refs_7_ = bf16[1024,128]{1,0:T(8,128)(2,1)S(1)} collective-permute-done((bf16[1024,128]{1,0:T(8,128)(2,1)S(1)}, bf16[1024,128]{1,0:T(8,128)(2,1)S(1)}, u32[]{:S(2)}, u32[]{:S(2)}) %collective-permute-start.7) | collective-permute-done | bytes 262176 | tf_op jit(solution)/shard_map/ppermute | solution.py:706
  28.1 0.8 %middle.2.total_ref.refs_9_ = f32[2048,512]{1,0:T(8,128)S(1)} custom-call(bf16[2304,512]{1,0:T(8,128)(2,1)S(1)} %get-tuple-element.59.refs_0_.acts_ref, f32[16,512]{1,0:T(8,128)S(1)} %get-tuple-element.49.log_ref.refs_2_.refs_1_, f32[224,512]{1,0:T(8,128)S(1)} %bitcast.6, ...), custom_call_target="tpu_custom_call", output_to_operand_aliasing={{}: (8, {})} | custom-call | flops 1024 | bytes 1024 | tf_op jit(solution)/shard_map/middle/pallas_call | solution.py:607
  28.9 1.0 %collective-permute-done.6.node_ref = bf16[512,128]{1,0:T(8,128)(2,1)S(1)} collective-permute-done((bf16[512,128]{1,0:T(8,128)(2,1)S(1)}, bf16[512,128]{1,0:T(8,128)(2,1)S(1)}, u32[]{:S(2)}, u32[]{:S(2)}) %collective-permute-start.6) | collective-permute-done | bytes 131104 | tf_op jit(solution)/shard_map/ppermute | solution.py:706
  29.9 0.9 %collective-permute-start.8 = (bf16[512,128]{1,0:T(8,128)(2,1)S(1)}, bf16[512,128]{1,0:T(8,128)(2,1)S(1)}, u32[]{:S(2)}, u32[]{:S(2)}) collective-permute-start(bf16[512,128]{1,0:T(8,128)(2,1)S(1)} %collective-permute-done.6.node_ref), channel_id=1, source_target_pairs={{0,2},{1,3},{2,0},{3,1},{4,6},{5,7},{6,4},{7,5},{8,10},{9,11},{10,... | collective-permute-start | bytes 393224 | tf_op jit(solution)/shard_map/ppermute | solution.py:706
  30.8 0.5 %last.3.refs_0_ = bf16[1,512,512]{2,1,0:T(8,128)(2,1)S(1)} custom-call(f32[2048,512]{1,0:T(8,128)S(1)} %middle.2.total_ref.refs_9_, bf16[2304,512]{1,0:T(8,128)(2,1)S(1)} %get-tuple-element.59.refs_0_.acts_ref, f32[16,512]{1,0:T(8,128)S(1)} %get-tuple-element.49.log_ref.refs_2_.refs_1_, f32[224,512]{1,0:T(8,128)S(1)} %bitcast.7, ...), custom_call_target="tpu_custom_call" | custom-call | flops 1024 | bytes 1024 | tf_op jit(solution)/shard_map/last/pallas_call | solution.py:690
  31.4 0.1 collective-permute-start.9
  31.5 0.5 %collective-permute-start.10 = (bf16[512,128]{1,0:T(8,128)(2,1)S(1)}, bf16[512,128]{1,0:T(8,128)(2,1)S(1)}, u32[]{:S(2)}, u32[]{:S(2)}) collective-permute-start(bf16[512,128]{1,0:T(8,128)(2,1)S(1)} %slice.22), channel_id=1, source_target_pairs={{0,1},{1,0},{2,3},{3,2},{4,5},{5,4},{6,7},{7,6},{8,9},{9,8},{10,11... | collective-permute-start | bytes 393224 | tf_op jit(solution)/shard_map/ppermute | solution.py:706
  32.0 0.1 collective-permute-start.11
  32.1 0.4 %collective-permute-start.12 = (bf16[512,128]{1,0:T(8,128)(2,1)S(1)}, bf16[512,128]{1,0:T(8,128)(2,1)S(1)}, u32[]{:S(2)}, u32[]{:S(2)}) collective-permute-start(bf16[512,128]{1,0:T(8,128)(2,1)S(1)} %get-tuple-element.83), channel_id=1, source_target_pairs={{0,1},{1,0},{2,3},{3,2},{4,5},{5,4},{6,7},{7,6},{8,9},{9,8},{10,11... | collective-permute-start | bytes 393224 | tf_op jit(solution)/shard_map/ppermute | solution.py:706
  32.5 2.4 %collective-permute-done.8.node_ref = bf16[512,128]{1,0:T(8,128)(2,1)S(1)} collective-permute-done((bf16[512,128]{1,0:T(8,128)(2,1)S(1)}, bf16[512,128]{1,0:T(8,128)(2,1)S(1)}, u32[]{:S(2)}, u32[]{:S(2)}) %collective-permute-start.8) | collective-permute-done | bytes 131104 | tf_op jit(solution)/shard_map/ppermute | solution.py:706
  34.9 0.0 collective-permute-done.9.refs_5_
  34.9 0.0 collective-permute-done.10.refs_6_
  34.9 0.0 collective-permute-done.11.refs_7_
  34.9 0.0 collective-permute-done.12.refs_8_
  34.9 0.1 collective-permute-start.13
  35.0 0.8 %middle.3.total_ref = f32[2048,512]{1,0:T(8,128)S(1)} custom-call(bf16[2304,512]{1,0:T(8,128)(2,1)S(1)} %get-tuple-element.59.refs_0_.acts_ref, f32[16,512]{1,0:T(8,128)S(1)} %get-tuple-element.49.log_ref.refs_2_.refs_1_, f32[224,512]{1,0:T(8,128)S(1)} %bitcast.8, ...), custom_call_target="tpu_custom_call", output_to_operand_aliasing={{}: (9, {})} | custom-call | flops 1024 | bytes 1024 | tf_op jit(solution)/shard_map/middle/pallas_call | solution.py:607
  35.8 0.5 %last.4.refs_1_ = bf16[1,512,512]{2,1,0:T(8,128)(2,1)S(1)} custom-call(f32[2048,512]{1,0:T(8,128)S(1)} %middle.3.total_ref, bf16[2304,512]{1,0:T(8,128)(2,1)S(1)} %get-tuple-element.59.refs_0_.acts_ref, f32[16,512]{1,0:T(8,128)S(1)} %get-tuple-element.49.log_ref.refs_2_.refs_1_, f32[224,512]{1,0:T(8,128)S(1)} %bitcast.9, ...), custom_call_target="tpu_custom_call" | custom-call | flops 1024 | bytes 1024 | tf_op jit(solution)/shard_map/last/pallas_call | solution.py:690
  36.3 0.2 collective-permute-done.13.node_ref
  36.5 1.8 %last.5 = bf16[512,2048]{1,0:T(8,128)(2,1)} custom-call(f32[2048,512]{1,0:T(8,128)S(1)} %middle.3.total_ref, bf16[2304,512]{1,0:T(8,128)(2,1)S(1)} %get-tuple-element.59.refs_0_.acts_ref, f32[16,512]{1,0:T(8,128)S(1)} %get-tuple-element.49.log_ref.refs_2_.refs_1_, f32[224,512]{1,0:T(8,128)S(1)} %bitcast.10, f32[128,128]{1,0:T(8,128)S(1)} %get-tuple-element.78.columns_ref, ...), custom_call_target="tpu_custom_call" | custom-call | flops 1024 | bytes 1024 | tf_op jit(solution)/shard_map/last/pallas_call | solution.py:690
  (6 shorter events, 0.1 us)
Async XLA Ops:
  2.1 5.8 %collective-permute-start = (bf16[3,2304]{1,0:T(4,128)(2,1)S(1)}, bf16[3,2304]{1,0:T(4,128)(2,1)S(1)}, u32[]{:S(2)}, u32[]{:S(2)}) collective-permute-start(bf16[3,2304]{1,0:T(4,128)(2,1)S(1)} %get-tuple-element.48), channel_id=1, source_target_pairs={{0,1},{1,2},{2,3},{3,4},{4,5},{5,6},{6,0},{7,8},{8,9},{9,10},{10,7... | collective-permute-start | bytes 41480 | tf_op jit(solution)/shard_map/ppermute | solution.py:731
  2.6 5.2 %collective-permute-start.1 = (bf16[3,2304]{1,0:T(4,128)(2,1)S(1)}, bf16[3,2304]{1,0:T(4,128)(2,1)S(1)}, u32[]{:S(2)}, u32[]{:S(2)}) collective-permute-start(bf16[3,2304]{1,0:T(4,128)(2,1)S(1)} %get-tuple-element.48), channel_id=1, source_target_pairs={{0,1},{1,0},{2,3},{3,2},{4,5},{5,4},{6,7},{7,6},{8,9},{9,8},{10,11... | collective-permute-start | bytes 41480 | tf_op jit(solution)/shard_map/ppermute | solution.py:706
  8.5 3.0 %copy-start = (f32[16,14,512]{2,0,1:T(8,128)S(1)}, f32[16,14,512]{2,0,1:T(8,128)}, u32[]{:S(2)}) copy-start(f32[16,14,512]{2,0,1:T(8,128)} %param.8) | copy-start | bytes 1376260
  8.5 3.0 %copy-start.1 = (f32[2048]{0:T(1024)S(1)}, f32[2048]{0:T(1024)}, u32[]{:S(2)}) copy-start(f32[2048]{0:T(1024)} %param.9) | copy-start | bytes 24580
  8.5 1.6 %collective-permute-start.2 = (bf16[1040,128]{1,0:T(8,128)(2,1)S(1)}, bf16[1040,128]{1,0:T(8,128)(2,1)S(1)}, u32[]{:S(2)}, u32[]{:S(2)}) collective-permute-start(bf16[1040,128]{1,0:T(8,128)(2,1)S(1)} %get-tuple-element.61), channel_id=1, source_target_pairs={{0,1},{1,0},{2,3},{3,2},{4,5},{5,4},{6,7},{7,6},{8,9},{9,8},{10,11... | collective-permute-start | bytes 798728 | tf_op jit(solution)/shard_map/ppermute | solution.py:706
  8.6 2.9 %collective-permute-start.4 = (bf16[1024,128]{1,0:T(8,128)(2,1)S(1)}, bf16[1024,128]{1,0:T(8,128)(2,1)S(1)}, u32[]{:S(2)}, u32[]{:S(2)}) collective-permute-start(bf16[1024,128]{1,0:T(8,128)(2,1)S(1)} %get-tuple-element.66), channel_id=1, source_target_pairs={{0,1},{1,0},{2,3},{3,2},{4,5},{5,4},{6,7},{7,6},{8,9},{9,8},{10,11... | collective-permute-start | bytes 786440 | tf_op jit(solution)/shard_map/ppermute | solution.py:706
  10.3 5.7 %collective-permute-start.3 = (bf16[528,128]{1,0:T(8,128)(2,1)S(1)}, bf16[528,128]{1,0:T(8,128)(2,1)S(1)}, u32[]{:S(2)}, u32[]{:S(2)}) collective-permute-start(bf16[528,128]{1,0:T(8,128)(2,1)S(1)} %get-tuple-element.64), channel_id=1, source_target_pairs={{0,2},{1,3},{2,0},{3,1},{4,6},{5,7},{6,4},{7,5},{8,10},{9,11},{10,... | collective-permute-start | bytes 405512 | tf_op jit(solution)/shard_map/ppermute | solution.py:706
  16.2 5.1 %collective-permute-start.5 = (bf16[528,128]{1,0:T(8,128)(2,1)S(1)}, bf16[528,128]{1,0:T(8,128)(2,1)S(1)}, u32[]{:S(2)}, u32[]{:S(2)}) collective-permute-start(bf16[528,128]{1,0:T(8,128)(2,1)S(1)} %get-tuple-element.70), channel_id=1, source_target_pairs={{0,4},{1,5},{2,6},{3,7},{4,0},{5,1},{6,2},{7,3},{8,12},{9,13},{10,... | collective-permute-start | bytes 405512 | tf_op jit(solution)/shard_map/ppermute | solution.py:706
  21.5 6.6 %collective-permute-start.7 = (bf16[1024,128]{1,0:T(8,128)(2,1)S(1)}, bf16[1024,128]{1,0:T(8,128)(2,1)S(1)}, u32[]{:S(2)}, u32[]{:S(2)}) collective-permute-start(bf16[1024,128]{1,0:T(8,128)(2,1)S(1)} %get-tuple-element.75), channel_id=1, source_target_pairs={{0,2},{1,3},{2,0},{3,1},{4,6},{5,7},{6,4},{7,5},{8,10},{9,11},{10,... | collective-permute-start | bytes 786440 | tf_op jit(solution)/shard_map/ppermute | solution.py:706
  22.6 7.3 %collective-permute-start.6 = (bf16[512,128]{1,0:T(8,128)(2,1)S(1)}, bf16[512,128]{1,0:T(8,128)(2,1)S(1)}, u32[]{:S(2)}, u32[]{:S(2)}) collective-permute-start(bf16[512,128]{1,0:T(8,128)(2,1)S(1)} %get-tuple-element.74), channel_id=1, source_target_pairs={{0,8},{1,9},{2,10},{3,11},{4,12},{5,13},{6,14},{7,15},{8,0},{9,1},... | collective-permute-start | bytes 393224 | tf_op jit(solution)/shard_map/ppermute | solution.py:706
  29.9 5.0 %collective-permute-start.8 = (bf16[512,128]{1,0:T(8,128)(2,1)S(1)}, bf16[512,128]{1,0:T(8,128)(2,1)S(1)}, u32[]{:S(2)}, u32[]{:S(2)}) collective-permute-start(bf16[512,128]{1,0:T(8,128)(2,1)S(1)} %collective-permute-done.6.node_ref), channel_id=1, source_target_pairs={{0,2},{1,3},{2,0},{3,1},{4,6},{5,7},{6,4},{7,5},{8,10},{9,11},{10,... | collective-permute-start | bytes 393224 | tf_op jit(solution)/shard_map/ppermute | solution.py:706
  31.4 3.5 %collective-permute-start.9 = (bf16[512,128]{1,0:T(8,128)(2,1)S(1)}, bf16[512,128]{1,0:T(8,128)(2,1)S(1)}, u32[]{:S(2)}, u32[]{:S(2)}) collective-permute-start(bf16[512,128]{1,0:T(8,128)(2,1)S(1)} %slice.21), channel_id=1, source_target_pairs={{0,1},{1,0},{2,3},{3,2},{4,5},{5,4},{6,7},{7,6},{8,9},{9,8},{10,11... | collective-permute-start | bytes 393224 | tf_op jit(solution)/shard_map/ppermute | solution.py:706
  31.5 3.4 %collective-permute-start.10 = (bf16[512,128]{1,0:T(8,128)(2,1)S(1)}, bf16[512,128]{1,0:T(8,128)(2,1)S(1)}, u32[]{:S(2)}, u32[]{:S(2)}) collective-permute-start(bf16[512,128]{1,0:T(8,128)(2,1)S(1)} %slice.22), channel_id=1, source_target_pairs={{0,1},{1,0},{2,3},{3,2},{4,5},{5,4},{6,7},{7,6},{8,9},{9,8},{10,11... | collective-permute-start | bytes 393224 | tf_op jit(solution)/shard_map/ppermute | solution.py:706
  32.0 2.9 %collective-permute-start.11 = (bf16[512,128]{1,0:T(8,128)(2,1)S(1)}, bf16[512,128]{1,0:T(8,128)(2,1)S(1)}, u32[]{:S(2)}, u32[]{:S(2)}) collective-permute-start(bf16[512,128]{1,0:T(8,128)(2,1)S(1)} %get-tuple-element.82), channel_id=1, source_target_pairs={{0,1},{1,0},{2,3},{3,2},{4,5},{5,4},{6,7},{7,6},{8,9},{9,8},{10,11... | collective-permute-start | bytes 393224 | tf_op jit(solution)/shard_map/ppermute | solution.py:706
  32.1 2.8 %collective-permute-start.12 = (bf16[512,128]{1,0:T(8,128)(2,1)S(1)}, bf16[512,128]{1,0:T(8,128)(2,1)S(1)}, u32[]{:S(2)}, u32[]{:S(2)}) collective-permute-start(bf16[512,128]{1,0:T(8,128)(2,1)S(1)} %get-tuple-element.83), channel_id=1, source_target_pairs={{0,1},{1,0},{2,3},{3,2},{4,5},{5,4},{6,7},{7,6},{8,9},{9,8},{10,11... | collective-permute-start | bytes 393224 | tf_op jit(solution)/shard_map/ppermute | solution.py:706
  34.9 1.6 %collective-permute-start.13 = (bf16[1024,128]{1,0:T(8,128)(2,1)S(1)}, bf16[1024,128]{1,0:T(8,128)(2,1)S(1)}, u32[]{:S(2)}, u32[]{:S(2)}) collective-permute-start(bf16[1024,128]{1,0:T(8,128)(2,1)S(1)} %pad_maximum_fusion.1), channel_id=1, source_target_pairs={{0,1},{1,0},{2,3},{3,2},{4,5},{5,4},{6,7},{7,6},{8,9},{9,8},{10,11... | collective-permute-start | bytes 786440 | tf_op jit(solution)/shard_map/ppermute | solution.py:706

commit v6 on v5

--- a/solution.py
+++ b/solution.py
@@ -753,21 +753,23 @@
         all_stats.append(stats)
     top = levels - 1
 
-    across = moved(own, 2)
     node = moved(send, 1 << top)
     count = len(got)
+    across = moved(own, 2)
     shared = (acts, log, gains, all_stats[:count])
-    direct = [{0: (slot, 0), 2: (count, slot * part)} for slot in range(count)]
+    direct = [{0: (slot, 0)} for slot in range(count)]
+    crossed = [{2: (0, slot * part)} for slot in range(count)]
     relayed = [{1: (slot, 0), 3: (count + slot, 0)} for slot in range(count)]
-    total = middle(near_made[0], *shared, [*got, across], direct, (0, 2), levels, shards)
+    total = middle(near_made[0], *shared, got, direct, (0,), levels, shards)
     node, total = lax.optimization_barrier((node, total))
     common = (acts, log, gains, near_made[3], all_stats[-1])
     node_across = moved(node, 2)
     own_done = last(total, *common, node, top, levels, (0,), shards, {})
     shares = [kept[:part] for kept in got]
     shares += [across[slot * part : (slot + 1) * part] for slot in range(count)]
-    own_done, shares = lax.optimization_barrier((own_done, shares))
+    own_done, shares, total = lax.optimization_barrier((own_done, shares, total))
     beside = [moved(kept, 1) for kept in shares]
+    total = middle(total, *shared, [across], crossed, (2,), levels, shards)
     node_across, beside, total = lax.optimization_barrier((node_across, beside, total))
     node_beside = moved(jnp.concatenate([node, node_across]), 1)
     total = middle(total, *shared, beside, relayed, (1, 3), levels, shards)

time: 38.4 us -> 38.4 us (level)
    pallas_call x2 -> x3, Pallas kernels: 1.55 us -> 1.66 us  [middle(): pl.pallas_call(functools.partial(middle_kernel, places=places, relatives=...]
  transfers between devices with their start and end apart: 14 -> 14, of which waited for: 8 -> 7; matrix products, arithmetic and copies ran while one was open for 0% -> 0% of each run, Pallas kernels for 29% -> 29%
where the time goes in v6:
time: 38.4 us; the launch traced here: 38.3 us
  Pallas kernels  15.9 us (41%)
  starting transfers between devices  12 us (31%)
  waiting for transfers between devices  9.99 us (26%)
    ppermute x13, starting transfers between devices, moved(): lax.ppermute(value, 'seq', [(i, i ^ apart) for i in range(lax.axis_size('...  11.5 us
    ppermute x13, waiting for transfers between devices, moved(): lax.ppermute(value, 'seq', [(i, i ^ apart) for i in range(lax.axis_size('...  9.47 us
    pallas_call x2, Pallas kernels, near(): pl.pallas_call(functools.partial(near_kernel, first=first, wide=wide, hea...  6.01 us
    pallas_call x3, Pallas kernels, last(): pl.pallas_call(functools.partial(last_kernel, level=level, relatives=rela...  2.84 us
    pallas_call x1, Pallas kernels, front(): pl.pallas_call(functools.partial(front_kernel, early=early), in_specs=[VM...  2.1 us
    pallas_call x1, Pallas kernels, load(): pl.pallas_call(functools.partial(load_kernel, early=early), in_specs=[HBM...  2.09 us
    pallas_call x3, Pallas kernels, middle(): pl.pallas_call(functools.partial(middle_kernel, places=places, relatives=...  1.66 us
  transfers between devices with their start and end apart: 14, of which 7 were waited for; matrix products, arithmetic and copies ran while one was open for 0% of the time, Pallas kernels for 29%

profile of v6, /device:TPU:0, one launch (start us, length us, event | category | flops | bytes accessed | tf_op | source)
XLA Modules:
  0.0 38.3 jit_solution(10787208652803130377)
XLA Ops:
  0.0 2.1 %load.1 = (bf16[512,2304]{1,0:T(8,128)(2,1)S(1)}, f32[4,2304]{1,0:T(4,128)S(1)}, f32[16,512]{1,0:T(8,128)S(1)}, bf16[3,2304]{1,0:T(4,128)(2,1)S(1)}, bf16[2304,5...) custom-call(bf16[512,2304]{1,0:T(8,128)(2,1)} %xbc_hbm.1, ...), custom_call_target="tpu_custom_call" | custom-call | flops 1024 | bytes 1024 | tf_op jit(solution)/shard_map/load/pallas_call | solution.py:174
  2.1 0.5 %collective-permute-start = (bf16[3,2304]{1,0:T(4,128)(2,1)S(1)}, bf16[3,2304]{1,0:T(4,128)(2,1)S(1)}, u32[]{:S(2)}, u32[]{:S(2)}) collective-permute-start(bf16[3,2304]{1,0:T(4,128)(2,1)S(1)} %get-tuple-element.49), channel_id=1, source_target_pairs={{0,1},{1,2},{2,3},{3,4},{4,5},{5,6},{6,0},{7,8},{8,9},{9,10},{10,7... | collective-permute-start | bytes 41480 | tf_op jit(solution)/shard_map/ppermute | solution.py:731
  2.6 2.6 %collective-permute-start.1 = (bf16[3,2304]{1,0:T(4,128)(2,1)S(1)}, bf16[3,2304]{1,0:T(4,128)(2,1)S(1)}, u32[]{:S(2)}, u32[]{:S(2)}) collective-permute-start(bf16[3,2304]{1,0:T(4,128)(2,1)S(1)} %get-tuple-element.49), channel_id=1, source_target_pairs={{0,1},{1,0},{2,3},{3,2},{4,5},{5,4},{6,7},{7,6},{8,9},{9,8},{10,11... | collective-permute-start | bytes 41480 | tf_op jit(solution)/shard_map/ppermute | solution.py:706
  5.2 2.1 %front.1 = (bf16[2304,512]{1,0:T(8,128)(2,1)S(1)}, bf16[128,2304]{1,0:T(8,128)(2,1)S(1)}, f32[2048,128]{1,0:T(8,128)S(1)}) custom-call(bf16[512,2304]{1,0:T(8,128)(2,1)S(1)} %get-tuple-element.52.xbc_ref, f32[4,2304]{1,0:T(4,128)S(1)} %get-tuple-element.51.taps_ref, ...), custom_call_target="tpu_custom_call", output_to_operand_aliasing={{0}: (4, {}), {1}: (5, {}), {2}: (6, {})} | custom-call | tf_op jit(solution)/shard_map/front/pallas_call | solution.py:212
  7.3 0.5 %collective-permute-done.far_edge_ref = bf16[3,2304]{1,0:T(4,128)(2,1)S(1)} collective-permute-done((bf16[3,2304]{1,0:T(4,128)(2,1)S(1)}, bf16[3,2304]{1,0:T(4,128)(2,1)S(1)}, u32[]{:S(2)}, u32[]{:S(2)}) %collective-permute-start) | collective-permute-done | bytes 13856 | tf_op jit(solution)/shard_map/ppermute | solution.py:731
  7.8 0.0 collective-permute-done.1.near_edge_ref
  7.8 0.6 %edge.1 = (bf16[2304,512]{1,0:T(8,128)(2,1)S(1)}, bf16[512,128]{1,0:T(8,128)(2,1)S(1)}, f32[2048,128]{1,0:T(8,128)S(1)}, bf16[1040,128]{1,0:T(8,128)(2,1)S(1)}, bf16[1024,128]{1,0:T(8,128)(2,1)S(1)}) custom-call(bf16[3,2304]{1,0:T(4,128)(2,1)S(1)} %collective-permute-done.far_edge_ref, ...), custom_call_target="tpu_custom_call", output_to_operand_aliasing={{0}: (6, {}), {1}: (7, {}), {2}: (8, {})} | custom-call | flops 1024 | bytes 1024 | tf_op jit(solution)/shard_map/edge/pallas_call | solution.py:277
  8.5 0.0 copy-start
  8.5 0.0 copy-start.1
  8.5 0.1 collective-permute-start.2
  8.6 0.5 %collective-permute-start.4 = (bf16[1024,128]{1,0:T(8,128)(2,1)S(1)}, bf16[1024,128]{1,0:T(8,128)(2,1)S(1)}, u32[]{:S(2)}, u32[]{:S(2)}) collective-permute-start(bf16[1024,128]{1,0:T(8,128)(2,1)S(1)} %get-tuple-element.67), channel_id=1, source_target_pairs={{0,1},{1,0},{2,3},{3,2},{4,5},{5,4},{6,7},{7,6},{8,9},{9,8},{10,11... | collective-permute-start | bytes 786440 | tf_op jit(solution)/shard_map/ppermute | solution.py:706
  9.1 1.0 %collective-permute-done.2.got_ref = bf16[1040,128]{1,0:T(8,128)(2,1)S(1)} collective-permute-done((bf16[1040,128]{1,0:T(8,128)(2,1)S(1)}, bf16[1040,128]{1,0:T(8,128)(2,1)S(1)}, u32[]{:S(2)}, u32[]{:S(2)}) %collective-permute-start.2) | collective-permute-done | bytes 266272 | tf_op jit(solution)/shard_map/ppermute | solution.py:706
  10.1 0.2 pair.1
  10.3 1.1 %collective-permute-start.3 = (bf16[528,128]{1,0:T(8,128)(2,1)S(1)}, bf16[528,128]{1,0:T(8,128)(2,1)S(1)}, u32[]{:S(2)}, u32[]{:S(2)}) collective-permute-start(bf16[528,128]{1,0:T(8,128)(2,1)S(1)} %get-tuple-element.65), channel_id=1, source_target_pairs={{0,2},{1,3},{2,0},{3,1},{4,6},{5,7},{6,4},{7,5},{8,10},{9,11},{10,... | collective-permute-start | bytes 405512 | tf_op jit(solution)/shard_map/ppermute | solution.py:706
  11.4 0.0 collective-permute-done.4
  11.5 0.0 copy-done
  11.5 0.0 copy-done.1
  11.5 3.1 %near.2 = (f32[2048,512]{1,0:T(8,128)S(1)}, f32[512,512]{1,0:T(8,128)S(1)}, f32[3,512,128]{2,1,0:T(8,128)S(1)}, f32[128,128]{1,0:T(8,128)S(1)}) custom-call(bf16[2304,512]{1,0:T(8,128)(2,1)S(1)} %get-tuple-element.60.refs_0_.acts_ref, bf16[512,128]{1,0:T(8,128)(2,1)S(1)} %get-tuple-element.66.refs_1_, ...), custom_call_target="tpu_custom_call" | custom-call | flops 1073741824 | bytes 10485760 | tf_op jit(solution)/shard_map/near/pallas_call | solution.py:544
  14.6 1.4 %collective-permute-done.3.got_ref.refs_5_ = bf16[528,128]{1,0:T(8,128)(2,1)S(1)} collective-permute-done((bf16[528,128]{1,0:T(8,128)(2,1)S(1)}, bf16[528,128]{1,0:T(8,128)(2,1)S(1)}, u32[]{:S(2)}, u32[]{:S(2)}) %collective-permute-start.3) | collective-permute-done | bytes 135200 | tf_op jit(solution)/shard_map/ppermute | solution.py:706
  16.0 0.2 join.2
  16.2 1.5 %collective-permute-start.5 = (bf16[528,128]{1,0:T(8,128)(2,1)S(1)}, bf16[528,128]{1,0:T(8,128)(2,1)S(1)}, u32[]{:S(2)}, u32[]{:S(2)}) collective-permute-start(bf16[528,128]{1,0:T(8,128)(2,1)S(1)} %get-tuple-element.71), channel_id=1, source_target_pairs={{0,4},{1,5},{2,6},{3,7},{4,0},{5,1},{6,2},{7,3},{8,12},{9,13},{10,... | collective-permute-start | bytes 405512 | tf_op jit(solution)/shard_map/ppermute | solution.py:706
  17.7 2.9 %near.3._.refs_7_ = f32[2048,512]{1,0:T(8,128)S(1)} custom-call(bf16[2304,512]{1,0:T(8,128)(2,1)S(1)} %get-tuple-element.60.refs_0_.acts_ref, bf16[512,128]{1,0:T(8,128)(2,1)S(1)} %get-tuple-element.66.refs_1_, f32[16,512]{1,0:T(8,128)S(1)} %get-tuple-element.50.log_ref.refs_2_.refs_1_, f32[224,512]{1,0:T(8,128)S(1)} %bitcast.5, ...), custom_call_target="tpu_custom_call", output_to_operand_aliasing={{}: (8, {})} | custom-call | flops 1073741824 | bytes 10485760 | tf_op jit(solution)/shard_map/near/pallas_call | solution.py:544
  20.6 0.7 %collective-permute-done.5.got_ref.refs_1_.refs_6_ = bf16[528,128]{1,0:T(8,128)(2,1)S(1)} collective-permute-done((bf16[528,128]{1,0:T(8,128)(2,1)S(1)}, bf16[528,128]{1,0:T(8,128)(2,1)S(1)}, u32[]{:S(2)}, u32[]{:S(2)}) %collective-permute-start.5) | collective-permute-done | bytes 135200 | tf_op jit(solution)/shard_map/ppermute | solution.py:706
  21.3 0.2 join.3
  21.5 1.1 %collective-permute-start.8 = (bf16[1024,128]{1,0:T(8,128)(2,1)S(1)}, bf16[1024,128]{1,0:T(8,128)(2,1)S(1)}, u32[]{:S(2)}, u32[]{:S(2)}) collective-permute-start(bf16[1024,128]{1,0:T(8,128)(2,1)S(1)} %get-tuple-element.80), channel_id=1, source_target_pairs={{0,2},{1,3},{2,0},{3,1},{4,6},{5,7},{6,4},{7,5},{8,10},{9,11},{10,... | collective-permute-start | bytes 786440 | tf_op jit(solution)/shard_map/ppermute | solution.py:706
  22.6 2.6 %collective-permute-start.6 = (bf16[512,128]{1,0:T(8,128)(2,1)S(1)}, bf16[512,128]{1,0:T(8,128)(2,1)S(1)}, u32[]{:S(2)}, u32[]{:S(2)}) collective-permute-start(bf16[512,128]{1,0:T(8,128)(2,1)S(1)} %get-tuple-element.75), channel_id=1, source_target_pairs={{0,8},{1,9},{2,10},{3,11},{4,12},{5,13},{6,14},{7,15},{8,0},{9,1},... | collective-permute-start | bytes 393224 | tf_op jit(solution)/shard_map/ppermute | solution.py:706
  25.2 0.4 %middle.3.total_ref.refs_6_ = f32[2048,512]{1,0:T(8,128)S(1)} custom-call(bf16[2304,512]{1,0:T(8,128)(2,1)S(1)} %get-tuple-element.60.refs_0_.acts_ref, f32[16,512]{1,0:T(8,128)S(1)} %get-tuple-element.50.log_ref.refs_2_.refs_1_, f32[224,512]{1,0:T(8,128)S(1)} %bitcast.6, ...), custom_call_target="tpu_custom_call", output_to_operand_aliasing={{}: (7, {})} | custom-call | flops 1024 | bytes 1024 | tf_op jit(solution)/shard_map/middle/pallas_call | solution.py:607
  25.6 4.3 %collective-permute-done.6.node_ref = bf16[512,128]{1,0:T(8,128)(2,1)S(1)} collective-permute-done((bf16[512,128]{1,0:T(8,128)(2,1)S(1)}, bf16[512,128]{1,0:T(8,128)(2,1)S(1)}, u32[]{:S(2)}, u32[]{:S(2)}) %collective-permute-start.6) | collective-permute-done | bytes 131104 | tf_op jit(solution)/shard_map/ppermute | solution.py:706
  29.9 0.9 %collective-permute-start.7 = (bf16[512,128]{1,0:T(8,128)(2,1)S(1)}, bf16[512,128]{1,0:T(8,128)(2,1)S(1)}, u32[]{:S(2)}, u32[]{:S(2)}) collective-permute-start(bf16[512,128]{1,0:T(8,128)(2,1)S(1)} %collective-permute-done.6.node_ref), channel_id=1, source_target_pairs={{0,2},{1,3},{2,0},{3,1},{4,6},{5,7},{6,4},{7,5},{8,10},{9,11},{10,... | collective-permute-start | bytes 393224 | tf_op jit(solution)/shard_map/ppermute | solution.py:706
  30.8 0.5 %last.3.refs_0_ = bf16[1,512,512]{2,1,0:T(8,128)(2,1)S(1)} custom-call(f32[2048,512]{1,0:T(8,128)S(1)} %middle.3.total_ref.refs_6_, bf16[2304,512]{1,0:T(8,128)(2,1)S(1)} %get-tuple-element.60.refs_0_.acts_ref, f32[16,512]{1,0:T(8,128)S(1)} %get-tuple-element.50.log_ref.refs_2_.refs_1_, f32[224,512]{1,0:T(8,128)S(1)} %bitcast.7, ...), custom_call_target="tpu_custom_call" | custom-call | flops 1024 | bytes 1024 | tf_op jit(solution)/shard_map/last/pallas_call | solution.py:690
  31.4 0.0 collective-permute-done.8.refs_5_
  31.4 0.1 collective-permute-start.9
  31.5 0.5 %collective-permute-start.10 = (bf16[512,128]{1,0:T(8,128)(2,1)S(1)}, bf16[512,128]{1,0:T(8,128)(2,1)S(1)}, u32[]{:S(2)}, u32[]{:S(2)}) collective-permute-start(bf16[512,128]{1,0:T(8,128)(2,1)S(1)} %slice.22), channel_id=1, source_target_pairs={{0,1},{1,0},{2,3},{3,2},{4,5},{5,4},{6,7},{7,6},{8,9},{9,8},{10,11... | collective-permute-start | bytes 393224 | tf_op jit(solution)/shard_map/ppermute | solution.py:706
  32.0 0.1 collective-permute-start.11
  32.1 0.4 %collective-permute-start.12 = (bf16[512,128]{1,0:T(8,128)(2,1)S(1)}, bf16[512,128]{1,0:T(8,128)(2,1)S(1)}, u32[]{:S(2)}, u32[]{:S(2)}) collective-permute-start(bf16[512,128]{1,0:T(8,128)(2,1)S(1)} %get-tuple-element.84), channel_id=1, source_target_pairs={{0,1},{1,0},{2,3},{3,2},{4,5},{5,4},{6,7},{7,6},{8,9},{9,8},{10,11... | collective-permute-start | bytes 393224 | tf_op jit(solution)/shard_map/ppermute | solution.py:706
  32.5 0.4 %middle.4.refs_9_ = f32[2048,512]{1,0:T(8,128)S(1)} custom-call(bf16[2304,512]{1,0:T(8,128)(2,1)S(1)} %get-tuple-element.60.refs_0_.acts_ref, f32[16,512]{1,0:T(8,128)S(1)} %get-tuple-element.50.log_ref.refs_2_.refs_1_, f32[224,512]{1,0:T(8,128)S(1)} %bitcast.8, ...), custom_call_target="tpu_custom_call", output_to_operand_aliasing={{}: (6, {})} | custom-call | flops 1024 | bytes 1024 | tf_op jit(solution)/shard_map/middle/pallas_call | solution.py:607
  32.9 1.9 %collective-permute-done.7.node_ref = bf16[512,128]{1,0:T(8,128)(2,1)S(1)} collective-permute-done((bf16[512,128]{1,0:T(8,128)(2,1)S(1)}, bf16[512,128]{1,0:T(8,128)(2,1)S(1)}, u32[]{:S(2)}, u32[]{:S(2)}) %collective-permute-start.7) | collective-permute-done | bytes 131104 | tf_op jit(solution)/shard_map/ppermute | solution.py:706
  34.9 0.0 collective-permute-done.9.refs_5_
  34.9 0.0 collective-permute-done.10.refs_6_
  34.9 0.0 collective-permute-done.11.refs_7_
  34.9 0.0 collective-permute-done.12.refs_8_
  34.9 0.1 collective-permute-start.13
  35.0 0.8 %middle.5.total_ref = f32[2048,512]{1,0:T(8,128)S(1)} custom-call(bf16[2304,512]{1,0:T(8,128)(2,1)S(1)} %get-tuple-element.60.refs_0_.acts_ref, f32[16,512]{1,0:T(8,128)S(1)} %get-tuple-element.50.log_ref.refs_2_.refs_1_, f32[224,512]{1,0:T(8,128)S(1)} %bitcast.9, ...), custom_call_target="tpu_custom_call", output_to_operand_aliasing={{}: (9, {})} | custom-call | flops 1024 | bytes 1024 | tf_op jit(solution)/shard_map/middle/pallas_call | solution.py:607
  35.8 0.5 %last.4.refs_1_ = bf16[1,512,512]{2,1,0:T(8,128)(2,1)S(1)} custom-call(f32[2048,512]{1,0:T(8,128)S(1)} %middle.5.total_ref, bf16[2304,512]{1,0:T(8,128)(2,1)S(1)} %get-tuple-element.60.refs_0_.acts_ref, f32[16,512]{1,0:T(8,128)S(1)} %get-tuple-element.50.log_ref.refs_2_.refs_1_, f32[224,512]{1,0:T(8,128)S(1)} %bitcast.10, ...), custom_call_target="tpu_custom_call" | custom-call | flops 1024 | bytes 1024 | tf_op jit(solution)/shard_map/last/pallas_call | solution.py:690
  36.3 0.2 collective-permute-done.13.node_ref
  36.5 1.8 %last.5 = bf16[512,2048]{1,0:T(8,128)(2,1)} custom-call(f32[2048,512]{1,0:T(8,128)S(1)} %middle.5.total_ref, bf16[2304,512]{1,0:T(8,128)(2,1)S(1)} %get-tuple-element.60.refs_0_.acts_ref, f32[16,512]{1,0:T(8,128)S(1)} %get-tuple-element.50.log_ref.refs_2_.refs_1_, f32[224,512]{1,0:T(8,128)S(1)} %bitcast.11, f32[128,128]{1,0:T(8,128)S(1)} %get-tuple-element.78.columns_ref, ...), custom_call_target="tpu_custom_call" | custom-call | flops 1024 | bytes 1024 | tf_op jit(solution)/shard_map/last/pallas_call | solution.py:690
  (6 shorter events, 0.1 us)
Async XLA Ops:
  2.1 5.8 %collective-permute-start = (bf16[3,2304]{1,0:T(4,128)(2,1)S(1)}, bf16[3,2304]{1,0:T(4,128)(2,1)S(1)}, u32[]{:S(2)}, u32[]{:S(2)}) collective-permute-start(bf16[3,2304]{1,0:T(4,128)(2,1)S(1)} %get-tuple-element.49), channel_id=1, source_target_pairs={{0,1},{1,2},{2,3},{3,4},{4,5},{5,6},{6,0},{7,8},{8,9},{9,10},{10,7... | collective-permute-start | bytes 41480 | tf_op jit(solution)/shard_map/ppermute | solution.py:731
  2.6 5.2 %collective-permute-start.1 = (bf16[3,2304]{1,0:T(4,128)(2,1)S(1)}, bf16[3,2304]{1,0:T(4,128)(2,1)S(1)}, u32[]{:S(2)}, u32[]{:S(2)}) collective-permute-start(bf16[3,2304]{1,0:T(4,128)(2,1)S(1)} %get-tuple-element.49), channel_id=1, source_target_pairs={{0,1},{1,0},{2,3},{3,2},{4,5},{5,4},{6,7},{7,6},{8,9},{9,8},{10,11... | collective-permute-start | bytes 41480 | tf_op jit(solution)/shard_map/ppermute | solution.py:706
  8.5 3.0 %copy-start = (f32[16,14,512]{2,0,1:T(8,128)S(1)}, f32[16,14,512]{2,0,1:T(8,128)}, u32[]{:S(2)}) copy-start(f32[16,14,512]{2,0,1:T(8,128)} %param.8) | copy-start | bytes 1376260
  8.5 3.0 %copy-start.1 = (f32[2048]{0:T(1024)S(1)}, f32[2048]{0:T(1024)}, u32[]{:S(2)}) copy-start(f32[2048]{0:T(1024)} %param.9) | copy-start | bytes 24580
  8.5 1.6 %collective-permute-start.2 = (bf16[1040,128]{1,0:T(8,128)(2,1)S(1)}, bf16[1040,128]{1,0:T(8,128)(2,1)S(1)}, u32[]{:S(2)}, u32[]{:S(2)}) collective-permute-start(bf16[1040,128]{1,0:T(8,128)(2,1)S(1)} %get-tuple-element.62), channel_id=1, source_target_pairs={{0,1},{1,0},{2,3},{3,2},{4,5},{5,4},{6,7},{7,6},{8,9},{9,8},{10,11... | collective-permute-start | bytes 798728 | tf_op jit(solution)/shard_map/ppermute | solution.py:706
  8.6 2.9 %collective-permute-start.4 = (bf16[1024,128]{1,0:T(8,128)(2,1)S(1)}, bf16[1024,128]{1,0:T(8,128)(2,1)S(1)}, u32[]{:S(2)}, u32[]{:S(2)}) collective-permute-start(bf16[1024,128]{1,0:T(8,128)(2,1)S(1)} %get-tuple-element.67), channel_id=1, source_target_pairs={{0,1},{1,0},{2,3},{3,2},{4,5},{5,4},{6,7},{7,6},{8,9},{9,8},{10,11... | collective-permute-start | bytes 786440 | tf_op jit(solution)/shard_map/ppermute | solution.py:706
  10.3 5.7 %collective-permute-start.3 = (bf16[528,128]{1,0:T(8,128)(2,1)S(1)}, bf16[528,128]{1,0:T(8,128)(2,1)S(1)}, u32[]{:S(2)}, u32[]{:S(2)}) collective-permute-start(bf16[528,128]{1,0:T(8,128)(2,1)S(1)} %get-tuple-element.65), channel_id=1, source_target_pairs={{0,2},{1,3},{2,0},{3,1},{4,6},{5,7},{6,4},{7,5},{8,10},{9,11},{10,... | collective-permute-start | bytes 405512 | tf_op jit(solution)/shard_map/ppermute | solution.py:706
  16.2 5.1 %collective-permute-start.5 = (bf16[528,128]{1,0:T(8,128)(2,1)S(1)}, bf16[528,128]{1,0:T(8,128)(2,1)S(1)}, u32[]{:S(2)}, u32[]{:S(2)}) collective-permute-start(bf16[528,128]{1,0:T(8,128)(2,1)S(1)} %get-tuple-element.71), channel_id=1, source_target_pairs={{0,4},{1,5},{2,6},{3,7},{4,0},{5,1},{6,2},{7,3},{8,12},{9,13},{10,... | collective-permute-start | bytes 405512 | tf_op jit(solution)/shard_map/ppermute | solution.py:706
  21.5 9.9 %collective-permute-start.8 = (bf16[1024,128]{1,0:T(8,128)(2,1)S(1)}, bf16[1024,128]{1,0:T(8,128)(2,1)S(1)}, u32[]{:S(2)}, u32[]{:S(2)}) collective-permute-start(bf16[1024,128]{1,0:T(8,128)(2,1)S(1)} %get-tuple-element.80), channel_id=1, source_target_pairs={{0,2},{1,3},{2,0},{3,1},{4,6},{5,7},{6,4},{7,5},{8,10},{9,11},{10,... | collective-permute-start | bytes 786440 | tf_op jit(solution)/shard_map/ppermute | solution.py:706
  22.6 7.3 %collective-permute-start.6 = (bf16[512,128]{1,0:T(8,128)(2,1)S(1)}, bf16[512,128]{1,0:T(8,128)(2,1)S(1)}, u32[]{:S(2)}, u32[]{:S(2)}) collective-permute-start(bf16[512,128]{1,0:T(8,128)(2,1)S(1)} %get-tuple-element.75), channel_id=1, source_target_pairs={{0,8},{1,9},{2,10},{3,11},{4,12},{5,13},{6,14},{7,15},{8,0},{9,1},... | collective-permute-start | bytes 393224 | tf_op jit(solution)/shard_map/ppermute | solution.py:706
  29.9 5.0 %collective-permute-start.7 = (bf16[512,128]{1,0:T(8,128)(2,1)S(1)}, bf16[512,128]{1,0:T(8,128)(2,1)S(1)}, u32[]{:S(2)}, u32[]{:S(2)}) collective-permute-start(bf16[512,128]{1,0:T(8,128)(2,1)S(1)} %collective-permute-done.6.node_ref), channel_id=1, source_target_pairs={{0,2},{1,3},{2,0},{3,1},{4,6},{5,7},{6,4},{7,5},{8,10},{9,11},{10,... | collective-permute-start | bytes 393224 | tf_op jit(solution)/shard_map/ppermute | solution.py:706
  31.4 3.5 %collective-permute-start.9 = (bf16[512,128]{1,0:T(8,128)(2,1)S(1)}, bf16[512,128]{1,0:T(8,128)(2,1)S(1)}, u32[]{:S(2)}, u32[]{:S(2)}) collective-permute-start(bf16[512,128]{1,0:T(8,128)(2,1)S(1)} %slice.21), channel_id=1, source_target_pairs={{0,1},{1,0},{2,3},{3,2},{4,5},{5,4},{6,7},{7,6},{8,9},{9,8},{10,11... | collective-permute-start | bytes 393224 | tf_op jit(solution)/shard_map/ppermute | solution.py:706
  31.5 3.4 %collective-permute-start.10 = (bf16[512,128]{1,0:T(8,128)(2,1)S(1)}, bf16[512,128]{1,0:T(8,128)(2,1)S(1)}, u32[]{:S(2)}, u32[]{:S(2)}) collective-permute-start(bf16[512,128]{1,0:T(8,128)(2,1)S(1)} %slice.22), channel_id=1, source_target_pairs={{0,1},{1,0},{2,3},{3,2},{4,5},{5,4},{6,7},{7,6},{8,9},{9,8},{10,11... | collective-permute-start | bytes 393224 | tf_op jit(solution)/shard_map/ppermute | solution.py:706
  32.0 2.9 %collective-permute-start.11 = (bf16[512,128]{1,0:T(8,128)(2,1)S(1)}, bf16[512,128]{1,0:T(8,128)(2,1)S(1)}, u32[]{:S(2)}, u32[]{:S(2)}) collective-permute-start(bf16[512,128]{1,0:T(8,128)(2,1)S(1)} %get-tuple-element.83), channel_id=1, source_target_pairs={{0,1},{1,0},{2,3},{3,2},{4,5},{5,4},{6,7},{7,6},{8,9},{9,8},{10,11... | collective-permute-start | bytes 393224 | tf_op jit(solution)/shard_map/ppermute | solution.py:706
  32.1 2.8 %collective-permute-start.12 = (bf16[512,128]{1,0:T(8,128)(2,1)S(1)}, bf16[512,128]{1,0:T(8,128)(2,1)S(1)}, u32[]{:S(2)}, u32[]{:S(2)}) collective-permute-start(bf16[512,128]{1,0:T(8,128)(2,1)S(1)} %get-tuple-element.84), channel_id=1, source_target_pairs={{0,1},{1,0},{2,3},{3,2},{4,5},{5,4},{6,7},{7,6},{8,9},{9,8},{10,11... | collective-permute-start | bytes 393224 | tf_op jit(solution)/shard_map/ppermute | solution.py:706
  34.9 1.6 %collective-permute-start.13 = (bf16[1024,128]{1,0:T(8,128)(2,1)S(1)}, bf16[1024,128]{1,0:T(8,128)(2,1)S(1)}, u32[]{:S(2)}, u32[]{:S(2)}) collective-permute-start(bf16[1024,128]{1,0:T(8,128)(2,1)S(1)} %pad_maximum_fusion.1), channel_id=1, source_target_pairs={{0,1},{1,0},{2,3},{3,2},{4,5},{5,4},{6,7},{7,6},{8,9},{9,8},{10,11... | collective-permute-start | bytes 786440 | tf_op jit(solution)/shard_map/ppermute | solution.py:706

commit v7 on v6

--- a/solution.py
+++ b/solution.py
@@ -11,7 +11,7 @@
 BF16 = jnp.bfloat16
 LANES = 128
 GROUP = 8
-PARTS = 4
+PARTS = 3
 VMEM_LIMIT = 24 << 20
 HBM_SPEC = pl.BlockSpec(memory_space=pltpu.HBM)
 VMEM_SPEC = pl.BlockSpec(memory_space=pltpu.VMEM)
@@ -39,21 +39,19 @@
 
 def write_spans(message_ref, first_row, spans):
     head_count = spans.shape[0]
-    place = lax.broadcasted_iota(jnp.int32, spans.shape, 1) // (LANES // PARTS)
-    packed = jnp.zeros(spans.shape, F32)
-    for part in range(PARTS - 1):
-        rounded = spans.astype(BF16).astype(F32)
-        packed = jnp.where(place == part, rounded, packed)
-        spans = spans - rounded
-    message_ref[first_row : first_row + head_count, :] = packed.astype(BF16)
+    for part in range(PARTS):
+        rounded = spans.astype(BF16)
+        start = first_row + part * head_count
+        message_ref[start : start + head_count, :] = rounded
+        spans = spans - rounded.astype(F32)
 
 
 def read_spans(message_ref, first_row, head_count):
-    total = message_ref[first_row : first_row + head_count, :].astype(F32)
-    width = LANES // PARTS
-    while width < LANES:
-        total = total + pltpu.roll(total, width, 1)
-        width *= 2
+    total = None
+    for part in range(PARTS):
+        start = first_row + part * head_count
+        piece = message_ref[start : start + head_count, :].astype(F32)
+        total = piece if total is None else total + piece
     return total
 
 
@@ -282,7 +280,7 @@
             pltpu.VMEM(acts.shape, BF16),
             pltpu.VMEM(maps.shape, BF16),
             pltpu.VMEM(state.shape, F32),
-            pltpu.VMEM((inner // 2 + head_count, state_size), BF16),
+            pltpu.VMEM((inner // 2 + PARTS * head_count, state_size), BF16),
             pltpu.VMEM((inner // 2, state_size), BF16),
         ],
         input_output_aliases={6: 0, 7: 1, 8: 2},
@@ -338,7 +336,7 @@
         out_shape=[
             pltpu.VMEM((part, state_size), F32),
             pltpu.VMEM((4, head_count, LANES), F32),
-            pltpu.VMEM((part + head_count, state_size), BF16),
+            pltpu.VMEM((part + PARTS * head_count, state_size), BF16),
             pltpu.VMEM((part, state_size), BF16),
         ],
         compiler_params=params(),

time: 38.4 us -> 38.4 us (level)
  no operation moved by 1% of the time
where the time goes in v7:
time: 38.4 us; the launch traced here: 38.2 us
  Pallas kernels  15.7 us (41%)
  starting transfers between devices  12.1 us (32%)
  waiting for transfers between devices  10.1 us (26%)
    ppermute x13, starting transfers between devices, moved(): lax.ppermute(value, 'seq', [(i, i ^ apart) for i in range(lax.axis_size('...  11.6 us
    ppermute x13, waiting for transfers between devices, moved(): lax.ppermute(value, 'seq', [(i, i ^ apart) for i in range(lax.axis_size('...  9.59 us
    pallas_call x2, Pallas kernels, near(): pl.pallas_call(functools.partial(near_kernel, first=first, wide=wide, hea...  6.06 us
    pallas_call x3, Pallas kernels, last(): pl.pallas_call(functools.partial(last_kernel, level=level, relatives=rela...  2.84 us
    pallas_call x1, Pallas kernels, front(): pl.pallas_call(functools.partial(front_kernel, early=early), in_specs=[VM...  2.12 us
    pallas_call x1, Pallas kernels, load(): pl.pallas_call(functools.partial(load_kernel, early=early), in_specs=[HBM...  2.09 us
    pallas_call x3, Pallas kernels, middle(): pl.pallas_call(functools.partial(middle_kernel, places=places, relatives=...  1.65 us
  transfers between devices with their start and end apart: 14, of which 7 were waited for; matrix products, arithmetic and copies ran while one was open for 0% of the time, Pallas kernels for 29%

profile of v7, /device:TPU:0, one launch (start us, length us, event | category | flops | bytes accessed | tf_op | source)
XLA Modules:
  0.0 38.2 jit_solution(12116596876030421904)
XLA Ops:
  0.0 2.1 %load.1 = (bf16[512,2304]{1,0:T(8,128)(2,1)S(1)}, f32[4,2304]{1,0:T(4,128)S(1)}, f32[16,512]{1,0:T(8,128)S(1)}, bf16[3,2304]{1,0:T(4,128)(2,1)S(1)}, bf16[2304,5...) custom-call(bf16[512,2304]{1,0:T(8,128)(2,1)} %xbc_hbm.1, ...), custom_call_target="tpu_custom_call" | custom-call | flops 1024 | bytes 1024 | tf_op jit(solution)/shard_map/load/pallas_call | solution.py:172
  2.1 0.5 %collective-permute-start = (bf16[3,2304]{1,0:T(4,128)(2,1)S(1)}, bf16[3,2304]{1,0:T(4,128)(2,1)S(1)}, u32[]{:S(2)}, u32[]{:S(2)}) collective-permute-start(bf16[3,2304]{1,0:T(4,128)(2,1)S(1)} %get-tuple-element.49), channel_id=1, source_target_pairs={{0,1},{1,2},{2,3},{3,4},{4,5},{5,6},{6,0},{7,8},{8,9},{9,10},{10,7... | collective-permute-start | bytes 41480 | tf_op jit(solution)/shard_map/ppermute | solution.py:729
  2.6 2.6 %collective-permute-start.1 = (bf16[3,2304]{1,0:T(4,128)(2,1)S(1)}, bf16[3,2304]{1,0:T(4,128)(2,1)S(1)}, u32[]{:S(2)}, u32[]{:S(2)}) collective-permute-start(bf16[3,2304]{1,0:T(4,128)(2,1)S(1)} %get-tuple-element.49), channel_id=1, source_target_pairs={{0,1},{1,0},{2,3},{3,2},{4,5},{5,4},{6,7},{7,6},{8,9},{9,8},{10,11... | collective-permute-start | bytes 41480 | tf_op jit(solution)/shard_map/ppermute | solution.py:704
  5.2 2.1 %front.1 = (bf16[2304,512]{1,0:T(8,128)(2,1)S(1)}, bf16[128,2304]{1,0:T(8,128)(2,1)S(1)}, f32[2048,128]{1,0:T(8,128)S(1)}) custom-call(bf16[512,2304]{1,0:T(8,128)(2,1)S(1)} %get-tuple-element.52.xbc_ref, f32[4,2304]{1,0:T(4,128)S(1)} %get-tuple-element.51.taps_ref, ...), custom_call_target="tpu_custom_call", output_to_operand_aliasing={{0}: (4, {}), {1}: (5, {}), {2}: (6, {})} | custom-call | tf_op jit(solution)/shard_map/front/pallas_call | solution.py:210
  7.3 0.5 %collective-permute-done.far_edge_ref = bf16[3,2304]{1,0:T(4,128)(2,1)S(1)} collective-permute-done((bf16[3,2304]{1,0:T(4,128)(2,1)S(1)}, bf16[3,2304]{1,0:T(4,128)(2,1)S(1)}, u32[]{:S(2)}, u32[]{:S(2)}) %collective-permute-start) | collective-permute-done | bytes 13856 | tf_op jit(solution)/shard_map/ppermute | solution.py:729
  7.9 0.0 collective-permute-done.1.near_edge_ref
  7.9 0.6 %edge.1 = (bf16[2304,512]{1,0:T(8,128)(2,1)S(1)}, bf16[512,128]{1,0:T(8,128)(2,1)S(1)}, f32[2048,128]{1,0:T(8,128)S(1)}, bf16[1072,128]{1,0:T(8,128)(2,1)S(1)}, bf16[1024,128]{1,0:T(8,128)(2,1)S(1)}) custom-call(bf16[3,2304]{1,0:T(4,128)(2,1)S(1)} %collective-permute-done.far_edge_ref, ...), custom_call_target="tpu_custom_call", output_to_operand_aliasing={{0}: (6, {}), {1}: (7, {}), {2}: (8, {})} | custom-call | flops 1024 | bytes 1024 | tf_op jit(solution)/shard_map/edge/pallas_call | solution.py:275
  8.5 0.0 copy-start
  8.5 0.0 copy-start.1
  8.5 0.1 collective-permute-start.2
  8.6 0.5 %collective-permute-start.4 = (bf16[1024,128]{1,0:T(8,128)(2,1)S(1)}, bf16[1024,128]{1,0:T(8,128)(2,1)S(1)}, u32[]{:S(2)}, u32[]{:S(2)}) collective-permute-start(bf16[1024,128]{1,0:T(8,128)(2,1)S(1)} %get-tuple-element.67), channel_id=1, source_target_pairs={{0,1},{1,0},{2,3},{3,2},{4,5},{5,4},{6,7},{7,6},{8,9},{9,8},{10,11... | collective-permute-start | bytes 786440 | tf_op jit(solution)/shard_map/ppermute | solution.py:704
  9.1 1.0 %collective-permute-done.2.got_ref = bf16[1072,128]{1,0:T(8,128)(2,1)S(1)} collective-permute-done((bf16[1072,128]{1,0:T(8,128)(2,1)S(1)}, bf16[1072,128]{1,0:T(8,128)(2,1)S(1)}, u32[]{:S(2)}, u32[]{:S(2)}) %collective-permute-start.2) | collective-permute-done | bytes 274464 | tf_op jit(solution)/shard_map/ppermute | solution.py:704
  10.1 0.1 pair.1
  10.3 1.1 %collective-permute-start.3 = (bf16[560,128]{1,0:T(8,128)(2,1)S(1)}, bf16[560,128]{1,0:T(8,128)(2,1)S(1)}, u32[]{:S(2)}, u32[]{:S(2)}) collective-permute-start(bf16[560,128]{1,0:T(8,128)(2,1)S(1)} %get-tuple-element.65), channel_id=1, source_target_pairs={{0,2},{1,3},{2,0},{3,1},{4,6},{5,7},{6,4},{7,5},{8,10},{9,11},{10,... | collective-permute-start | bytes 430088 | tf_op jit(solution)/shard_map/ppermute | solution.py:704
  11.4 0.0 collective-permute-done.4
  11.5 0.0 copy-done
  11.5 0.0 copy-done.1
  11.5 3.2 %near.2 = (f32[2048,512]{1,0:T(8,128)S(1)}, f32[512,512]{1,0:T(8,128)S(1)}, f32[3,512,128]{2,1,0:T(8,128)S(1)}, f32[128,128]{1,0:T(8,128)S(1)}) custom-call(bf16[2304,512]{1,0:T(8,128)(2,1)S(1)} %get-tuple-element.60.refs_0_.acts_ref, bf16[512,128]{1,0:T(8,128)(2,1)S(1)} %get-tuple-element.66.refs_1_, ...), custom_call_target="tpu_custom_call" | custom-call | flops 1073741824 | bytes 10485760 | tf_op jit(solution)/shard_map/near/pallas_call | solution.py:542
  14.6 1.5 %collective-permute-done.3.got_ref.refs_5_ = bf16[560,128]{1,0:T(8,128)(2,1)S(1)} collective-permute-done((bf16[560,128]{1,0:T(8,128)(2,1)S(1)}, bf16[560,128]{1,0:T(8,128)(2,1)S(1)}, u32[]{:S(2)}, u32[]{:S(2)}) %collective-permute-start.3) | collective-permute-done | bytes 143392 | tf_op jit(solution)/shard_map/ppermute | solution.py:704
  16.1 0.1 join.2
  16.2 1.5 %collective-permute-start.5 = (bf16[560,128]{1,0:T(8,128)(2,1)S(1)}, bf16[560,128]{1,0:T(8,128)(2,1)S(1)}, u32[]{:S(2)}, u32[]{:S(2)}) collective-permute-start(bf16[560,128]{1,0:T(8,128)(2,1)S(1)} %get-tuple-element.71), channel_id=1, source_target_pairs={{0,4},{1,5},{2,6},{3,7},{4,0},{5,1},{6,2},{7,3},{8,12},{9,13},{10,... | collective-permute-start | bytes 430088 | tf_op jit(solution)/shard_map/ppermute | solution.py:704
  17.7 2.9 %near.3._.refs_7_ = f32[2048,512]{1,0:T(8,128)S(1)} custom-call(bf16[2304,512]{1,0:T(8,128)(2,1)S(1)} %get-tuple-element.60.refs_0_.acts_ref, bf16[512,128]{1,0:T(8,128)(2,1)S(1)} %get-tuple-element.66.refs_1_, f32[16,512]{1,0:T(8,128)S(1)} %get-tuple-element.50.log_ref.refs_2_.refs_1_, f32[224,512]{1,0:T(8,128)S(1)} %bitcast.5, ...), custom_call_target="tpu_custom_call", output_to_operand_aliasing={{}: (8, {})} | custom-call | flops 1073741824 | bytes 10485760 | tf_op jit(solution)/shard_map/near/pallas_call | solution.py:542
  20.6 0.8 %collective-permute-done.5.got_ref.refs_1_.refs_6_ = bf16[560,128]{1,0:T(8,128)(2,1)S(1)} collective-permute-done((bf16[560,128]{1,0:T(8,128)(2,1)S(1)}, bf16[560,128]{1,0:T(8,128)(2,1)S(1)}, u32[]{:S(2)}, u32[]{:S(2)}) %collective-permute-start.5) | collective-permute-done | bytes 143392 | tf_op jit(solution)/shard_map/ppermute | solution.py:704
  21.4 0.1 join.3
  21.4 1.1 %collective-permute-start.8 = (bf16[1024,128]{1,0:T(8,128)(2,1)S(1)}, bf16[1024,128]{1,0:T(8,128)(2,1)S(1)}, u32[]{:S(2)}, u32[]{:S(2)}) collective-permute-start(bf16[1024,128]{1,0:T(8,128)(2,1)S(1)} %get-tuple-element.80), channel_id=1, source_target_pairs={{0,2},{1,3},{2,0},{3,1},{4,6},{5,7},{6,4},{7,5},{8,10},{9,11},{10,... | collective-permute-start | bytes 786440 | tf_op jit(solution)/shard_map/ppermute | solution.py:704
  22.6 2.6 %collective-permute-start.6 = (bf16[512,128]{1,0:T(8,128)(2,1)S(1)}, bf16[512,128]{1,0:T(8,128)(2,1)S(1)}, u32[]{:S(2)}, u32[]{:S(2)}) collective-permute-start(bf16[512,128]{1,0:T(8,128)(2,1)S(1)} %get-tuple-element.75), channel_id=1, source_target_pairs={{0,8},{1,9},{2,10},{3,11},{4,12},{5,13},{6,14},{7,15},{8,0},{9,1},... | collective-permute-start | bytes 393224 | tf_op jit(solution)/shard_map/ppermute | solution.py:704
  25.2 0.4 %middle.3.total_ref.refs_6_ = f32[2048,512]{1,0:T(8,128)S(1)} custom-call(bf16[2304,512]{1,0:T(8,128)(2,1)S(1)} %get-tuple-element.60.refs_0_.acts_ref, f32[16,512]{1,0:T(8,128)S(1)} %get-tuple-element.50.log_ref.refs_2_.refs_1_, f32[224,512]{1,0:T(8,128)S(1)} %bitcast.6, ...), custom_call_target="tpu_custom_call", output_to_operand_aliasing={{}: (7, {})} | custom-call | flops 1024 | bytes 1024 | tf_op jit(solution)/shard_map/middle/pallas_call | solution.py:605
  25.6 4.2 %collective-permute-done.6.node_ref = bf16[512,128]{1,0:T(8,128)(2,1)S(1)} collective-permute-done((bf16[512,128]{1,0:T(8,128)(2,1)S(1)}, bf16[512,128]{1,0:T(8,128)(2,1)S(1)}, u32[]{:S(2)}, u32[]{:S(2)}) %collective-permute-start.6) | collective-permute-done | bytes 131104 | tf_op jit(solution)/shard_map/ppermute | solution.py:704
  29.8 1.0 %collective-permute-start.7 = (bf16[512,128]{1,0:T(8,128)(2,1)S(1)}, bf16[512,128]{1,0:T(8,128)(2,1)S(1)}, u32[]{:S(2)}, u32[]{:S(2)}) collective-permute-start(bf16[512,128]{1,0:T(8,128)(2,1)S(1)} %collective-permute-done.6.node_ref), channel_id=1, source_target_pairs={{0,2},{1,3},{2,0},{3,1},{4,6},{5,7},{6,4},{7,5},{8,10},{9,11},{10,... | collective-permute-start | bytes 393224 | tf_op jit(solution)/shard_map/ppermute | solution.py:704
  30.8 0.5 %last.3.refs_0_ = bf16[1,512,512]{2,1,0:T(8,128)(2,1)S(1)} custom-call(f32[2048,512]{1,0:T(8,128)S(1)} %middle.3.total_ref.refs_6_, bf16[2304,512]{1,0:T(8,128)(2,1)S(1)} %get-tuple-element.60.refs_0_.acts_ref, f32[16,512]{1,0:T(8,128)S(1)} %get-tuple-element.50.log_ref.refs_2_.refs_1_, f32[224,512]{1,0:T(8,128)S(1)} %bitcast.7, ...), custom_call_target="tpu_custom_call" | custom-call | flops 1024 | bytes 1024 | tf_op jit(solution)/shard_map/last/pallas_call | solution.py:688
  31.4 0.0 collective-permute-done.8.refs_5_
  31.4 0.1 collective-permute-start.9
  31.5 0.5 %collective-permute-start.10 = (bf16[512,128]{1,0:T(8,128)(2,1)S(1)}, bf16[512,128]{1,0:T(8,128)(2,1)S(1)}, u32[]{:S(2)}, u32[]{:S(2)}) collective-permute-start(bf16[512,128]{1,0:T(8,128)(2,1)S(1)} %slice.22), channel_id=1, source_target_pairs={{0,1},{1,0},{2,3},{3,2},{4,5},{5,4},{6,7},{7,6},{8,9},{9,8},{10,11... | collective-permute-start | bytes 393224 | tf_op jit(solution)/shard_map/ppermute | solution.py:704
  32.0 0.1 collective-permute-start.11
  32.1 0.4 %collective-permute-start.12 = (bf16[512,128]{1,0:T(8,128)(2,1)S(1)}, bf16[512,128]{1,0:T(8,128)(2,1)S(1)}, u32[]{:S(2)}, u32[]{:S(2)}) collective-permute-start(bf16[512,128]{1,0:T(8,128)(2,1)S(1)} %get-tuple-element.84), channel_id=1, source_target_pairs={{0,1},{1,0},{2,3},{3,2},{4,5},{5,4},{6,7},{7,6},{8,9},{9,8},{10,11... | collective-permute-start | bytes 393224 | tf_op jit(solution)/shard_map/ppermute | solution.py:704
  32.5 0.4 %middle.4.refs_9_ = f32[2048,512]{1,0:T(8,128)S(1)} custom-call(bf16[2304,512]{1,0:T(8,128)(2,1)S(1)} %get-tuple-element.60.refs_0_.acts_ref, f32[16,512]{1,0:T(8,128)S(1)} %get-tuple-element.50.log_ref.refs_2_.refs_1_, f32[224,512]{1,0:T(8,128)S(1)} %bitcast.8, ...), custom_call_target="tpu_custom_call", output_to_operand_aliasing={{}: (6, {})} | custom-call | flops 1024 | bytes 1024 | tf_op jit(solution)/shard_map/middle/pallas_call | solution.py:605
  32.9 1.9 %collective-permute-done.7.node_ref = bf16[512,128]{1,0:T(8,128)(2,1)S(1)} collective-permute-done((bf16[512,128]{1,0:T(8,128)(2,1)S(1)}, bf16[512,128]{1,0:T(8,128)(2,1)S(1)}, u32[]{:S(2)}, u32[]{:S(2)}) %collective-permute-start.7) | collective-permute-done | bytes 131104 | tf_op jit(solution)/shard_map/ppermute | solution.py:704
  34.8 0.0 collective-permute-done.9.refs_5_
  34.8 0.0 collective-permute-done.10.refs_6_
  34.8 0.0 collective-permute-done.11.refs_7_
  34.8 0.0 collective-permute-done.12.refs_8_
  34.9 0.1 collective-permute-start.13
  34.9 0.8 %middle.5.total_ref = f32[2048,512]{1,0:T(8,128)S(1)} custom-call(bf16[2304,512]{1,0:T(8,128)(2,1)S(1)} %get-tuple-element.60.refs_0_.acts_ref, f32[16,512]{1,0:T(8,128)S(1)} %get-tuple-element.50.log_ref.refs_2_.refs_1_, f32[224,512]{1,0:T(8,128)S(1)} %bitcast.9, ...), custom_call_target="tpu_custom_call", output_to_operand_aliasing={{}: (9, {})} | custom-call | flops 1024 | bytes 1024 | tf_op jit(solution)/shard_map/middle/pallas_call | solution.py:605
  35.7 0.5 %last.4.refs_1_ = bf16[1,512,512]{2,1,0:T(8,128)(2,1)S(1)} custom-call(f32[2048,512]{1,0:T(8,128)S(1)} %middle.5.total_ref, bf16[2304,512]{1,0:T(8,128)(2,1)S(1)} %get-tuple-element.60.refs_0_.acts_ref, f32[16,512]{1,0:T(8,128)S(1)} %get-tuple-element.50.log_ref.refs_2_.refs_1_, f32[224,512]{1,0:T(8,128)S(1)} %bitcast.10, ...), custom_call_target="tpu_custom_call" | custom-call | flops 1024 | bytes 1024 | tf_op jit(solution)/shard_map/last/pallas_call | solution.py:688
  36.3 0.2 collective-permute-done.13.node_ref
  36.5 1.8 %last.5 = bf16[512,2048]{1,0:T(8,128)(2,1)} custom-call(f32[2048,512]{1,0:T(8,128)S(1)} %middle.5.total_ref, bf16[2304,512]{1,0:T(8,128)(2,1)S(1)} %get-tuple-element.60.refs_0_.acts_ref, f32[16,512]{1,0:T(8,128)S(1)} %get-tuple-element.50.log_ref.refs_2_.refs_1_, f32[224,512]{1,0:T(8,128)S(1)} %bitcast.11, f32[128,128]{1,0:T(8,128)S(1)} %get-tuple-element.78.columns_ref, ...), custom_call_target="tpu_custom_call" | custom-call | flops 1024 | bytes 1024 | tf_op jit(solution)/shard_map/last/pallas_call | solution.py:688
  (6 shorter events, 0.1 us)
Async XLA Ops:
  2.1 5.8 %collective-permute-start = (bf16[3,2304]{1,0:T(4,128)(2,1)S(1)}, bf16[3,2304]{1,0:T(4,128)(2,1)S(1)}, u32[]{:S(2)}, u32[]{:S(2)}) collective-permute-start(bf16[3,2304]{1,0:T(4,128)(2,1)S(1)} %get-tuple-element.49), channel_id=1, source_target_pairs={{0,1},{1,2},{2,3},{3,4},{4,5},{5,6},{6,0},{7,8},{8,9},{9,10},{10,7... | collective-permute-start | bytes 41480 | tf_op jit(solution)/shard_map/ppermute | solution.py:729
  2.6 5.2 %collective-permute-start.1 = (bf16[3,2304]{1,0:T(4,128)(2,1)S(1)}, bf16[3,2304]{1,0:T(4,128)(2,1)S(1)}, u32[]{:S(2)}, u32[]{:S(2)}) collective-permute-start(bf16[3,2304]{1,0:T(4,128)(2,1)S(1)} %get-tuple-element.49), channel_id=1, source_target_pairs={{0,1},{1,0},{2,3},{3,2},{4,5},{5,4},{6,7},{7,6},{8,9},{9,8},{10,11... | collective-permute-start | bytes 41480 | tf_op jit(solution)/shard_map/ppermute | solution.py:704
  8.5 3.0 %copy-start = (f32[16,14,512]{2,0,1:T(8,128)S(1)}, f32[16,14,512]{2,0,1:T(8,128)}, u32[]{:S(2)}) copy-start(f32[16,14,512]{2,0,1:T(8,128)} %param.8) | copy-start | bytes 1376260
  8.5 3.0 %copy-start.1 = (f32[2048]{0:T(1024)S(1)}, f32[2048]{0:T(1024)}, u32[]{:S(2)}) copy-start(f32[2048]{0:T(1024)} %param.9) | copy-start | bytes 24580
  8.5 1.6 %collective-permute-start.2 = (bf16[1072,128]{1,0:T(8,128)(2,1)S(1)}, bf16[1072,128]{1,0:T(8,128)(2,1)S(1)}, u32[]{:S(2)}, u32[]{:S(2)}) collective-permute-start(bf16[1072,128]{1,0:T(8,128)(2,1)S(1)} %get-tuple-element.62), channel_id=1, source_target_pairs={{0,1},{1,0},{2,3},{3,2},{4,5},{5,4},{6,7},{7,6},{8,9},{9,8},{10,11... | collective-permute-start | bytes 823304 | tf_op jit(solution)/shard_map/ppermute | solution.py:704
  8.6 2.8 %collective-permute-start.4 = (bf16[1024,128]{1,0:T(8,128)(2,1)S(1)}, bf16[1024,128]{1,0:T(8,128)(2,1)S(1)}, u32[]{:S(2)}, u32[]{:S(2)}) collective-permute-start(bf16[1024,128]{1,0:T(8,128)(2,1)S(1)} %get-tuple-element.67), channel_id=1, source_target_pairs={{0,1},{1,0},{2,3},{3,2},{4,5},{5,4},{6,7},{7,6},{8,9},{9,8},{10,11... | collective-permute-start | bytes 786440 | tf_op jit(solution)/shard_map/ppermute | solution.py:704
  10.3 5.9 %collective-permute-start.3 = (bf16[560,128]{1,0:T(8,128)(2,1)S(1)}, bf16[560,128]{1,0:T(8,128)(2,1)S(1)}, u32[]{:S(2)}, u32[]{:S(2)}) collective-permute-start(bf16[560,128]{1,0:T(8,128)(2,1)S(1)} %get-tuple-element.65), channel_id=1, source_target_pairs={{0,2},{1,3},{2,0},{3,1},{4,6},{5,7},{6,4},{7,5},{8,10},{9,11},{10,... | collective-permute-start | bytes 430088 | tf_op jit(solution)/shard_map/ppermute | solution.py:704
  16.2 5.2 %collective-permute-start.5 = (bf16[560,128]{1,0:T(8,128)(2,1)S(1)}, bf16[560,128]{1,0:T(8,128)(2,1)S(1)}, u32[]{:S(2)}, u32[]{:S(2)}) collective-permute-start(bf16[560,128]{1,0:T(8,128)(2,1)S(1)} %get-tuple-element.71), channel_id=1, source_target_pairs={{0,4},{1,5},{2,6},{3,7},{4,0},{5,1},{6,2},{7,3},{8,12},{9,13},{10,... | collective-permute-start | bytes 430088 | tf_op jit(solution)/shard_map/ppermute | solution.py:704
  21.4 9.9 %collective-permute-start.8 = (bf16[1024,128]{1,0:T(8,128)(2,1)S(1)}, bf16[1024,128]{1,0:T(8,128)(2,1)S(1)}, u32[]{:S(2)}, u32[]{:S(2)}) collective-permute-start(bf16[1024,128]{1,0:T(8,128)(2,1)S(1)} %get-tuple-element.80), channel_id=1, source_target_pairs={{0,2},{1,3},{2,0},{3,1},{4,6},{5,7},{6,4},{7,5},{8,10},{9,11},{10,... | collective-permute-start | bytes 786440 | tf_op jit(solution)/shard_map/ppermute | solution.py:704
  22.6 7.3 %collective-permute-start.6 = (bf16[512,128]{1,0:T(8,128)(2,1)S(1)}, bf16[512,128]{1,0:T(8,128)(2,1)S(1)}, u32[]{:S(2)}, u32[]{:S(2)}) collective-permute-start(bf16[512,128]{1,0:T(8,128)(2,1)S(1)} %get-tuple-element.75), channel_id=1, source_target_pairs={{0,8},{1,9},{2,10},{3,11},{4,12},{5,13},{6,14},{7,15},{8,0},{9,1},... | collective-permute-start | bytes 393224 | tf_op jit(solution)/shard_map/ppermute | solution.py:704
  29.8 5.0 %collective-permute-start.7 = (bf16[512,128]{1,0:T(8,128)(2,1)S(1)}, bf16[512,128]{1,0:T(8,128)(2,1)S(1)}, u32[]{:S(2)}, u32[]{:S(2)}) collective-permute-start(bf16[512,128]{1,0:T(8,128)(2,1)S(1)} %collective-permute-done.6.node_ref), channel_id=1, source_target_pairs={{0,2},{1,3},{2,0},{3,1},{4,6},{5,7},{6,4},{7,5},{8,10},{9,11},{10,... | collective-permute-start | bytes 393224 | tf_op jit(solution)/shard_map/ppermute | solution.py:704
  31.4 3.4 %collective-permute-start.9 = (bf16[512,128]{1,0:T(8,128)(2,1)S(1)}, bf16[512,128]{1,0:T(8,128)(2,1)S(1)}, u32[]{:S(2)}, u32[]{:S(2)}) collective-permute-start(bf16[512,128]{1,0:T(8,128)(2,1)S(1)} %slice.21), channel_id=1, source_target_pairs={{0,1},{1,0},{2,3},{3,2},{4,5},{5,4},{6,7},{7,6},{8,9},{9,8},{10,11... | collective-permute-start | bytes 393224 | tf_op jit(solution)/shard_map/ppermute | solution.py:704
  31.5 3.3 %collective-permute-start.10 = (bf16[512,128]{1,0:T(8,128)(2,1)S(1)}, bf16[512,128]{1,0:T(8,128)(2,1)S(1)}, u32[]{:S(2)}, u32[]{:S(2)}) collective-permute-start(bf16[512,128]{1,0:T(8,128)(2,1)S(1)} %slice.22), channel_id=1, source_target_pairs={{0,1},{1,0},{2,3},{3,2},{4,5},{5,4},{6,7},{7,6},{8,9},{9,8},{10,11... | collective-permute-start | bytes 393224 | tf_op jit(solution)/shard_map/ppermute | solution.py:704
  32.0 2.9 %collective-permute-start.11 = (bf16[512,128]{1,0:T(8,128)(2,1)S(1)}, bf16[512,128]{1,0:T(8,128)(2,1)S(1)}, u32[]{:S(2)}, u32[]{:S(2)}) collective-permute-start(bf16[512,128]{1,0:T(8,128)(2,1)S(1)} %get-tuple-element.83), channel_id=1, source_target_pairs={{0,1},{1,0},{2,3},{3,2},{4,5},{5,4},{6,7},{7,6},{8,9},{9,8},{10,11... | collective-permute-start | bytes 393224 | tf_op jit(solution)/shard_map/ppermute | solution.py:704
  32.1 2.8 %collective-permute-start.12 = (bf16[512,128]{1,0:T(8,128)(2,1)S(1)}, bf16[512,128]{1,0:T(8,128)(2,1)S(1)}, u32[]{:S(2)}, u32[]{:S(2)}) collective-permute-start(bf16[512,128]{1,0:T(8,128)(2,1)S(1)} %get-tuple-element.84), channel_id=1, source_target_pairs={{0,1},{1,0},{2,3},{3,2},{4,5},{5,4},{6,7},{7,6},{8,9},{9,8},{10,11... | collective-permute-start | bytes 393224 | tf_op jit(solution)/shard_map/ppermute | solution.py:704
  34.9 1.6 %collective-permute-start.13 = (bf16[1024,128]{1,0:T(8,128)(2,1)S(1)}, bf16[1024,128]{1,0:T(8,128)(2,1)S(1)}, u32[]{:S(2)}, u32[]{:S(2)}) collective-permute-start(bf16[1024,128]{1,0:T(8,128)(2,1)S(1)} %pad_maximum_fusion.1), channel_id=1, source_target_pairs={{0,1},{1,0},{2,3},{3,2},{4,5},{5,4},{6,7},{7,6},{8,9},{9,8},{10,11... | collective-permute-start | bytes 786440 | tf_op jit(solution)/shard_map/ppermute | solution.py:704

commit v8 on v7

--- a/solution.py
+++ b/solution.py
@@ -618,7 +618,7 @@
 
 def last_kernel(
     total_ref, acts_ref, log_ref, gains_ref, columns_ref, stats_ref, node_ref, *refs,
-    level, relatives, done, shards, base
+    level, relatives, done, sends, shards, base
 ):
     head_count, rows = log_ref.shape
     share = head_count // shards
@@ -628,7 +628,7 @@
     shard = lax.axis_index("seq") % shards
     queries = acts_ref[inner + state_size :, :]
     copies = []
-    if done:
+    if sends:
         out_hbm, mixed_ref, sems = refs[-3:]
 
     def send(source_ref, place, relative, first, count):
@@ -642,10 +642,9 @@
         )
         copies[-1].start()
 
-    if done:
-        for relative, source_ref in zip(done, refs):
-            send(source_ref, 0, relative, 0, rows)
-    else:
+    for relative, source_ref in zip(done, refs):
+        send(source_ref, 0, relative, 0, rows)
+    if not sends:
         (mixed_ref,) = refs
     for place, relative in enumerate(relatives):
         term = far_product(node_ref, place * part, part, queries)
@@ -672,32 +671,43 @@
                 scale = lax.rsqrt(mean + 1e-05)
                 mixed = (total * scale * gain_columns[local]).astype(BF16).T
                 mixed_ref[place, span, local * LANES : (local + 1) * LANES] = mixed
-            if done:
+            if sends:
                 send(mixed_ref, place, relative, first, LANES)
     for copy in copies:
         copy.wait()
 
 
-def last(total, acts, log, gains, columns, stats, node, level, levels, relatives, shards, done):
+def last(
+    total, acts, log, gains, columns, stats, node, level, levels, relatives, shards,
+    done=None, whole=None, sends=True
+):
     head_count, rows = log.shape
     share = head_count // shards
-    operands = [total, acts, log, gains, columns, stats, node, *done.values()]
+    done = done or {}
+    operands = in_vmem(total, acts, log, gains, columns, stats, node, *done.values())
+    specs = [VMEM_SPEC] * len(operands)
+    aliases = {}
+    if whole is not None:
+        aliases = {len(operands): 0}
+        operands += in_hbm(whole)
+        specs.append(HBM_SPEC)
     mixed = pltpu.VMEM((len(relatives), rows, share * LANES), BF16)
     copies = len(done) + len(relatives) * rows // LANES
-    whole = jax.ShapeDtypeStruct((rows, head_count * LANES), BF16)
+    out = jax.ShapeDtypeStruct((rows, head_count * LANES), BF16)
     return pl.pallas_call(
         functools.partial(
-            last_kernel, level=level, relatives=relatives, done=tuple(done), shards=shards,
-            base=gains.shape[0] // head_count - levels,
+            last_kernel, level=level, relatives=relatives, done=tuple(done), sends=sends,
+            shards=shards, base=gains.shape[0] // head_count - levels,
         ),
-        in_specs=[VMEM_SPEC] * len(operands),
-        out_specs=HBM_SPEC if done else VMEM_SPEC,
-        out_shape=whole if done else mixed,
-        scratch_shapes=[mixed, pltpu.SemaphoreType.DMA((copies,))] if done else [],
+        in_specs=specs,
+        out_specs=HBM_SPEC if sends else VMEM_SPEC,
+        out_shape=out if sends else mixed,
+        input_output_aliases=aliases,
+        scratch_shapes=[mixed, pltpu.SemaphoreType.DMA((copies,))] if sends else [],
         compiler_params=params(),
         cost_estimate=small_cost(),
         name="last",
-    )(*in_vmem(*operands))
+    )(*operands)
 
 
 def moved(value, apart):
@@ -762,18 +772,17 @@
     node, total = lax.optimization_barrier((node, total))
     common = (acts, log, gains, near_made[3], all_stats[-1])
     node_across = moved(node, 2)
-    own_done = last(total, *common, node, top, levels, (0,), shards, {})
+    mixed = last(total, *common, node, top, levels, (0,), shards)
     shares = [kept[:part] for kept in got]
     shares += [across[slot * part : (slot + 1) * part] for slot in range(count)]
-    own_done, shares, total = lax.optimization_barrier((own_done, shares, total))
+    mixed, shares, total = lax.optimization_barrier((mixed, shares, total))
     beside = [moved(kept, 1) for kept in shares]
     total = middle(total, *shared, [across], crossed, (2,), levels, shards)
     node_across, beside, total = lax.optimization_barrier((node_across, beside, total))
     node_beside = moved(jnp.concatenate([node, node_across]), 1)
     total = middle(total, *shared, beside, relayed, (1, 3), levels, shards)
-    across_done = last(total, *common, node_across, top, levels, (2,), shards, {})
-    done = {0: own_done, 2: across_done}
-    return last(total, *common, node_beside, top, levels, (1, 3), shards, done)
+    done = {2: last(total, *common, node_across, top, levels, (2,), shards, sends=False)}
+    return last(total, *common, node_beside, top, levels, (1, 3), shards, done, mixed)
 
 
 def solution(mesh):

time: 38.4 us -> 38.4 us (level)
  waiting for transfers between devices: 10.1 us -> 9.33 us
  Pallas kernels: 15.7 us -> 16.4 us
    ppermute x13, waiting for transfers between devices: 9.59 us -> 8.82 us  [moved(): lax.ppermute(value, 'seq', [(i, i ^ apart) for i in range(lax.axis_size('...]
    pallas_call x3, Pallas kernels: 2.84 us -> 3.6 us  [last(): pl.pallas_call(functools.partial(last_kernel, level=level, relatives=rela...]
  transfers between devices with their start and end apart: 14 -> 14, of which waited for: 7 -> 7; matrix products, arithmetic and copies ran while one was open for 0% -> 0% of each run, Pallas kernels for 29% -> 31%
where the time goes in v8:
time: 38.4 us; the launch traced here: 38.2 us
  Pallas kernels  16.4 us (43%)
  starting transfers between devices  12.1 us (32%)
  waiting for transfers between devices  9.33 us (24%)
    ppermute x13, starting transfers between devices, moved(): lax.ppermute(value, 'seq', [(i, i ^ apart) for i in range(lax.axis_size('...  11.6 us
    ppermute x13, waiting for transfers between devices, moved(): lax.ppermute(value, 'seq', [(i, i ^ apart) for i in range(lax.axis_size('...  8.82 us
    pallas_call x2, Pallas kernels, near(): pl.pallas_call(functools.partial(near_kernel, first=first, wide=wide, hea...  6.06 us
    pallas_call x3, Pallas kernels, last(): pl.pallas_call(functools.partial(last_kernel, level=level, relatives=rela...  3.6 us
    pallas_call x1, Pallas kernels, front(): pl.pallas_call(functools.partial(front_kernel, early=early), in_specs=[VM...  2.12 us
    pallas_call x1, Pallas kernels, load(): pl.pallas_call(functools.partial(load_kernel, early=early), in_specs=[HBM...  2.09 us
    pallas_call x3, Pallas kernels, middle(): pl.pallas_call(functools.partial(middle_kernel, places=places, relatives=...  1.65 us
  transfers between devices with their start and end apart: 14, of which 7 were waited for; matrix products, arithmetic and copies ran while one was open for 0% of the time, Pallas kernels for 31%

profile of v8, /device:TPU:0, one launch (start us, length us, event | category | flops | bytes accessed | tf_op | source)
XLA Modules:
  0.0 38.2 jit_solution(2165526647760817431)
XLA Ops:
  0.0 2.1 %load.1 = (bf16[512,2304]{1,0:T(8,128)(2,1)S(1)}, f32[4,2304]{1,0:T(4,128)S(1)}, f32[16,512]{1,0:T(8,128)S(1)}, bf16[3,2304]{1,0:T(4,128)(2,1)S(1)}, bf16[2304,5...) custom-call(bf16[512,2304]{1,0:T(8,128)(2,1)} %xbc_hbm.1, ...), custom_call_target="tpu_custom_call" | custom-call | flops 1024 | bytes 1024 | tf_op jit(solution)/shard_map/load/pallas_call | solution.py:172
  2.1 0.5 %collective-permute-start = (bf16[3,2304]{1,0:T(4,128)(2,1)S(1)}, bf16[3,2304]{1,0:T(4,128)(2,1)S(1)}, u32[]{:S(2)}, u32[]{:S(2)}) collective-permute-start(bf16[3,2304]{1,0:T(4,128)(2,1)S(1)} %get-tuple-element.49), channel_id=1, source_target_pairs={{0,1},{1,2},{2,3},{3,4},{4,5},{5,6},{6,0},{7,8},{8,9},{9,10},{10,7... | collective-permute-start | bytes 41480 | tf_op jit(solution)/shard_map/ppermute | solution.py:739
  2.6 2.6 %collective-permute-start.1 = (bf16[3,2304]{1,0:T(4,128)(2,1)S(1)}, bf16[3,2304]{1,0:T(4,128)(2,1)S(1)}, u32[]{:S(2)}, u32[]{:S(2)}) collective-permute-start(bf16[3,2304]{1,0:T(4,128)(2,1)S(1)} %get-tuple-element.49), channel_id=1, source_target_pairs={{0,1},{1,0},{2,3},{3,2},{4,5},{5,4},{6,7},{7,6},{8,9},{9,8},{10,11... | collective-permute-start | bytes 41480 | tf_op jit(solution)/shard_map/ppermute | solution.py:714
  5.2 2.1 %front.1 = (bf16[2304,512]{1,0:T(8,128)(2,1)S(1)}, bf16[128,2304]{1,0:T(8,128)(2,1)S(1)}, f32[2048,128]{1,0:T(8,128)S(1)}) custom-call(bf16[512,2304]{1,0:T(8,128)(2,1)S(1)} %get-tuple-element.52.xbc_ref, f32[4,2304]{1,0:T(4,128)S(1)} %get-tuple-element.51.taps_ref, ...), custom_call_target="tpu_custom_call", output_to_operand_aliasing={{0}: (4, {}), {1}: (5, {}), {2}: (6, {})} | custom-call | tf_op jit(solution)/shard_map/front/pallas_call | solution.py:210
  7.3 0.5 %collective-permute-done.far_edge_ref = bf16[3,2304]{1,0:T(4,128)(2,1)S(1)} collective-permute-done((bf16[3,2304]{1,0:T(4,128)(2,1)S(1)}, bf16[3,2304]{1,0:T(4,128)(2,1)S(1)}, u32[]{:S(2)}, u32[]{:S(2)}) %collective-permute-start) | collective-permute-done | bytes 13856 | tf_op jit(solution)/shard_map/ppermute | solution.py:739
  7.9 0.0 collective-permute-done.1.near_edge_ref
  7.9 0.6 %edge.1 = (bf16[2304,512]{1,0:T(8,128)(2,1)S(1)}, bf16[512,128]{1,0:T(8,128)(2,1)S(1)}, f32[2048,128]{1,0:T(8,128)S(1)}, bf16[1072,128]{1,0:T(8,128)(2,1)S(1)}, bf16[1024,128]{1,0:T(8,128)(2,1)S(1)}) custom-call(bf16[3,2304]{1,0:T(4,128)(2,1)S(1)} %collective-permute-done.far_edge_ref, ...), custom_call_target="tpu_custom_call", output_to_operand_aliasing={{0}: (6, {}), {1}: (7, {}), {2}: (8, {})} | custom-call | flops 1024 | bytes 1024 | tf_op jit(solution)/shard_map/edge/pallas_call | solution.py:275
  8.5 0.0 copy-start
  8.5 0.0 copy-start.1
  8.5 0.1 collective-permute-start.2
  8.6 0.5 %collective-permute-start.4 = (bf16[1024,128]{1,0:T(8,128)(2,1)S(1)}, bf16[1024,128]{1,0:T(8,128)(2,1)S(1)}, u32[]{:S(2)}, u32[]{:S(2)}) collective-permute-start(bf16[1024,128]{1,0:T(8,128)(2,1)S(1)} %get-tuple-element.67), channel_id=1, source_target_pairs={{0,1},{1,0},{2,3},{3,2},{4,5},{5,4},{6,7},{7,6},{8,9},{9,8},{10,11... | collective-permute-start | bytes 786440 | tf_op jit(solution)/shard_map/ppermute | solution.py:714
  9.1 1.0 %collective-permute-done.2.got_ref = bf16[1072,128]{1,0:T(8,128)(2,1)S(1)} collective-permute-done((bf16[1072,128]{1,0:T(8,128)(2,1)S(1)}, bf16[1072,128]{1,0:T(8,128)(2,1)S(1)}, u32[]{:S(2)}, u32[]{:S(2)}) %collective-permute-start.2) | collective-permute-done | bytes 274464 | tf_op jit(solution)/shard_map/ppermute | solution.py:714
  10.1 0.1 pair.1
  10.3 1.1 %collective-permute-start.3 = (bf16[560,128]{1,0:T(8,128)(2,1)S(1)}, bf16[560,128]{1,0:T(8,128)(2,1)S(1)}, u32[]{:S(2)}, u32[]{:S(2)}) collective-permute-start(bf16[560,128]{1,0:T(8,128)(2,1)S(1)} %get-tuple-element.65), channel_id=1, source_target_pairs={{0,2},{1,3},{2,0},{3,1},{4,6},{5,7},{6,4},{7,5},{8,10},{9,11},{10,... | collective-permute-start | bytes 430088 | tf_op jit(solution)/shard_map/ppermute | solution.py:714
  11.4 0.0 collective-permute-done.4
  11.5 0.0 copy-done
  11.5 0.0 copy-done.1
  11.5 3.2 %near.2 = (f32[2048,512]{1,0:T(8,128)S(1)}, f32[512,512]{1,0:T(8,128)S(1)}, f32[3,512,128]{2,1,0:T(8,128)S(1)}, f32[128,128]{1,0:T(8,128)S(1)}) custom-call(bf16[2304,512]{1,0:T(8,128)(2,1)S(1)} %get-tuple-element.60.refs_0_.acts_ref, bf16[512,128]{1,0:T(8,128)(2,1)S(1)} %get-tuple-element.66.refs_1_, ...), custom_call_target="tpu_custom_call" | custom-call | flops 1073741824 | bytes 10485760 | tf_op jit(solution)/shard_map/near/pallas_call | solution.py:542
  14.6 1.5 %collective-permute-done.3.got_ref.refs_5_ = bf16[560,128]{1,0:T(8,128)(2,1)S(1)} collective-permute-done((bf16[560,128]{1,0:T(8,128)(2,1)S(1)}, bf16[560,128]{1,0:T(8,128)(2,1)S(1)}, u32[]{:S(2)}, u32[]{:S(2)}) %collective-permute-start.3) | collective-permute-done | bytes 143392 | tf_op jit(solution)/shard_map/ppermute | solution.py:714
  16.1 0.1 join.2
  16.2 1.5 %collective-permute-start.5 = (bf16[560,128]{1,0:T(8,128)(2,1)S(1)}, bf16[560,128]{1,0:T(8,128)(2,1)S(1)}, u32[]{:S(2)}, u32[]{:S(2)}) collective-permute-start(bf16[560,128]{1,0:T(8,128)(2,1)S(1)} %get-tuple-element.71), channel_id=1, source_target_pairs={{0,4},{1,5},{2,6},{3,7},{4,0},{5,1},{6,2},{7,3},{8,12},{9,13},{10,... | collective-permute-start | bytes 430088 | tf_op jit(solution)/shard_map/ppermute | solution.py:714
  17.7 2.9 %near.3._.refs_7_ = f32[2048,512]{1,0:T(8,128)S(1)} custom-call(bf16[2304,512]{1,0:T(8,128)(2,1)S(1)} %get-tuple-element.60.refs_0_.acts_ref, bf16[512,128]{1,0:T(8,128)(2,1)S(1)} %get-tuple-element.66.refs_1_, f32[16,512]{1,0:T(8,128)S(1)} %get-tuple-element.50.log_ref.refs_2_.refs_1_, f32[224,512]{1,0:T(8,128)S(1)} %bitcast.5, ...), custom_call_target="tpu_custom_call", output_to_operand_aliasing={{}: (8, {})} | custom-call | flops 1073741824 | bytes 10485760 | tf_op jit(solution)/shard_map/near/pallas_call | solution.py:542
  20.6 0.8 %collective-permute-done.5.got_ref.refs_1_.refs_6_ = bf16[560,128]{1,0:T(8,128)(2,1)S(1)} collective-permute-done((bf16[560,128]{1,0:T(8,128)(2,1)S(1)}, bf16[560,128]{1,0:T(8,128)(2,1)S(1)}, u32[]{:S(2)}, u32[]{:S(2)}) %collective-permute-start.5) | collective-permute-done | bytes 143392 | tf_op jit(solution)/shard_map/ppermute | solution.py:714
  21.4 0.1 join.3
  21.4 1.1 %collective-permute-start.8 = (bf16[1024,128]{1,0:T(8,128)(2,1)S(1)}, bf16[1024,128]{1,0:T(8,128)(2,1)S(1)}, u32[]{:S(2)}, u32[]{:S(2)}) collective-permute-start(bf16[1024,128]{1,0:T(8,128)(2,1)S(1)} %get-tuple-element.80), channel_id=1, source_target_pairs={{0,2},{1,3},{2,0},{3,1},{4,6},{5,7},{6,4},{7,5},{8,10},{9,11},{10,... | collective-permute-start | bytes 786440 | tf_op jit(solution)/shard_map/ppermute | solution.py:714
  22.6 2.6 %collective-permute-start.6 = (bf16[512,128]{1,0:T(8,128)(2,1)S(1)}, bf16[512,128]{1,0:T(8,128)(2,1)S(1)}, u32[]{:S(2)}, u32[]{:S(2)}) collective-permute-start(bf16[512,128]{1,0:T(8,128)(2,1)S(1)} %get-tuple-element.75), channel_id=1, source_target_pairs={{0,8},{1,9},{2,10},{3,11},{4,12},{5,13},{6,14},{7,15},{8,0},{9,1},... | collective-permute-start | bytes 393224 | tf_op jit(solution)/shard_map/ppermute | solution.py:714
  25.2 0.4 %middle.3.total_ref.refs_6_ = f32[2048,512]{1,0:T(8,128)S(1)} custom-call(bf16[2304,512]{1,0:T(8,128)(2,1)S(1)} %get-tuple-element.60.refs_0_.acts_ref, f32[16,512]{1,0:T(8,128)S(1)} %get-tuple-element.50.log_ref.refs_2_.refs_1_, f32[224,512]{1,0:T(8,128)S(1)} %bitcast.6, ...), custom_call_target="tpu_custom_call", output_to_operand_aliasing={{}: (7, {})} | custom-call | flops 1024 | bytes 1024 | tf_op jit(solution)/shard_map/middle/pallas_call | solution.py:605
  25.7 4.2 %collective-permute-done.6.node_ref = bf16[512,128]{1,0:T(8,128)(2,1)S(1)} collective-permute-done((bf16[512,128]{1,0:T(8,128)(2,1)S(1)}, bf16[512,128]{1,0:T(8,128)(2,1)S(1)}, u32[]{:S(2)}, u32[]{:S(2)}) %collective-permute-start.6) | collective-permute-done | bytes 131104 | tf_op jit(solution)/shard_map/ppermute | solution.py:714
  29.8 1.0 %collective-permute-start.7 = (bf16[512,128]{1,0:T(8,128)(2,1)S(1)}, bf16[512,128]{1,0:T(8,128)(2,1)S(1)}, u32[]{:S(2)}, u32[]{:S(2)}) collective-permute-start(bf16[512,128]{1,0:T(8,128)(2,1)S(1)} %collective-permute-done.6.node_ref), channel_id=1, source_target_pairs={{0,2},{1,3},{2,0},{3,1},{4,6},{5,7},{6,4},{7,5},{8,10},{9,11},{10,... | collective-permute-start | bytes 393224 | tf_op jit(solution)/shard_map/ppermute | solution.py:714
  30.8 1.3 %last.3.refs_1_ = bf16[512,2048]{1,0:T(8,128)(2,1)} custom-call(f32[2048,512]{1,0:T(8,128)S(1)} %middle.3.total_ref.refs_6_, bf16[2304,512]{1,0:T(8,128)(2,1)S(1)} %get-tuple-element.60.refs_0_.acts_ref, f32[16,512]{1,0:T(8,128)S(1)} %get-tuple-element.50.log_ref.refs_2_.refs_1_, f32[224,512]{1,0:T(8,128)S(1)} %bitcast.7, ...), custom_call_target="tpu_custom_call" | custom-call | flops 1024 | bytes 1024 | tf_op jit(solution)/shard_map/last/pallas_call | solution.py:697
  32.1 0.0 collective-permute-done.8.refs_5_
  32.2 0.1 collective-permute-start.10
  32.2 0.5 %collective-permute-start.11 = (bf16[512,128]{1,0:T(8,128)(2,1)S(1)}, bf16[512,128]{1,0:T(8,128)(2,1)S(1)}, u32[]{:S(2)}, u32[]{:S(2)}) collective-permute-start(bf16[512,128]{1,0:T(8,128)(2,1)S(1)} %get-tuple-element.83), channel_id=1, source_target_pairs={{0,1},{1,0},{2,3},{3,2},{4,5},{5,4},{6,7},{7,6},{8,9},{9,8},{10,11... | collective-permute-start | bytes 393224 | tf_op jit(solution)/shard_map/ppermute | solution.py:714
  32.7 0.1 collective-permute-start.12
  32.8 0.4 %collective-permute-start.9 = (bf16[512,128]{1,0:T(8,128)(2,1)S(1)}, bf16[512,128]{1,0:T(8,128)(2,1)S(1)}, u32[]{:S(2)}, u32[]{:S(2)}) collective-permute-start(bf16[512,128]{1,0:T(8,128)(2,1)S(1)} %slice.21), channel_id=1, source_target_pairs={{0,1},{1,0},{2,3},{3,2},{4,5},{5,4},{6,7},{7,6},{8,9},{9,8},{10,11... | collective-permute-start | bytes 393224 | tf_op jit(solution)/shard_map/ppermute | solution.py:714
  33.3 0.4 %middle.4.refs_9_ = f32[2048,512]{1,0:T(8,128)S(1)} custom-call(bf16[2304,512]{1,0:T(8,128)(2,1)S(1)} %get-tuple-element.60.refs_0_.acts_ref, f32[16,512]{1,0:T(8,128)S(1)} %get-tuple-element.50.log_ref.refs_2_.refs_1_, f32[224,512]{1,0:T(8,128)S(1)} %bitcast.8, ...), custom_call_target="tpu_custom_call", output_to_operand_aliasing={{}: (6, {})} | custom-call | flops 1024 | bytes 1024 | tf_op jit(solution)/shard_map/middle/pallas_call | solution.py:605
  33.7 1.1 %collective-permute-done.7.node_ref = bf16[512,128]{1,0:T(8,128)(2,1)S(1)} collective-permute-done((bf16[512,128]{1,0:T(8,128)(2,1)S(1)}, bf16[512,128]{1,0:T(8,128)(2,1)S(1)}, u32[]{:S(2)}, u32[]{:S(2)}) %collective-permute-start.7) | collective-permute-done | bytes 131104 | tf_op jit(solution)/shard_map/ppermute | solution.py:714
  34.8 0.0 collective-permute-done.10.refs_6_
  34.8 0.0 collective-permute-done.11.refs_7_
  34.8 0.0 collective-permute-done.12.refs_8_
  34.8 0.0 collective-permute-done.9.refs_5_
  34.9 0.1 collective-permute-start.13
  34.9 0.8 %middle.5.total_ref = f32[2048,512]{1,0:T(8,128)S(1)} custom-call(bf16[2304,512]{1,0:T(8,128)(2,1)S(1)} %get-tuple-element.60.refs_0_.acts_ref, f32[16,512]{1,0:T(8,128)S(1)} %get-tuple-element.50.log_ref.refs_2_.refs_1_, f32[224,512]{1,0:T(8,128)S(1)} %bitcast.9, ...), custom_call_target="tpu_custom_call", output_to_operand_aliasing={{}: (9, {})} | custom-call | flops 1024 | bytes 1024 | tf_op jit(solution)/shard_map/middle/pallas_call | solution.py:605
  35.7 0.5 %last.4.refs_0_ = bf16[1,512,512]{2,1,0:T(8,128)(2,1)S(1)} custom-call(f32[2048,512]{1,0:T(8,128)S(1)} %middle.5.total_ref, bf16[2304,512]{1,0:T(8,128)(2,1)S(1)} %get-tuple-element.60.refs_0_.acts_ref, f32[16,512]{1,0:T(8,128)S(1)} %get-tuple-element.50.log_ref.refs_2_.refs_1_, f32[224,512]{1,0:T(8,128)S(1)} %bitcast.10, ...), custom_call_target="tpu_custom_call" | custom-call | flops 1024 | bytes 1024 | tf_op jit(solution)/shard_map/last/pallas_call | solution.py:697
  36.3 0.2 collective-permute-done.13.node_ref
  36.5 1.8 %last.5 = bf16[512,2048]{1,0:T(8,128)(2,1)} custom-call(f32[2048,512]{1,0:T(8,128)S(1)} %middle.5.total_ref, bf16[2304,512]{1,0:T(8,128)(2,1)S(1)} %get-tuple-element.60.refs_0_.acts_ref, f32[16,512]{1,0:T(8,128)S(1)} %get-tuple-element.50.log_ref.refs_2_.refs_1_, f32[224,512]{1,0:T(8,128)S(1)} %bitcast.11, ...), custom_call_target="tpu_custom_call", output_to_operand_aliasing={{}: (8, {})} | custom-call | flops 1024 | bytes 1024 | tf_op jit(solution)/shard_map/last/pallas_call | solution.py:697
  (6 shorter events, 0.1 us)
Async XLA Ops:
  2.1 5.8 %collective-permute-start = (bf16[3,2304]{1,0:T(4,128)(2,1)S(1)}, bf16[3,2304]{1,0:T(4,128)(2,1)S(1)}, u32[]{:S(2)}, u32[]{:S(2)}) collective-permute-start(bf16[3,2304]{1,0:T(4,128)(2,1)S(1)} %get-tuple-element.49), channel_id=1, source_target_pairs={{0,1},{1,2},{2,3},{3,4},{4,5},{5,6},{6,0},{7,8},{8,9},{9,10},{10,7... | collective-permute-start | bytes 41480 | tf_op jit(solution)/shard_map/ppermute | solution.py:739
  2.6 5.2 %collective-permute-start.1 = (bf16[3,2304]{1,0:T(4,128)(2,1)S(1)}, bf16[3,2304]{1,0:T(4,128)(2,1)S(1)}, u32[]{:S(2)}, u32[]{:S(2)}) collective-permute-start(bf16[3,2304]{1,0:T(4,128)(2,1)S(1)} %get-tuple-element.49), channel_id=1, source_target_pairs={{0,1},{1,0},{2,3},{3,2},{4,5},{5,4},{6,7},{7,6},{8,9},{9,8},{10,11... | collective-permute-start | bytes 41480 | tf_op jit(solution)/shard_map/ppermute | solution.py:714
  8.5 3.0 %copy-start = (f32[16,14,512]{2,0,1:T(8,128)S(1)}, f32[16,14,512]{2,0,1:T(8,128)}, u32[]{:S(2)}) copy-start(f32[16,14,512]{2,0,1:T(8,128)} %param.8) | copy-start | bytes 1376260
  8.5 3.0 %copy-start.1 = (f32[2048]{0:T(1024)S(1)}, f32[2048]{0:T(1024)}, u32[]{:S(2)}) copy-start(f32[2048]{0:T(1024)} %param.9) | copy-start | bytes 24580
  8.5 1.6 %collective-permute-start.2 = (bf16[1072,128]{1,0:T(8,128)(2,1)S(1)}, bf16[1072,128]{1,0:T(8,128)(2,1)S(1)}, u32[]{:S(2)}, u32[]{:S(2)}) collective-permute-start(bf16[1072,128]{1,0:T(8,128)(2,1)S(1)} %get-tuple-element.62), channel_id=1, source_target_pairs={{0,1},{1,0},{2,3},{3,2},{4,5},{5,4},{6,7},{7,6},{8,9},{9,8},{10,11... | collective-permute-start | bytes 823304 | tf_op jit(solution)/shard_map/ppermute | solution.py:714
  8.6 2.8 %collective-permute-start.4 = (bf16[1024,128]{1,0:T(8,128)(2,1)S(1)}, bf16[1024,128]{1,0:T(8,128)(2,1)S(1)}, u32[]{:S(2)}, u32[]{:S(2)}) collective-permute-start(bf16[1024,128]{1,0:T(8,128)(2,1)S(1)} %get-tuple-element.67), channel_id=1, source_target_pairs={{0,1},{1,0},{2,3},{3,2},{4,5},{5,4},{6,7},{7,6},{8,9},{9,8},{10,11... | collective-permute-start | bytes 786440 | tf_op jit(solution)/shard_map/ppermute | solution.py:714
  10.3 5.9 %collective-permute-start.3 = (bf16[560,128]{1,0:T(8,128)(2,1)S(1)}, bf16[560,128]{1,0:T(8,128)(2,1)S(1)}, u32[]{:S(2)}, u32[]{:S(2)}) collective-permute-start(bf16[560,128]{1,0:T(8,128)(2,1)S(1)} %get-tuple-element.65), channel_id=1, source_target_pairs={{0,2},{1,3},{2,0},{3,1},{4,6},{5,7},{6,4},{7,5},{8,10},{9,11},{10,... | collective-permute-start | bytes 430088 | tf_op jit(solution)/shard_map/ppermute | solution.py:714
  16.2 5.2 %collective-permute-start.5 = (bf16[560,128]{1,0:T(8,128)(2,1)S(1)}, bf16[560,128]{1,0:T(8,128)(2,1)S(1)}, u32[]{:S(2)}, u32[]{:S(2)}) collective-permute-start(bf16[560,128]{1,0:T(8,128)(2,1)S(1)} %get-tuple-element.71), channel_id=1, source_target_pairs={{0,4},{1,5},{2,6},{3,7},{4,0},{5,1},{6,2},{7,3},{8,12},{9,13},{10,... | collective-permute-start | bytes 430088 | tf_op jit(solution)/shard_map/ppermute | solution.py:714
  21.4 10.7 %collective-permute-start.8 = (bf16[1024,128]{1,0:T(8,128)(2,1)S(1)}, bf16[1024,128]{1,0:T(8,128)(2,1)S(1)}, u32[]{:S(2)}, u32[]{:S(2)}) collective-permute-start(bf16[1024,128]{1,0:T(8,128)(2,1)S(1)} %get-tuple-element.80), channel_id=1, source_target_pairs={{0,2},{1,3},{2,0},{3,1},{4,6},{5,7},{6,4},{7,5},{8,10},{9,11},{10,... | collective-permute-start | bytes 786440 | tf_op jit(solution)/shard_map/ppermute | solution.py:714
  22.6 7.3 %collective-permute-start.6 = (bf16[512,128]{1,0:T(8,128)(2,1)S(1)}, bf16[512,128]{1,0:T(8,128)(2,1)S(1)}, u32[]{:S(2)}, u32[]{:S(2)}) collective-permute-start(bf16[512,128]{1,0:T(8,128)(2,1)S(1)} %get-tuple-element.75), channel_id=1, source_target_pairs={{0,8},{1,9},{2,10},{3,11},{4,12},{5,13},{6,14},{7,15},{8,0},{9,1},... | collective-permute-start | bytes 393224 | tf_op jit(solution)/shard_map/ppermute | solution.py:714
  29.8 5.0 %collective-permute-start.7 = (bf16[512,128]{1,0:T(8,128)(2,1)S(1)}, bf16[512,128]{1,0:T(8,128)(2,1)S(1)}, u32[]{:S(2)}, u32[]{:S(2)}) collective-permute-start(bf16[512,128]{1,0:T(8,128)(2,1)S(1)} %collective-permute-done.6.node_ref), channel_id=1, source_target_pairs={{0,2},{1,3},{2,0},{3,1},{4,6},{5,7},{6,4},{7,5},{8,10},{9,11},{10,... | collective-permute-start | bytes 393224 | tf_op jit(solution)/shard_map/ppermute | solution.py:714
  32.2 2.7 %collective-permute-start.10 = (bf16[512,128]{1,0:T(8,128)(2,1)S(1)}, bf16[512,128]{1,0:T(8,128)(2,1)S(1)}, u32[]{:S(2)}, u32[]{:S(2)}) collective-permute-start(bf16[512,128]{1,0:T(8,128)(2,1)S(1)} %slice.22), channel_id=1, source_target_pairs={{0,1},{1,0},{2,3},{3,2},{4,5},{5,4},{6,7},{7,6},{8,9},{9,8},{10,11... | collective-permute-start | bytes 393224 | tf_op jit(solution)/shard_map/ppermute | solution.py:714
  32.2 2.6 %collective-permute-start.11 = (bf16[512,128]{1,0:T(8,128)(2,1)S(1)}, bf16[512,128]{1,0:T(8,128)(2,1)S(1)}, u32[]{:S(2)}, u32[]{:S(2)}) collective-permute-start(bf16[512,128]{1,0:T(8,128)(2,1)S(1)} %get-tuple-element.83), channel_id=1, source_target_pairs={{0,1},{1,0},{2,3},{3,2},{4,5},{5,4},{6,7},{7,6},{8,9},{9,8},{10,11... | collective-permute-start | bytes 393224 | tf_op jit(solution)/shard_map/ppermute | solution.py:714
  32.7 2.1 %collective-permute-start.12 = (bf16[512,128]{1,0:T(8,128)(2,1)S(1)}, bf16[512,128]{1,0:T(8,128)(2,1)S(1)}, u32[]{:S(2)}, u32[]{:S(2)}) collective-permute-start(bf16[512,128]{1,0:T(8,128)(2,1)S(1)} %get-tuple-element.84), channel_id=1, source_target_pairs={{0,1},{1,0},{2,3},{3,2},{4,5},{5,4},{6,7},{7,6},{8,9},{9,8},{10,11... | collective-permute-start | bytes 393224 | tf_op jit(solution)/shard_map/ppermute | solution.py:714
  32.8 2.0 %collective-permute-start.9 = (bf16[512,128]{1,0:T(8,128)(2,1)S(1)}, bf16[512,128]{1,0:T(8,128)(2,1)S(1)}, u32[]{:S(2)}, u32[]{:S(2)}) collective-permute-start(bf16[512,128]{1,0:T(8,128)(2,1)S(1)} %slice.21), channel_id=1, source_target_pairs={{0,1},{1,0},{2,3},{3,2},{4,5},{5,4},{6,7},{7,6},{8,9},{9,8},{10,11... | collective-permute-start | bytes 393224 | tf_op jit(solution)/shard_map/ppermute | solution.py:714
  34.9 1.6 %collective-permute-start.13 = (bf16[1024,128]{1,0:T(8,128)(2,1)S(1)}, bf16[1024,128]{1,0:T(8,128)(2,1)S(1)}, u32[]{:S(2)}, u32[]{:S(2)}) collective-permute-start(bf16[1024,128]{1,0:T(8,128)(2,1)S(1)} %pad_maximum_fusion.1), channel_id=1, source_target_pairs={{0,1},{1,0},{2,3},{3,2},{4,5},{5,4},{6,7},{7,6},{8,9},{9,8},{10,11... | collective-permute-start | bytes 786440 | tf_op jit(solution)/shard_map/ppermute | solution.py:714
